TPU v7x, 32 devices: a whole 2x2x4 slice. The times are simulated.
32 devices in a mesh: groups: 2 (over x), gx: 16 (over z, y, core).
Axes of the slice: x: 2, y: 2, z: 4, core: 2. Of those that a mesh axis runs over, the one named last changes fastest.
Arguments:
- probes: float32 [64, 1024, 512], P(None, ('groups', 'gx')), parts along dimension 1, as said below
- kappa: float32 [1024, 512], P(('groups', 'gx')), parts along dimension 0, may hold values from 0.1 to 0.8
- speed: float32 [1024, 512], P(('groups', 'gx')), parts along dimension 0, may hold values from 0.05 to 0.5
- friction: float32 [1024, 512], P(('groups', 'gx')), parts along dimension 0, may hold values from 0.1 to 1
- upwind: int32 [1024, 16], P(('groups', 'gx')), parts along dimension 0, may hold values from 0 to 3
- probe_sites: int32 [128], P('groups'), parts along dimension 0, may hold values from 0 to 262143
Outputs:
- basis: float32 [64, 1024, 512], P(None, ('groups', 'gx')), parts along dimension 1
- factor: float32 [128, 64], P('groups'), parts along dimension 0
There are 2 independent parts, one for each index of `groups`. A program takes and returns all parts, laid end to end along the dimension named above; each array names one. Nothing has to cross between parts.
Inputs may be any that keep to these rules, and one draw needn't show every extreme that they name: upwind neighbour of a block of 32 cells of one row: 0 above, 1 below, 2 left, 3 right. `probe_sites`: flat index row * 512 + column of the cell of probe k's impulse. `probes`: probe fields.
All inputs are finite; a program needn't handle non-finite values.
Results may differ from a plain program's by a relative error of at most 0.0003.
Values sent between devices are 32-bit elements; how exact they have to be, the bound alone decides.
No kernel may reach another device: no remote copies, remote signals or barrier semaphores. Data moves between devices by JAX's collectives and lax.ppermute only.
A program may use at most 64 MiB of HBM per device.

v0:
```python
import functools
import math

import jax
import jax.numpy as jnp
from jax import lax
from jax.experimental import pallas as pl
from jax.experimental.pallas import tpu as pltpu
from jax.sharding import PartitionSpec as P

TIME_STEP = 0.2
IMPULSE_GAIN = 3.0
AXIS = "gx"
DEPTH = 4
PACK = 8
MIB = 1024 * 1024


def rolled(row, by):
    return pltpu.roll(row, by % row.shape[-1], row.ndim - 1)


def weight_row(weights, row, layer, like):
    return jnp.broadcast_to(weights[row, layer : layer + 1, :], like)


def sweep_row(source, at, target, to, probes, columns, center, above, below, left, right):
    for first in range(0, probes, 8):
        octet = slice(first, first + 8)
        middle = source[at, octet, :]
        target[to, octet, :] = (
            center * middle
            + above * source[at - 1, octet, :]
            + below * source[at + 1, octet, :]
            + left * rolled(middle, 1)
            + right * rolled(middle, -1)
        )


def forward_row(source, at, target, to, weights, w_at, probes, columns):
    like = (8, columns)
    sweep_row(
        source, at, target, to, probes, columns,
        *[weight_row(weights, w_at, layer, like) for layer in range(5)],
    )


def adjoint_row(source, at, target, to, weights, w_at, probes, columns):
    like = (8, columns)
    sweep_row(
        source, at, target, to, probes, columns,
        weight_row(weights, w_at, 0, like),
        weight_row(weights, w_at - 1, 2, like),
        weight_row(weights, w_at + 1, 1, like),
        rolled(weight_row(weights, w_at, 4, like), 1),
        rolled(weight_row(weights, w_at, 3, like), -1),
    )


def add_impulses(sites, target, first_row, row_count, base, probes, columns, strength):
    column_ids = lax.broadcasted_iota(jnp.int32, (1, columns), 1)

    def one(k, carry):
        site = sites[k]
        row = site // columns - first_row

        @pl.when((row >= 0) & (row < row_count))
        def _():
            hit = jnp.where(column_ids == site % columns, strength, 0.0)
            target[base + row, pl.ds(k, 1), :] += hit

        return carry

    lax.fori_loop(0, probes, one, 0)


def pack_kernel(cells, kappa, speed, friction, upwind, weights, to_below, to_above, sems):
    probes, rows, columns = cells.shape
    copies = []
    for r in range(DEPTH):
        for side, target in enumerate((to_above, to_below)):
            row = r if side == 0 else rows - DEPTH + r
            copies.append(
                pltpu.make_async_copy(cells.at[:, row, :], target.at[r, pl.ds(0, probes), :], sems.at[side, r])
            )
    for copy in copies:
        copy.start()
    blocks = upwind.shape[1]
    width = columns // blocks
    spread = (
        lax.broadcasted_iota(jnp.int32, (blocks, columns), 1) // width
        == lax.broadcasted_iota(jnp.int32, (blocks, columns), 0)
    ).astype(jnp.bfloat16)
    directions = jnp.dot(
        upwind[...].astype(jnp.float32).astype(jnp.bfloat16), spread, preferred_element_type=jnp.float32
    )
    column_ids = lax.broadcasted_iota(jnp.int32, (rows, columns), 1)
    k, s = kappa[...], speed[...]
    layers = [1.0 - TIME_STEP * (4.0 * k + s + friction[...])]
    for direction in range(4):
        chosen = jnp.where(jnp.abs(directions - direction) < 0.5, s, 0.0)
        layers.append(TIME_STEP * (k + chosen))
    layers[3] = jnp.where(column_ids == 0, 0.0, layers[3])
    layers[4] = jnp.where(column_ids == columns - 1, 0.0, layers[4])
    for index in range(PACK):
        layer = layers[index] if index < 5 else jnp.zeros((rows, columns), jnp.float32)
        for r in range(rows):
            weights[r, index : index + 1, :] = layer[r : r + 1, :]
    for r in range(DEPTH):
        to_above[r, probes:, :] = weights[r]
        to_below[r, probes:, :] = weights[rows - DEPTH + r]
    for copy in copies:
        copy.wait()


def inner_kernel(strength, sites, cells, weights, response, top, bottom, v, f1, f2, a1, sems):
    rows, probes, columns = v.shape
    first_row = lax.axis_index(AXIS) * rows

    copies = [pltpu.make_async_copy(cells.at[:, r, :], v.at[r], sems.at[r]) for r in range(rows)]
    for copy in copies:
        copy.start()
    for copy in copies:
        copy.wait()
    add_impulses(sites, v, first_row, rows, 0, probes, columns, strength)

    def sweep(row_fn, source, target, first, last):
        def body(r, carry):
            row_fn(source, r, target, r, weights, r, probes, columns)
            return carry

        lax.fori_loop(first, last, body, 0)

    sweep(forward_row, v, f1, 1, rows - 1)
    sweep(forward_row, f1, f2, 2, rows - 2)
    sweep(adjoint_row, f2, a1, 3, rows - 3)

    def body(r, carry):
        adjoint_row(a1, r, response, r - DEPTH, weights, r, probes, columns)
        return carry

    lax.fori_loop(DEPTH, rows - DEPTH, body, 0)
    for level, field in enumerate((v, f1, f2, a1)):
        for j in range(2):
            top[level, j] = field[level + j]
            bottom[level, j] = field[rows - 2 - level + j]


def edge_kernel(strength, rows, sites, above, below, weights, top, bottom, out_top, out_bottom, w, va, vb, la, lb):
    probes, columns = top.shape[2:]
    first_row = lax.axis_index(AXIS) * rows
    half = 3 * DEPTH
    for r in range(DEPTH):
        w[r] = above[r, probes:, :]
        w[half + 2 * DEPTH + r] = below[r, probes:, :]
        va[r] = above[r, :probes, :]
        vb[2 + r] = below[r, :probes, :]
    for r in range(2 * DEPTH):
        w[DEPTH + r] = weights[r]
        w[half + r] = weights[rows - 2 * DEPTH + r]
    for j in range(2):
        va[DEPTH + j] = top[0, j]
        vb[j] = bottom[0, j]
        for level in range(1, 4):
            la[level - 1, DEPTH + j] = top[level, j]
            lb[level - 1, j] = bottom[level, j]
    add_impulses(sites, va, first_row - DEPTH, DEPTH, 0, probes, columns, strength)
    add_impulses(sites, vb, first_row + rows, DEPTH, 2, probes, columns, strength)
    chain_a = [va, la.at[0], la.at[1], la.at[2], out_top]
    chain_b = [vb, lb.at[0], lb.at[1], lb.at[2], out_bottom]
    for level in range(4):
        row_fn = forward_row if level < 2 else adjoint_row

        def body(j, carry, level=level, row_fn=row_fn):
            row_fn(chain_a[level], j + 1, chain_a[level + 1], j, w, level + 1 + j, probes, columns)
            to = j if level == 3 else j + 2
            row_fn(chain_b[level], j + 1, chain_b[level + 1], to, w, half + 2 * DEPTH - 1 - level + j, probes, columns)
            return carry

        lax.fori_loop(0, DEPTH, body, 0)


def whole(memory=pltpu.VMEM):
    return pl.BlockSpec(memory_space=memory)


def summed(value):
    count = lax.axis_size(AXIS)
    if count & (count - 1):
        return lax.psum(value, AXIS)
    distance = 1
    while distance < count:
        value = value + lax.ppermute(value, AXIS, [(i, i ^ distance) for i in range(count)])
        distance *= 2
    return value


def responses(probes, kappa, speed, friction, upwind, probe_sites):
    count, rows, columns = probes.shape
    strength = IMPULSE_GAIN * math.sqrt(rows * columns * lax.axis_size(AXIS))
    f32 = jnp.float32
    params = pltpu.CompilerParams(vmem_limit_bytes=56 * MIB)
    halo = jax.ShapeDtypeStruct((DEPTH, count + PACK, columns), f32)
    weights, to_below, to_above = pl.pallas_call(
        pack_kernel,
        out_shape=(jax.ShapeDtypeStruct((rows, PACK, columns), f32), halo, halo),
        in_specs=[whole(pl.ANY), whole(), whole(), whole(), whole()],
        out_specs=(whole(), whole(), whole()),
        scratch_shapes=[pltpu.SemaphoreType.DMA((2, DEPTH))],
        compiler_params=params,
        name="pack",
    )(probes, kappa, speed, friction, upwind)
    size = lax.axis_size(AXIS)
    from_above = lax.ppermute(to_below, AXIS, [(i, i + 1) for i in range(size - 1)])
    from_below = lax.ppermute(to_above, AXIS, [(i + 1, i) for i in range(size - 1)])
    kept = jax.ShapeDtypeStruct((4, 2, count, columns), f32)
    field = pltpu.VMEM((rows, count, columns), f32)
    inner, top, bottom = pl.pallas_call(
        functools.partial(inner_kernel, strength),
        out_shape=(jax.ShapeDtypeStruct((rows - 2 * DEPTH, count, columns), f32), kept, kept),
        in_specs=[whole(pltpu.SMEM), whole(pl.ANY), whole()],
        out_specs=(whole(), whole(), whole()),
        scratch_shapes=[field] * 4 + [pltpu.SemaphoreType.DMA((rows,))],
        compiler_params=params,
        cost_estimate=pl.CostEstimate(flops=10**10, bytes_accessed=16 * MIB, transcendentals=0),
        name="inner_rows",
    )(probe_sites, probes, weights)
    outer = jax.ShapeDtypeStruct((DEPTH, count, columns), f32)
    fields = pltpu.VMEM((DEPTH + 2, count, columns), f32)
    levels = pltpu.VMEM((3, DEPTH + 2, count, columns), f32)
    out_top, out_bottom = pl.pallas_call(
        functools.partial(edge_kernel, strength, rows),
        out_shape=(outer, outer),
        in_specs=[whole(pltpu.SMEM)] + [whole()] * 5,
        out_specs=(whole(), whole()),
        scratch_shapes=[pltpu.VMEM((6 * DEPTH, PACK, columns), f32), fields, fields, levels, levels],
        compiler_params=params,
        name="edge_rows",
    )(probe_sites, from_above, from_below, weights, top, bottom)
    return out_top, inner, out_bottom


def gram_factor(field):
    local_gram = jnp.einsum("rkc,rlc->kl", field, field, precision=lax.Precision.HIGHEST)
    return jnp.linalg.cholesky(summed(local_gram))


def on_device(probes, kappa, speed, friction, upwind, probe_sites):
    count, rows, columns = probes.shape
    field = jnp.concatenate(responses(probes, kappa, speed, friction, upwind, probe_sites), axis=0)
    cell_scale = math.sqrt(rows * columns * lax.axis_size(AXIS))
    identity = jnp.eye(count, dtype=jnp.float32)
    lowers = []
    for _ in range(2):
        lower = gram_factor(field)
        inverse = jax.scipy.linalg.solve_triangular(lower, identity, lower=True)
        field = jnp.einsum("kl,rlc->rkc", inverse, field, precision=lax.Precision.HIGHEST)
        lowers.append(lower)
    factor = jnp.dot(lowers[0], lowers[1], precision=lax.Precision.HIGHEST).T / cell_scale
    return (jnp.swapaxes(field, 0, 1) * cell_scale, factor)


def solution(mesh):
    return jax.shard_map(
        on_device,
        mesh=mesh,
        in_specs=(
            P(None, ("groups", "gx"), None),
            P(("groups", "gx"), None),
            P(("groups", "gx"), None),
            P(("groups", "gx"), None),
            P(("groups", "gx"), None),
            P("groups"),
        ),
        out_specs=(P(None, ("groups", "gx"), None), P("groups", None)),
        check_vma=False,
    )
```

profile of v0, /device:TPU:0, one launch (start us, length us, event | category | flops | bytes accessed | tf_op | source)
XLA Modules:
  0.0 128.2 jit_solution(14586540144915784702)
XLA Ops:
  0.6 1.4 %copy.8.upwind = s32[32,16]{1,0:T(8,128)} copy(s32[32,16]{0,1:T(8,128)} %param.13) | data formatting | bytes 4096 | tf_op args[4]
  2.0 3.6 %pack.1 = (f32[32,8,512]{2,1,0:T(8,128)}, f32[4,72,512]{2,1,0:T(8,128)}, f32[4,72,512]{2,1,0:T(8,128)}) custom-call(f32[64,32,512]{2,1,0:T(8,128)} %cells.3, f32[32,512]{1,0:T(8,128)} %kappa.1, f32[32,512]{1,0:T(8,128)} %speed.1, f32[32,512]{1,0:T(8,128)} %friction.1, s32[32,16]{1,0:T(8,128)} %copy.8.upwind), custom_call_target="tpu_custom_call" | custom-call | tf_op jit(solution)/shard_map/pack/pallas_call | solution.py:204
  5.6 2.4 %collective-permute-start = (f32[4,72,512]{2,1,0:T(8,128)}, f32[4,72,512]{2,1,0:T(8,128)S(1)}, u32[]{:S(2)}, u32[]{:S(2)}) collective-permute-start(f32[4,72,512]{2,1,0:T(8,128)} %get-tuple-element.12), channel_id=1, source_target_pairs={{0,1},{1,2},{2,3},{3,4},{4,5},{5,6},{6,7},{7,8},{8,9},{9,10},{10,1... | collective-permute-start | bytes 1769480 | tf_op jit(solution)/shard_map/ppermute | solution.py:214
  8.0 1.3 %collective-permute-start.1 = (f32[4,72,512]{2,1,0:T(8,128)}, f32[4,72,512]{2,1,0:T(8,128)S(1)}, u32[]{:S(2)}, u32[]{:S(2)}) collective-permute-start(f32[4,72,512]{2,1,0:T(8,128)} %get-tuple-element.13), channel_id=1, source_target_pairs={{1,0},{2,1},{3,2},{4,3},{5,4},{6,5},{7,6},{8,7},{9,8},{10,9},{11,1... | collective-permute-start | bytes 1769480 | tf_op jit(solution)/shard_map/ppermute | solution.py:215
  9.3 23.1 %inner_rows.1 = (f32[24,64,512]{2,1,0:T(8,128)}, f32[4,2,64,512]{3,2,1,0:T(8,128)}, f32[4,2,64,512]{3,2,1,0:T(8,128)}) custom-call(s32[64]{0:T(128)} %sites.3, f32[64,32,512]{2,1,0:T(8,128)} %cells.3, f32[32,8,512]{2,1,0:T(8,128)} %get-tuple-element.14.weights), custom_call_target="tpu_custom_call" | custom-call | flops 10000000000 | bytes 16777216 | tf_op jit(solution)/shard_map/inner_rows/pallas_call | solution.py:218
  32.5 0.0 copy-start.2
  32.5 0.8 copy-done.3
  33.3 0.2 copy-done.4
  33.5 9.6 %edge_rows.1 = (f32[4,64,512]{2,1,0:T(8,128)}, f32[4,64,512]{2,1,0:T(8,128)}) custom-call(s32[64]{0:T(128)} %sites.3, f32[4,72,512]{2,1,0:T(8,128)} %copy-done.3, f32[4,72,512]{2,1,0:T(8,128)} %copy-done.4, f32[32,8,512]{2,1,0:T(8,128)} %get-tuple-element.14.weights, f32[4,2,64,512]{3,2,1,0:T(8,128)} %get-tuple-element.15.top, ...), custom_call_target="tpu_custom_call" | custom-call | tf_op jit(solution)/shard_map/edge_rows/pallas_call | solution.py:231
  43.2 1.1 constant_dynamic-update-slice_fusion.2
  44.3 0.4 constant_dynamic-update-slice_fusion.1
  44.8 0.0 copy-start
  44.8 3.4 %convolution_bitcast_fusion.2 = f32[64,64]{0,1:T(8,128)S(1)} fusion(f32[32,64,512]{2,1,0:T(8,128)S(1)} %constant_dynamic-update-slice_fusion), kind=kOutput, calls=%fused_computation.9 | convolution fusion | flops 805306368 | bytes 4210688 | tf_op jit(solution)/shard_map/rkc,rlc->kl/dot_general | solution.py:244
  48.2 3.3 %collective-permute-start.2 = (f32[64,64]{0,1:T(8,128)S(1)}, f32[64,64]{0,1:T(8,128)S(1)}, u32[]{:S(2)}, u32[]{:S(2)}) collective-permute-start(f32[64,64]{0,1:T(8,128)S(1)} %convolution_bitcast_fusion.2), channel_id=1, source_target_pairs={{0,1},{1,0},{2,3},{3,2},{4,5},{5,4},{6,7},{7,6},{8,9},{9,8},{10,11... | collective-permute-start | bytes 49160 | tf_op jit(solution)/shard_map/ppermute | solution.py:193
  51.5 0.9 collective-permute-done.2
  52.4 1.8 %collective-permute-start.3 = (f32[64,64]{0,1:T(8,128)S(1)}, f32[64,64]{0,1:T(8,128)S(1)}, u32[]{:S(2)}, u32[]{:S(2)}) collective-permute-start(f32[64,64]{0,1:T(8,128)S(1)} %add.33), channel_id=1, source_target_pairs={{0,2},{1,3},{2,0},{3,1},{4,6},{5,7},{6,4},{7,5},{8,10},{9,11},{10,... | collective-permute-start | bytes 49160 | tf_op jit(solution)/shard_map/ppermute | solution.py:193
  54.2 2.1 %collective-permute-done.3 = f32[64,64]{0,1:T(8,128)S(1)} collective-permute-done((f32[64,64]{0,1:T(8,128)S(1)}, f32[64,64]{0,1:T(8,128)S(1)}, u32[]{:S(2)}, u32[]{:S(2)}) %collective-permute-start.3) | collective-permute-done | bytes 16416 | tf_op jit(solution)/shard_map/ppermute | solution.py:193
  56.3 2.7 %collective-permute-start.4 = (f32[64,64]{0,1:T(8,128)S(1)}, f32[64,64]{0,1:T(8,128)S(1)}, u32[]{:S(2)}, u32[]{:S(2)}) collective-permute-start(f32[64,64]{0,1:T(8,128)S(1)} %add.34), channel_id=1, source_target_pairs={{0,4},{1,5},{2,6},{3,7},{4,0},{5,1},{6,2},{7,3},{8,12},{9,13},{10,... | collective-permute-start | bytes 49160 | tf_op jit(solution)/shard_map/ppermute | solution.py:193
  59.0 1.9 %collective-permute-done.4 = f32[64,64]{0,1:T(8,128)S(1)} collective-permute-done((f32[64,64]{0,1:T(8,128)S(1)}, f32[64,64]{0,1:T(8,128)S(1)}, u32[]{:S(2)}, u32[]{:S(2)}) %collective-permute-start.4) | collective-permute-done | bytes 16416 | tf_op jit(solution)/shard_map/ppermute | solution.py:193
  60.9 2.9 %collective-permute-start.5 = (f32[64,64]{0,1:T(8,128)S(1)}, f32[64,64]{0,1:T(8,128)S(1)}, u32[]{:S(2)}, u32[]{:S(2)}) collective-permute-start(f32[64,64]{0,1:T(8,128)S(1)} %add.35), channel_id=1, source_target_pairs={{0,8},{1,9},{2,10},{3,11},{4,12},{5,13},{6,14},{7,15},{8,0},{9,1},... | collective-permute-start | bytes 49160 | tf_op jit(solution)/shard_map/ppermute | solution.py:193
  63.8 1.9 %collective-permute-done.5 = f32[64,64]{0,1:T(8,128)S(1)} collective-permute-done((f32[64,64]{0,1:T(8,128)S(1)}, f32[64,64]{0,1:T(8,128)S(1)}, u32[]{:S(2)}, u32[]{:S(2)}) %collective-permute-start.5) | collective-permute-done | bytes 16416 | tf_op jit(solution)/shard_map/ppermute | solution.py:193
  65.7 0.1 copy.11
  65.8 5.8 %cholesky.44 = f32[64,64]{1,0:T(8,128)S(1)} custom-call(f32[64,64]{1,0:T(8,128)S(1)} %fusion.15), custom_call_target="Cholesky" | custom-call | tf_op jit(solution)/shard_map/jit(cholesky)/cholesky | solution.py:245
  71.7 0.6 compare_reduce_fusion.1
  72.4 0.6 fusion.19
  72.9 4.9 %custom-call.6 = f32[1,64,64]{1,2,0:T(8,128)S(1)} custom-call(f32[1,64,64]{2,1,0:T(8,128)S(1)} %fusion.19), custom_call_target="InvertDiagBlocksLowerTriangular" | custom-call | tf_op jit(solution)/shard_map/jit(_solve_triangular)/triangular_solve | solution.py:256
  77.8 0.3 convolution_bitcast_fusion.1
  78.1 5.9 %fusion.30 = f32[32,512,64]{1,2,0:T(8,128)S(1)} fusion(f32[32,64,512]{2,1,0:T(8,128)} %copy-done, f32[64,64,1]{1,0,2:T(8,128)S(1)} %convolution_bitcast_fusion.1), kind=kOutput, calls=%fused_computation.39 | convolution fusion | flops 805306368 | bytes 8404992 | tf_op jit(solution)/shard_map/kl,rlc->rkc/dot_general | solution.py:257
  84.0 0.0 copy-start.1
  84.0 2.0 %copy-done.1 = f32[32,512,64]{1,2,0:T(8,128)} copy-done((f32[32,512,64]{1,2,0:T(8,128)}, f32[32,512,64]{1,2,0:T(8,128)S(1)}, u32[]{:S(2)}) %copy-start.1) | copy-done | bytes 4194328
  86.0 3.4 %fusion.7 = f32[64,64]{0,1:T(8,128)S(1)} fusion(f32[32,512,64]{1,2,0:T(8,128)S(1)} %fusion.30), kind=kOutput, calls=%fused_computation.5 | convolution fusion | flops 805306368 | bytes 4210688 | tf_op jit(solution)/shard_map/rkc,rlc->kl/dot_general | solution.py:244
  89.4 0.1 collective-permute-start.6
  89.5 1.2 collective-permute-done.6
  90.7 1.1 collective-permute-start.7
  91.8 2.8 %collective-permute-done.7 = f32[64,64]{0,1:T(8,128)S(1)} collective-permute-done((f32[64,64]{0,1:T(8,128)S(1)}, f32[64,64]{0,1:T(8,128)S(1)}, u32[]{:S(2)}, u32[]{:S(2)}) %collective-permute-start.7) | collective-permute-done | bytes 16416 | tf_op jit(solution)/shard_map/ppermute | solution.py:193
  94.6 2.0 %collective-permute-start.8 = (f32[64,64]{0,1:T(8,128)S(1)}, f32[64,64]{0,1:T(8,128)S(1)}, u32[]{:S(2)}, u32[]{:S(2)}) collective-permute-start(f32[64,64]{0,1:T(8,128)S(1)} %add.38), channel_id=1, source_target_pairs={{0,4},{1,5},{2,6},{3,7},{4,0},{5,1},{6,2},{7,3},{8,12},{9,13},{10,... | collective-permute-start | bytes 49160 | tf_op jit(solution)/shard_map/ppermute | solution.py:193
  96.6 1.9 %collective-permute-done.8 = f32[64,64]{0,1:T(8,128)S(1)} collective-permute-done((f32[64,64]{0,1:T(8,128)S(1)}, f32[64,64]{0,1:T(8,128)S(1)}, u32[]{:S(2)}, u32[]{:S(2)}) %collective-permute-start.8) | collective-permute-done | bytes 16416 | tf_op jit(solution)/shard_map/ppermute | solution.py:193
  98.6 2.9 %collective-permute-start.9 = (f32[64,64]{0,1:T(8,128)S(1)}, f32[64,64]{0,1:T(8,128)S(1)}, u32[]{:S(2)}, u32[]{:S(2)}) collective-permute-start(f32[64,64]{0,1:T(8,128)S(1)} %add.39), channel_id=1, source_target_pairs={{0,8},{1,9},{2,10},{3,11},{4,12},{5,13},{6,14},{7,15},{8,0},{9,1},... | collective-permute-start | bytes 49160 | tf_op jit(solution)/shard_map/ppermute | solution.py:193
  101.4 1.9 %collective-permute-done.9 = f32[64,64]{0,1:T(8,128)S(1)} collective-permute-done((f32[64,64]{0,1:T(8,128)S(1)}, f32[64,64]{0,1:T(8,128)S(1)}, u32[]{:S(2)}, u32[]{:S(2)}) %collective-permute-start.9) | collective-permute-done | bytes 16416 | tf_op jit(solution)/shard_map/ppermute | solution.py:193
  103.4 0.1 copy.14
  103.5 5.8 %cholesky.55 = f32[64,64]{1,0:T(8,128)S(1)} custom-call(f32[64,64]{1,0:T(8,128)S(1)} %fusion.13), custom_call_target="Cholesky" | custom-call | tf_op jit(solution)/shard_map/jit(cholesky)/cholesky | solution.py:245
  109.4 0.7 compare_reduce_fusion
  110.1 2.1 %convolution_multiply_fusion = f32[64,64]{1,0:T(8,128)} fusion(f32[64,64]{1,0:T(8,128)S(1)} %cholesky.55, f32[64,64]{1,0:T(8,128)S(1)} %cholesky.44, pred[]{:T(512)} %compare_reduce_fusion, pred[]{:T(512)} %compare_reduce_fusion.1), kind=kOutput, calls=%fused_computation.6 | convolution fusion | flops 3174400 | bytes 49154 | tf_op jit(solution)/shard_map/dot_general | solution.py:259
  112.2 0.7 select_bitcast_fusion
  112.9 4.9 %custom-call.7 = f32[1,64,64]{1,2,0:T(8,128)S(1)} custom-call(f32[1,64,64]{2,1,0:T(8,128)S(1)} %select_bitcast_fusion), custom_call_target="InvertDiagBlocksLowerTriangular" | custom-call | tf_op jit(solution)/shard_map/jit(_solve_triangular)/triangular_solve | solution.py:256
  117.8 0.3 convolution_bitcast_fusion
  118.0 5.7 %fusion.4 = f32[64,32,512]{2,0,1:T(8,128)S(1)} fusion(f32[64,64,1]{1,0,2:T(8,128)S(1)} %convolution_bitcast_fusion, f32[32,512,64]{1,2,0:T(8,128)} %copy-done.1), kind=kOutput, calls=%fused_computation.4 | convolution fusion | flops 806354944 | bytes 8404992 | tf_op jit(solution)/shard_map/kl,rlc->rkc/dot_general | solution.py:257
  123.8 4.4 %copy.15 = f32[64,32,512]{2,1,0:T(8,128)} copy(f32[64,32,512]{2,0,1:T(8,128)S(1)} %fusion.4) | data formatting | bytes 8388608
  (21 shorter events, 0.2 us)
Async XLA Ops:
  5.6 26.9 %collective-permute-start = (f32[4,72,512]{2,1,0:T(8,128)}, f32[4,72,512]{2,1,0:T(8,128)S(1)}, u32[]{:S(2)}, u32[]{:S(2)}) collective-permute-start(f32[4,72,512]{2,1,0:T(8,128)} %get-tuple-element.12), channel_id=1, source_target_pairs={{0,1},{1,2},{2,3},{3,4},{4,5},{5,6},{6,7},{7,8},{8,9},{9,10},{10,1... | collective-permute-start | bytes 1769480 | tf_op jit(solution)/shard_map/ppermute | solution.py:214
  8.0 24.5 %collective-permute-start.1 = (f32[4,72,512]{2,1,0:T(8,128)}, f32[4,72,512]{2,1,0:T(8,128)S(1)}, u32[]{:S(2)}, u32[]{:S(2)}) collective-permute-start(f32[4,72,512]{2,1,0:T(8,128)} %get-tuple-element.13), channel_id=1, source_target_pairs={{1,0},{2,1},{3,2},{4,3},{5,4},{6,5},{7,6},{8,7},{9,8},{10,9},{11,1... | collective-permute-start | bytes 1769480 | tf_op jit(solution)/shard_map/ppermute | solution.py:215
  32.5 11.8 %copy-start.2 = (f32[24,64,512]{2,1,0:T(8,128)S(1)}, f32[24,64,512]{2,1,0:T(8,128)}, u32[]{:S(2)}) copy-start(f32[24,64,512]{2,1,0:T(8,128)} %get-tuple-element.18) | copy-start | bytes 9437188
  32.5 0.8 copy-start.3
  32.5 1.0 copy-start.4
  43.2 1.6 %copy-start.5 = (f32[4,64,512]{2,1,0:T(8,128)S(1)}, f32[4,64,512]{2,1,0:T(8,128)}, u32[]{:S(2)}) copy-start(f32[4,64,512]{2,1,0:T(8,128)} %get-tuple-element.19) | copy-start | bytes 1572868
  44.8 3.4 %copy-start = (f32[32,64,512]{2,1,0:T(8,128)}, f32[32,64,512]{2,1,0:T(8,128)S(1)}, u32[]{:S(2)}) copy-start(f32[32,64,512]{2,1,0:T(8,128)S(1)} %constant_dynamic-update-slice_fusion) | copy-start | bytes 12582916
  48.2 4.1 %collective-permute-start.2 = (f32[64,64]{0,1:T(8,128)S(1)}, f32[64,64]{0,1:T(8,128)S(1)}, u32[]{:S(2)}, u32[]{:S(2)}) collective-permute-start(f32[64,64]{0,1:T(8,128)S(1)} %convolution_bitcast_fusion.2), channel_id=1, source_target_pairs={{0,1},{1,0},{2,3},{3,2},{4,5},{5,4},{6,7},{7,6},{8,9},{9,8},{10,11... | collective-permute-start | bytes 49160 | tf_op jit(solution)/shard_map/ppermute | solution.py:193
  52.4 3.9 %collective-permute-start.3 = (f32[64,64]{0,1:T(8,128)S(1)}, f32[64,64]{0,1:T(8,128)S(1)}, u32[]{:S(2)}, u32[]{:S(2)}) collective-permute-start(f32[64,64]{0,1:T(8,128)S(1)} %add.33), channel_id=1, source_target_pairs={{0,2},{1,3},{2,0},{3,1},{4,6},{5,7},{6,4},{7,5},{8,10},{9,11},{10,... | collective-permute-start | bytes 49160 | tf_op jit(solution)/shard_map/ppermute | solution.py:193
  56.3 4.6 %collective-permute-start.4 = (f32[64,64]{0,1:T(8,128)S(1)}, f32[64,64]{0,1:T(8,128)S(1)}, u32[]{:S(2)}, u32[]{:S(2)}) collective-permute-start(f32[64,64]{0,1:T(8,128)S(1)} %add.34), channel_id=1, source_target_pairs={{0,4},{1,5},{2,6},{3,7},{4,0},{5,1},{6,2},{7,3},{8,12},{9,13},{10,... | collective-permute-start | bytes 49160 | tf_op jit(solution)/shard_map/ppermute | solution.py:193
  60.9 4.8 %collective-permute-start.5 = (f32[64,64]{0,1:T(8,128)S(1)}, f32[64,64]{0,1:T(8,128)S(1)}, u32[]{:S(2)}, u32[]{:S(2)}) collective-permute-start(f32[64,64]{0,1:T(8,128)S(1)} %add.35), channel_id=1, source_target_pairs={{0,8},{1,9},{2,10},{3,11},{4,12},{5,13},{6,14},{7,15},{8,0},{9,1},... | collective-permute-start | bytes 49160 | tf_op jit(solution)/shard_map/ppermute | solution.py:193
  84.0 2.0 %copy-start.1 = (f32[32,512,64]{1,2,0:T(8,128)}, f32[32,512,64]{1,2,0:T(8,128)S(1)}, u32[]{:S(2)}) copy-start(f32[32,512,64]{1,2,0:T(8,128)S(1)} %fusion.30) | copy-start | bytes 12582916
  89.4 1.3 collective-permute-start.6
  90.7 3.9 %collective-permute-start.7 = (f32[64,64]{0,1:T(8,128)S(1)}, f32[64,64]{0,1:T(8,128)S(1)}, u32[]{:S(2)}, u32[]{:S(2)}) collective-permute-start(f32[64,64]{0,1:T(8,128)S(1)} %add.37), channel_id=1, source_target_pairs={{0,2},{1,3},{2,0},{3,1},{4,6},{5,7},{6,4},{7,5},{8,10},{9,11},{10,... | collective-permute-start | bytes 49160 | tf_op jit(solution)/shard_map/ppermute | solution.py:193
  94.6 3.9 %collective-permute-start.8 = (f32[64,64]{0,1:T(8,128)S(1)}, f32[64,64]{0,1:T(8,128)S(1)}, u32[]{:S(2)}, u32[]{:S(2)}) collective-permute-start(f32[64,64]{0,1:T(8,128)S(1)} %add.38), channel_id=1, source_target_pairs={{0,4},{1,5},{2,6},{3,7},{4,0},{5,1},{6,2},{7,3},{8,12},{9,13},{10,... | collective-permute-start | bytes 49160 | tf_op jit(solution)/shard_map/ppermute | solution.py:193
  98.6 4.8 %collective-permute-start.9 = (f32[64,64]{0,1:T(8,128)S(1)}, f32[64,64]{0,1:T(8,128)S(1)}, u32[]{:S(2)}, u32[]{:S(2)}) collective-permute-start(f32[64,64]{0,1:T(8,128)S(1)} %add.39), channel_id=1, source_target_pairs={{0,8},{1,9},{2,10},{3,11},{4,12},{5,13},{6,14},{7,15},{8,0},{9,1},... | collective-permute-start | bytes 49160 | tf_op jit(solution)/shard_map/ppermute | solution.py:193
where the time goes:
time: 129 us; the launch traced here: 128 us
  Pallas kernels  36.4 us (28%)
  other arithmetic  24.2 us (19%)
  matrix products  21.1 us (16%)
  starting transfers between devices  20.4 us (16%)
  waiting for transfers between devices  14.7 us (11%)
  local copies, waits for them, and re-layouts  10.6 us (8%)
    pallas_call x1, Pallas kernels, responses(): pl.pallas_call(functools.partial(inner_kernel, strength), out_shape=(jax....  23.1 us
    ppermute x8, starting transfers between devices, summed(): lax.ppermute(value, AXIS, [(i, i ^ distance) for i in range(count)])  16.7 us
    ppermute x8, waiting for transfers between devices, summed(): lax.ppermute(value, AXIS, [(i, i ^ distance) for i in range(count)])  14.7 us
    another operation x6, other arithmetic, gram_factor(): return jnp.linalg.cholesky(summed(local_gram))  13.1 us
    dot_general x2, matrix products, on_device(): jnp.einsum('kl,rlc->rkc', inverse, field, precision=lax.Precision.HIGHEST)  11.7 us
    another operation x4, other arithmetic, on_device(): inverse = jax.scipy.linalg.solve_triangular(lower, identity, lower=True)  11 us
    unnamed x16, local copies, waits for them, and re-layouts  10.4 us
    pallas_call x1, Pallas kernels, responses(): pl.pallas_call(functools.partial(edge_kernel, strength, rows), out_shape=...  9.65 us
  transfers between devices with their start and end apart: 10, of which 8 were waited for; matrix products, arithmetic and copies ran while one was open for 0% of the time, Pallas kernels for 18%

commit v1 on v0

v1 whole, which is shorter than its diff:
```python
import functools
import math

import jax
import jax.numpy as jnp
from jax import lax
from jax.experimental import pallas as pl
from jax.experimental.pallas import tpu as pltpu
from jax.sharding import PartitionSpec as P

TIME_STEP = 0.2
IMPULSE_GAIN = 3.0
AXIS = "gx"
DEPTH = 4
PACK = 8
MIB = 1024 * 1024


def rolled(row, by):
    return pltpu.roll(row, by % row.shape[-1], row.ndim - 1)


def weight_row(weights, row, layer, like):
    return jnp.broadcast_to(weights[layer, pl.ds(row, 1), :], like)


def in_steps(first, last, body, step=6):
    whole_steps = (last - first) // step

    def several(index, carry):
        for j in range(step):
            body(first + index * step + j)
        return carry

    lax.fori_loop(0, whole_steps, several, 0)
    for r in range(first + whole_steps * step, last):
        body(r)


def sweep_row(source, at, target, to, probes, columns, center, above, below, left, right):
    for first in range(0, probes, 8):
        octet = slice(first, first + 8)
        middle = source[at, octet, :]
        target[to, octet, :] = (
            center * middle
            + above * source[at - 1, octet, :]
            + below * source[at + 1, octet, :]
            + left * rolled(middle, 1)
            + right * rolled(middle, -1)
        )


def forward_row(source, at, target, to, weights, w_at, probes, columns):
    like = (8, columns)
    sweep_row(
        source, at, target, to, probes, columns,
        *[weight_row(weights, w_at, layer, like) for layer in range(5)],
    )


def adjoint_row(source, at, target, to, weights, w_at, probes, columns):
    like = (8, columns)
    sweep_row(
        source, at, target, to, probes, columns,
        weight_row(weights, w_at, 0, like),
        weight_row(weights, w_at - 1, 2, like),
        weight_row(weights, w_at + 1, 1, like),
        rolled(weight_row(weights, w_at, 4, like), 1),
        rolled(weight_row(weights, w_at, 3, like), -1),
    )


def add_impulses(sites, target, place_of, probes, columns, strength):
    column_ids = lax.broadcasted_iota(jnp.int32, (1, columns), 1)

    def one(k, carry):
        site = sites[k]
        held, place = place_of(lax.div(site, columns))

        @pl.when(held)
        def _():
            hit = jnp.where(column_ids == lax.rem(site, columns), strength, 0.0)
            target[place, pl.ds(k, 1), :] += hit

        return carry

    lax.fori_loop(0, probes, one, 0)


def pack_kernel(cells, kappa, speed, friction, upwind, weights, to_below, to_above, sems):
    probes, rows, columns = cells.shape
    copies = []
    for r in range(DEPTH):
        for side, target in enumerate((to_above, to_below)):
            row = r if side == 0 else rows - DEPTH + r
            copies.append(
                pltpu.make_async_copy(cells.at[:, row, :], target.at[r, pl.ds(0, probes), :], sems.at[side, r])
            )
    for copy in copies:
        copy.start()
    blocks = upwind.shape[0]
    width = columns // blocks
    spread = (
        lax.broadcasted_iota(jnp.int32, (blocks, columns), 1) // width
        == lax.broadcasted_iota(jnp.int32, (blocks, columns), 0)
    ).astype(jnp.bfloat16)
    directions = lax.dot_general(
        upwind[...].astype(jnp.float32).astype(jnp.bfloat16), spread, (((0,), (0,)), ((), ())),
        preferred_element_type=jnp.float32,
    )
    column_ids = lax.broadcasted_iota(jnp.int32, (rows, columns), 1)
    k, s = kappa[...], speed[...]
    layers = [1.0 - TIME_STEP * (4.0 * k + s + friction[...])]
    for direction in range(4):
        chosen = jnp.where(jnp.abs(directions - direction) < 0.5, s, 0.0)
        layers.append(TIME_STEP * (k + chosen))
    layers[3] = jnp.where(column_ids == 0, 0.0, layers[3])
    layers[4] = jnp.where(column_ids == columns - 1, 0.0, layers[4])
    for index, layer in enumerate(layers):
        weights[index] = layer
        for r in range(DEPTH):
            to_above[r, probes + index : probes + index + 1, :] = layer[r : r + 1]
            to_below[r, probes + index : probes + index + 1, :] = layer[rows - DEPTH + r : rows - DEPTH + r + 1]
    for r in range(DEPTH):
        for side in (to_above, to_below):
            side[r, probes + 5 :, :] = jnp.zeros((PACK - 5, columns), jnp.float32)
    for copy in copies:
        copy.wait()


def inner_kernel(
    strength, sites, cells, weights, digits, scale, pairs, top, bottom, v, f1, f2, a1, response, kept, sums, sems, out_sems
):
    rows, probes, columns = v.shape
    first_row = lax.axis_index(AXIS) * rows

    copies = [pltpu.make_async_copy(cells.at[:, r, :], v.at[r], sems.at[r]) for r in range(rows)]
    for copy in copies:
        copy.start()
    for copy in copies:
        copy.wait()
    add_impulses(
        sites, v, lambda row: ((row >= first_row) & (row < first_row + rows), row - first_row), probes, columns, strength
    )

    def sweep(row_fn, source, target, first, shift=0):
        def body(r):
            row_fn(source, r, target, r - shift, weights, r, probes, columns)

        in_steps(first, rows - first, body)

    sweep(forward_row, v, f1, 1)
    sweep(forward_row, f1, f2, 2)
    sweep(adjoint_row, f2, a1, 3)
    sweep(adjoint_row, a1, response, DEPTH, DEPTH)
    for level, field in enumerate((v, f1, f2, a1)):
        for j in range(2):
            top[level, j] = field[level + j]
            bottom[level, j] = field[rows - 2 - level + j]
    high, low = gram_pair(response, rows - 2 * DEPTH, digits, scale, kept, sums, out_sems)
    pairs[...] = jnp.concatenate([folded(high), folded(low)], axis=0)


def edge_kernel(
    strength, rows, sites, above, below, weights, top, bottom, inner_pairs, digits, scale, pairs,
    w, va, la, lb, response, kept, sums, out_sems,
):
    probes, columns = top.shape[2:]
    first_row = lax.axis_index(AXIS) * rows
    start_a, start_b = 2 * DEPTH, 4 * DEPTH
    vb = va.at[DEPTH + 2 :]
    for layer in range(5):
        for r in range(DEPTH):
            w[layer, DEPTH + r : DEPTH + r + 1, :] = above[r, probes + layer : probes + layer + 1, :]
            w[layer, start_b + 2 * DEPTH + r : start_b + 2 * DEPTH + r + 1, :] = below[
                r, probes + layer : probes + layer + 1, :
            ]
        w[layer, start_a : start_a + 8, :] = weights[layer, :8, :]
        w[layer, start_b : start_b + 8, :] = weights[layer, rows - 8 :, :]
    for r in range(DEPTH):
        va[r] = above[r, :probes, :]
        vb[2 + r] = below[r, :probes, :]
    for j in range(2):
        va[DEPTH + j] = top[0, j]
        vb[j] = bottom[0, j]
        for level in range(1, 4):
            la[level - 1, DEPTH + j] = top[level, j]
            lb[level - 1, j] = bottom[level, j]

    def place_of(row):
        near = row - first_row
        is_above = (near >= -DEPTH) & (near < 0)
        is_below = (near >= rows) & (near < rows + DEPTH)
        return is_above | is_below, jnp.where(is_above, near + DEPTH, near - rows + DEPTH + 4)

    add_impulses(sites, va, place_of, probes, columns, strength)
    chain_a = [va, la.at[0], la.at[1], la.at[2], response]
    chain_b = [vb, lb.at[0], lb.at[1], lb.at[2], response]
    for level in range(4):
        row_fn = forward_row if level < 2 else adjoint_row
        for j in range(DEPTH):
            row_fn(chain_a[level], j + 1, chain_a[level + 1], j, w, start_a + level - 3 + j, probes, columns)
            to = j + (DEPTH if level == 3 else 2)
            row_fn(chain_b[level], j + 1, chain_b[level + 1], to, w, start_b + 7 - level + j, probes, columns)
    ours = gram_pair(response, 2 * DEPTH, digits, scale, kept, sums, out_sems)
    half = probes // 2
    high, low = pair_sum(ours, (unfolded(inner_pairs[:half, :]), unfolded(inner_pairs[half:, :])))
    pairs[...] = jnp.concatenate([folded(high), folded(low)], axis=0)


DIGITS = 4
ROUNDER = 12582912.0


def rounded(value):
    return (value + ROUNDER) - ROUNDER


def digits_of(value):
    out = []
    for position in range(DIGITS):
        digit = rounded(value)
        out.append(digit)
        if position < DIGITS - 1:
            value = (value - digit) * 256.0
    return out


def largest_power(fits, like):
    power = jnp.full(like, 2.0**-63, jnp.float32)
    for step in (64, 32, 16, 8, 4, 2, 1):
        candidate = power * 2.0**step
        power = jnp.where((candidate <= 2.0**63) & fits(candidate), candidate, power)
    return power


def unit(size):
    return lax.broadcasted_iota(jnp.int32, (size, size), 0) == lax.broadcasted_iota(jnp.int32, (size, size), 1)


def as_row(column):
    size = column.shape[0]
    return jnp.sum(jnp.where(unit(size), jnp.broadcast_to(column, (size, size)), 0.0), axis=0, keepdims=True)


def pair_of(high, low):
    total = high + low
    return total, low - (total - high)


def pair_sum(a, b):
    (a_high, a_low), (b_high, b_low) = a, b
    total = a_high + b_high
    back = total - a_high
    error = (a_high - (total - back)) + (b_high - back)
    return pair_of(total, error + (a_low + b_low))


def gram_pair(field, rows, cells_out, scale_out, cells, sums, sems):
    probes, columns = field.shape[1:]

    def largest(index, so_far):
        for r in (2 * index, 2 * index + 1):
            so_far = tuple(jnp.maximum(m, jnp.abs(field[r, 8 * o : 8 * o + 8, :])) for o, m in enumerate(so_far))
        return so_far

    tops = lax.fori_loop(0, rows // 2, largest, tuple(jnp.zeros((8, columns), jnp.float32) for _ in range(probes // 8)))
    top = jnp.concatenate([jnp.max(m, axis=1, keepdims=True) for m in tops], axis=0)
    scale = largest_power(lambda power: top * power <= 128.0, (probes, 1))
    inverse = 1.0 / scale
    scale_out[...] = jnp.broadcast_to(inverse, scale_out.shape)
    sums[...] = jnp.zeros_like(sums)

    def cut(index, carry):
        for pair in range(2):
            for r in (4 * index + 2 * pair, 4 * index + 2 * pair + 1):
                parts = digits_of(field[r] * scale)
                cells[r] = jnp.concatenate([part.astype(jnp.bfloat16) for part in parts], axis=0)
                pltpu.make_async_copy(cells.at[r], cells_out.at[r], sems.at[r]).start()
        total = sums[...]
        for pair in range(2):
            r = 4 * index + 2 * pair
            two = jnp.concatenate([cells[r], cells[r + 1]], axis=1)
            product = lax.dot_general(two, two, (((1,), (1,)), ((), ())), preferred_element_type=jnp.float32)
            total = total + product.astype(jnp.int32)
        sums[...] = total
        return carry

    lax.fori_loop(0, rows // 4, cut, 0)
    places = []
    for place in range(2 * DIGITS - 1):
        terms = [
            sums[a * probes : (a + 1) * probes, (place - a) * probes : (place - a + 1) * probes]
            for a in range(DIGITS)
            if 0 <= place - a < DIGITS
        ]
        places.append(functools.reduce(lambda x, y: x + y, terms))
    for place in range(2 * DIGITS - 2, 0, -1):
        places[place - 1] = places[place - 1] + (places[place] >> 8)
        places[place] = places[place] & 255
    f32 = jnp.float32
    high = (places[0] >> 8).astype(f32) * 256.0
    middle = ((places[0] & 255) * 65536 + places[1] * 256 + places[2]).astype(f32) * 2.0**-16
    low = (places[3] * 65536 + places[4] * 256 + places[5]).astype(f32) * 2.0**-40
    total, rest = pair_of(high, middle)
    total, rest = pair_of(total, rest + low)
    across = as_row(inverse)
    def wait(r, carry):
        pltpu.make_async_copy(cells.at[r], cells_out.at[r], sems.at[r]).wait()
        return carry

    lax.fori_loop(0, rows, wait, 0)
    return total * inverse * across, rest * inverse * across


def folded(square):
    half = square.shape[0] // 2
    return jnp.concatenate([square[:half], square[half:]], axis=1)


def unfolded(block):
    half = block.shape[1] // 2
    return jnp.concatenate([block[:, :half], block[:, half:]], axis=0)


def dot(a, b, dims=((1,), (0,))):
    return lax.dot_general(
        a, b, (dims, ((), ())), precision=lax.Precision.HIGHEST, preferred_element_type=jnp.float32
    )


def turned_over(block):
    size, wide = block.shape
    square = jnp.concatenate([block, jnp.zeros((wide - size, wide), jnp.float32)], axis=0)
    return jnp.transpose(square)[:, :size]


def eliminated(block):
    size, wide = block.shape
    groups = [block[8 * g : 8 * g + 8] for g in range(size // 8)]
    like = (8, wide)
    below = lax.broadcasted_iota(jnp.int32, like, 0)
    for j in range(size):
        g, s = divmod(j, 8)
        row = jnp.broadcast_to(groups[g][s : s + 1], like)
        scaled = row / jnp.broadcast_to(row[:, j : j + 1], like)
        for other in range(g, size // 8):
            column = jnp.broadcast_to(groups[other][:, j : j + 1], like)
            if other == g:
                if s == 7:
                    continue
                column = jnp.where(below > s, column, 0.0)
            groups[other] = groups[other] - column * scaled
    return normalised(jnp.concatenate(groups, axis=0))


def normalised(block):
    size, wide = block.shape
    row_ids = lax.broadcasted_iota(jnp.int32, block.shape, 0)
    lanes = lax.broadcasted_iota(jnp.int32, block.shape, 1)
    pivots = jnp.sum(jnp.where(row_ids == lanes, block, 0.0), axis=1, keepdims=True)
    scale = lax.rsqrt(pivots)
    scale = scale * (1.5 - 0.5 * pivots * scale * scale)
    block = block * scale
    keep = (lanes >= row_ids) & ((lanes < size) | (lanes - size <= row_ids))
    return jnp.where(keep, block, 0.0)


def eliminated_slowly(block, work):
    size, wide = block.shape
    work[...] = block
    row_ids = lax.broadcasted_iota(jnp.int32, (size, 1), 0)
    lanes = lax.broadcasted_iota(jnp.int32, (1, wide), 1)

    def step(j, carry):
        row = work[pl.ds(j, 1), :]
        pivot = jnp.sum(jnp.where(lanes == j, row, 0.0), axis=1, keepdims=True)
        column = jnp.sum(jnp.where(lanes == j, work[...], 0.0), axis=1, keepdims=True)
        work[...] = work[...] - jnp.where(row_ids > j, column, 0.0) * (row / pivot)
        return carry

    lax.fori_loop(0, size, step, 0)
    return normalised(work[...])


def stacked_digits(value):
    return jnp.concatenate([part.astype(jnp.bfloat16) for part in digits_of(value)], axis=0)


def residual(high, low, left, right):
    size = high.shape[0]
    product = lax.dot_general(left, right, (((1,), (1,)), ((), ())), preferred_element_type=jnp.float32)
    places = []
    for place in range(2 * DIGITS - 1):
        terms = [
            product[a * size : (a + 1) * size, (place - a) * size : (place - a + 1) * size]
            for a in range(DIGITS)
            if 0 <= place - a < DIGITS
        ]
        places.append(functools.reduce(lambda x, y: x + y, terms))
    rest = high
    total = jnp.zeros_like(high)
    for place in range(5):
        if place == 2:
            rest = rest + low * 2.0**16
        digit = rounded(rest) if place < 4 else rest
        rest = (rest - digit) * 256.0
        total = total * 256.0 + (digit - places[place])
    total = total - (places[5] * 2.0**-8 + places[6] * 2.0**-16)
    return total * 2.0**-32


def solve_kernel(
    cell_scale, pairs, inner_scale, edge_scale, inner, edge, basis, factor,
    inner_cells, edge_cells, rows_out, work, change, change_inverse, in_sems, out_sems,
):
    size = pairs.shape[0]
    inner_rows, edge_rows = inner.shape[0], edge.shape[0]
    rows = inner_rows + edge_rows
    loads = [
        pltpu.make_async_copy(inner, inner_cells, in_sems.at[0]),
        pltpu.make_async_copy(edge, edge_cells, in_sems.at[1]),
    ]
    for copy in loads:
        copy.start()
    high, low = unfolded(pairs[: size // 2, :]), unfolded(pairs[size // 2 :, :])
    is_diagonal = unit(size)
    diagonal = jnp.sum(jnp.where(is_diagonal, high, 0.0), axis=1, keepdims=True)
    scale = largest_power(lambda power: diagonal * power * power < 1.0, (size, 1))
    across = as_row(scale)
    high, low = high * scale * across, low * scale * across
    identity = jnp.where(is_diagonal, 1.0, 0.0)
    first = eliminated(jnp.concatenate([high, identity], axis=1))
    inverse = first[:, size:]
    lower = turned_over(first)[:size]
    lower_digits = stacked_digits(lower * 128.0)
    missed = residual(high * 2.0**14, low * 2.0**14, lower_digits, lower_digits) * 2.0**-14
    inverse_top = jnp.max(jnp.abs(inverse), axis=1, keepdims=True)
    inverse_scale = largest_power(lambda power: inverse_top * power <= 128.0, (size, 1))
    goal = identity * (inverse_scale * 128.0)
    skew = residual(
        goal, jnp.zeros_like(goal), stacked_digits(inverse * inverse_scale), stacked_digits(first[:, :size] * 128.0)
    ) * (-1.0 / 128.0 / inverse_scale)
    near = identity + skew
    error = dot(dot(inverse, missed), inverse, ((1,), (1,))) + (dot(near, near, ((1,), (1,))) - identity)
    weight = jnp.where(
        is_diagonal, 0.5,
        jnp.where(
            lax.broadcasted_iota(jnp.int32, (size, size), 0) > lax.broadcasted_iota(jnp.int32, (size, size), 1), 1.0, 0.0
        ),
    )
    spread = jnp.sum(error * error)
    is_small = spread < 4e-4

    @pl.when(is_small)
    def _():
        y = weight * error
        for _ in range(4):
            y = weight * (error - dot(y, y, ((1,), (1,))))
        change[...] = y
        square = dot(y, y)
        change_inverse[...] = (identity - y) + dot(identity - y, square)

    @pl.when(jnp.logical_not(is_small))
    def _():
        second = eliminated_slowly(jnp.concatenate([identity + error, identity], axis=1), work)
        change[...] = turned_over(second)[:size] - identity
        change_inverse[...] = second[:, size:]

    turn = change[...] - skew
    full = lower + dot(lower, turn - dot(skew, turn))
    full = jnp.concatenate([full, jnp.zeros_like(full)], axis=1)
    factor[...] = turned_over(full)[:size] / across * (1.0 / cell_scale)
    mixing = dot(change_inverse[...], inverse) * across * cell_scale

    def stacked(cut):
        whole_part = mixing * as_row(cut[:, :1])
        pieces = []
        for _ in range(3):
            piece = whole_part.astype(jnp.bfloat16)
            whole_part = whole_part - piece.astype(jnp.float32)
            pieces.append(piece.astype(jnp.float32))
        tall = jnp.concatenate(pieces, axis=0)
        return jnp.concatenate([tall * 256.0**-a for a in range(DIGITS)], axis=1).astype(jnp.bfloat16)

    def finish(matrix, cells, first_row, count, shift):
        def one(r, carry):
            product = jnp.dot(matrix, cells[r + shift], preferred_element_type=jnp.float32)
            rows_out[r + first_row] = product[:size] + (product[size : 2 * size] + product[2 * size :])
            pltpu.make_async_copy(rows_out.at[r + first_row], basis.at[:, r + first_row, :], out_sems.at[r + first_row]).start()
            return carry

        lax.fori_loop(0, count, one, 0, unroll=4)

    for copy in loads:
        copy.wait()
    finish(stacked(inner_scale), inner_cells, DEPTH, inner_rows, 0)
    matrix = stacked(edge_scale)
    finish(matrix, edge_cells, 0, DEPTH, 0)
    finish(matrix, edge_cells, rows - DEPTH, DEPTH, DEPTH)

    def wait(r, carry):
        pltpu.make_async_copy(rows_out.at[r], basis.at[:, r, :], out_sems.at[r]).wait()
        return carry

    lax.fori_loop(0, rows, wait, 0)


def whole(memory=pltpu.VMEM):
    return pl.BlockSpec(memory_space=memory)


def call(kernel, name, out_shape, in_specs, out_specs, scratch_shapes=(), cost=None):
    return pl.pallas_call(
        kernel,
        out_shape=out_shape,
        in_specs=in_specs,
        out_specs=out_specs,
        scratch_shapes=scratch_shapes,
        compiler_params=pltpu.CompilerParams(vmem_limit_bytes=56 * MIB),
        cost_estimate=cost,
        name=name,
    )


def summed(pairs):
    count = lax.axis_size(AXIS)
    half = pairs.shape[0] // 2

    def add(a, b):
        return jnp.concatenate(pair_sum((a[:half], a[half:]), (b[:half], b[half:])), axis=0)

    if count & (count - 1):
        total = pairs
        for step in range(1, count):
            total = add(total, lax.ppermute(pairs, AXIS, [(i, (i + step) % count) for i in range(count)]))
        return total
    distance = 1
    while distance < count:
        pairs = add(pairs, lax.ppermute(pairs, AXIS, [(i, i ^ distance) for i in range(count)]))
        distance *= 2
    return pairs


def on_device(probes, kappa, speed, friction, upwind, probe_sites):
    count, rows, columns = probes.shape
    size = lax.axis_size(AXIS)
    f32 = jnp.float32
    cell_scale = math.sqrt(rows * columns * size)
    strength = IMPULSE_GAIN * cell_scale
    shape = jax.ShapeDtypeStruct
    halo = shape((DEPTH, count + PACK, columns), f32)
    weights, to_below, to_above = call(
        pack_kernel,
        "pack",
        (shape((5, rows, columns), f32), halo, halo),
        [whole(pl.ANY), whole(), whole(), whole(), whole()],
        (whole(), whole(), whole()),
        [pltpu.SemaphoreType.DMA((2, DEPTH))],
    )(probes, kappa, speed, friction, upwind.T)
    from_above = lax.ppermute(to_below, AXIS, [(i, i + 1) for i in range(size - 1)])
    from_below = lax.ppermute(to_above, AXIS, [(i + 1, i) for i in range(size - 1)])
    edge_count = 2 * DEPTH
    inner_count = rows - edge_count
    tall = DIGITS * count

    def digit_rows(number):
        return shape((number, tall, columns), jnp.bfloat16), shape((count, 128), f32), shape((count, 2 * count), f32)

    def digit_scratch(number):
        return [
            pltpu.VMEM((number, count, columns), f32),
            pltpu.VMEM((number, tall, columns), jnp.bfloat16),
            pltpu.VMEM((tall, tall), jnp.int32),
        ]

    kept = shape((4, 2, count, columns), f32)
    field = pltpu.VMEM((rows, count, columns), f32)
    inner, inner_scale, pairs, top, bottom = call(
        functools.partial(inner_kernel, strength),
        "inner_rows",
        digit_rows(inner_count) + (kept, kept),
        [whole(pltpu.SMEM), whole(pl.ANY), whole()],
        (whole(pl.ANY), whole(), whole(), whole(), whole()),
        [field] * 4
        + digit_scratch(inner_count)
        + [pltpu.SemaphoreType.DMA((rows,)), pltpu.SemaphoreType.DMA((inner_count,))],
        pl.CostEstimate(flops=10**10, bytes_accessed=16 * MIB, transcendentals=0),
    )(probe_sites, probes, weights)
    fields = pltpu.VMEM((2 * DEPTH + 4, count, columns), f32)
    levels = pltpu.VMEM((3, DEPTH + 2, count, columns), f32)
    edge, edge_scale, pairs = call(
        functools.partial(edge_kernel, strength, rows),
        "edge_rows",
        digit_rows(edge_count),
        [whole(pltpu.SMEM)] + [whole()] * 6,
        (whole(pl.ANY), whole(), whole()),
        [pltpu.VMEM((5, 8 * DEPTH, columns), f32), fields, levels, levels]
        + digit_scratch(edge_count)
        + [pltpu.SemaphoreType.DMA((edge_count,))],
    )(probe_sites, from_above, from_below, weights, top, bottom, pairs)
    pairs = summed(pairs)
    square = pltpu.VMEM((count, count), f32)
    return call(
        functools.partial(solve_kernel, cell_scale),
        "solve",
        (shape((count, rows, columns), f32), shape((count, count), f32)),
        [whole(), whole(), whole(), whole(pl.ANY), whole(pl.ANY)],
        (whole(pl.ANY), whole()),
        [
            pltpu.VMEM((inner_count, tall, columns), jnp.bfloat16),
            pltpu.VMEM((edge_count, tall, columns), jnp.bfloat16),
            pltpu.VMEM((rows, count, columns), f32),
            pltpu.VMEM((count, 2 * count), f32),
            square,
            square,
            pltpu.SemaphoreType.DMA((2,)),
            pltpu.SemaphoreType.DMA((rows,)),
        ],
    )(pairs, inner_scale, edge_scale, inner, edge)


def solution(mesh):
    return jax.shard_map(
        on_device,
        mesh=mesh,
        in_specs=(
            P(None, ("groups", "gx"), None),
            P(("groups", "gx"), None),
            P(("groups", "gx"), None),
            P(("groups", "gx"), None),
            P(("groups", "gx"), None),
            P("groups"),
        ),
        out_specs=(P(None, ("groups", "gx"), None), P("groups", None)),
        check_vma=False,
    )
```

time: 129 us -> 80.4 us (0.62)
  other arithmetic: 24.2 us -> 1.43 us
  matrix products: 21.1 us -> 0 us
  Pallas kernels: 36.4 us -> 54.9 us
  local copies, waits for them, and re-layouts: 10.6 us -> 1 us
  waiting for transfers between devices: 14.7 us -> 7.03 us
  starting transfers between devices: 20.4 us -> 14.8 us
    another operation x10 -> x0, other arithmetic: 24.1 us -> none  [the longest x6 13.1 us: gram_factor(): return jnp.linalg.cholesky(summed(local_gram))]
    dot_general x5 -> x0, matrix products: 20.6 us -> none  [the longest x2 11.7 us: on_device(): jnp.einsum('kl,rlc->rkc', inverse, field, precision=lax.Precision.HIGHEST)]
    pallas_call x3 -> x4, Pallas kernels: 36.4 us -> 54.9 us  [the longest x1 21.7 us: on_device(): call(functools.partial(inner_kernel, strength), 'inner_rows', digit_rows(...]
    unnamed x16 -> x4, local copies, waits for them, and re-layouts: 10.4 us -> 1 us
    ppermute x10 -> x6, waiting for transfers between devices: 14.7 us -> 7.03 us  [the longest x4 7.03 us: summed(): lax.ppermute(pairs, AXIS, [(i, i ^ distance) for i in range(count)])]
    ppermute x10 -> x6, starting transfers between devices: 20.4 us -> 14.8 us  [the longest x4 11.1 us: summed(): lax.ppermute(pairs, AXIS, [(i, i ^ distance) for i in range(count)])]
  transfers between devices with their start and end apart: 10 -> 6, of which waited for: 8 -> 4; matrix products, arithmetic and copies ran while one was open for 0% -> 0% of each run, Pallas kernels for 18% -> 27%
where the time goes in v1:
time: 80.4 us; the launch traced here: 79.9 us
  Pallas kernels  54.9 us (68%)
  starting transfers between devices  14.8 us (18%)
  waiting for transfers between devices  7.03 us (9%)
  other arithmetic  1.43 us (2%)
  local copies, waits for them, and re-layouts  1 us (1%)
    pallas_call x1, Pallas kernels, on_device(): call(functools.partial(inner_kernel, strength), 'inner_rows', digit_rows(...  21.7 us
    pallas_call x1, Pallas kernels, on_device(): call(functools.partial(solve_kernel, cell_scale), 'solve', (shape((count,...  20.5 us
    ppermute x4, starting transfers between devices, summed(): lax.ppermute(pairs, AXIS, [(i, i ^ distance) for i in range(count)])  11.1 us
    pallas_call x1, Pallas kernels, on_device(): call(functools.partial(edge_kernel, strength, rows), 'edge_rows', digit_r...  9.2 us
    ppermute x4, waiting for transfers between devices, summed(): lax.ppermute(pairs, AXIS, [(i, i ^ distance) for i in range(count)])  7.03 us
    pallas_call x1, Pallas kernels, on_device(): call(pack_kernel, 'pack', (shape((5, rows, columns), f32), halo, halo), [...  3.53 us
    ppermute x1, starting transfers between devices, on_device(): lax.ppermute(to_below, AXIS, [(i, i + 1) for i in range(size - 1)])  2.39 us
  transfers between devices with their start and end apart: 6, of which 4 were waited for; matrix products, arithmetic and copies ran while one was open for 0% of the time, Pallas kernels for 27%

profile of v1, /device:TPU:0, one launch (start us, length us, event | category | flops | bytes accessed | tf_op | source)
XLA Modules:
  0.0 79.9 jit_solution(10219931640951837354)
XLA Ops:
  0.6 3.5 %pack.1 = (f32[5,32,512]{2,1,0:T(8,128)}, f32[4,72,512]{2,1,0:T(8,128)}, f32[4,72,512]{2,1,0:T(8,128)}) custom-call(f32[64,32,512]{2,1,0:T(8,128)} %cells.3, f32[32,512]{1,0:T(8,128)} %kappa.1, f32[32,512]{1,0:T(8,128)} %speed.1, f32[32,512]{1,0:T(8,128)} %friction.1, s32[16,32]{1,0:T(8,128)} %bitcast.1), custom_call_target="tpu_custom_call" | custom-call | tf_op jit(solution)/shard_map/pack/pallas_call | solution.py:553
  4.2 2.4 %collective-permute-start = (f32[4,72,512]{2,1,0:T(8,128)}, f32[4,72,512]{2,1,0:T(8,128)S(1)}, u32[]{:S(2)}, u32[]{:S(2)}) collective-permute-start(f32[4,72,512]{2,1,0:T(8,128)} %get-tuple-element.13), channel_id=1, source_target_pairs={{0,1},{1,2},{2,3},{3,4},{4,5},{5,6},{6,7},{7,8},{8,9},{9,10},{10,1... | collective-permute-start | bytes 1769480 | tf_op jit(solution)/shard_map/ppermute | solution.py:561
  6.6 1.3 %collective-permute-start.1 = (f32[4,72,512]{2,1,0:T(8,128)}, f32[4,72,512]{2,1,0:T(8,128)S(1)}, u32[]{:S(2)}, u32[]{:S(2)}) collective-permute-start(f32[4,72,512]{2,1,0:T(8,128)} %get-tuple-element.14), channel_id=1, source_target_pairs={{1,0},{2,1},{3,2},{4,3},{5,4},{6,5},{7,6},{8,7},{9,8},{10,9},{11,1... | collective-permute-start | bytes 1769480 | tf_op jit(solution)/shard_map/ppermute | solution.py:562
  7.9 21.7 %inner_rows.1 = (bf16[24,256,512]{2,1,0:T(8,128)(2,1)}, f32[64,128]{1,0:T(8,128)}, f32[64,128]{1,0:T(8,128)}, f32[4,2,64,512]{3,2,1,0:T(8,128)}, f32[4,2,64,512]{3,2,1,0:T(8,128)}) custom-call(s32[64]{0:T(128)} %sites.3, f32[64,32,512]{2,1,0:T(8,128)} %cells.3, f32[5,32,512]{2,1,0:T(8,128)} %get-tuple-element.15.weights), custom_call_target="tpu_custom_call" | custom-call | flops 10000000000 | bytes 16777216 | tf_op jit(solution)/shard_map/inner_rows/pallas_call | solution.py:579
  29.5 0.0 collective-permute-done.above
  29.6 0.0 copy-start
  29.6 0.0 collective-permute-done.1.below
  29.6 0.0 copy-start.1
  29.6 0.8 copy-done
  30.4 0.2 copy-done.1
  30.6 9.2 %edge_rows.1 = (bf16[8,256,512]{2,1,0:T(8,128)(2,1)}, f32[64,128]{1,0:T(8,128)}, f32[64,128]{1,0:T(8,128)}) custom-call(s32[64]{0:T(128)} %sites.3, f32[4,72,512]{2,1,0:T(8,128)} %copy-done, f32[4,72,512]{2,1,0:T(8,128)} %copy-done.1, f32[5,32,512]{2,1,0:T(8,128)} %get-tuple-element.15.weights, f32[4,2,64,512]{3,2,1,0:T(8,128)} %get-tuple-element.16.top, ...), custom_call_target="tpu_custom_call" | custom-call | tf_op jit(solution)/shard_map/edge_rows/pallas_call | solution.py:592
  39.8 3.2 %collective-permute-start.2 = (f32[64,128]{1,0:T(8,128)}, f32[64,128]{1,0:T(8,128)S(1)}, u32[]{:S(2)}, u32[]{:S(2)}) collective-permute-start(f32[64,128]{1,0:T(8,128)} %get-tuple-element.19), channel_id=1, source_target_pairs={{0,1},{1,0},{2,3},{3,2},{4,5},{5,4},{6,7},{7,6},{8,9},{9,8},{10,11... | collective-permute-start | bytes 98312 | tf_op jit(solution)/shard_map/ppermute | solution.py:540
  43.0 1.1 %collective-permute-done.2 = f32[64,128]{1,0:T(8,128)S(1)} collective-permute-done((f32[64,128]{1,0:T(8,128)}, f32[64,128]{1,0:T(8,128)S(1)}, u32[]{:S(2)}, u32[]{:S(2)}) %collective-permute-start.2) | collective-permute-done | bytes 32800 | tf_op jit(solution)/shard_map/ppermute | solution.py:540
  44.1 0.7 subtract_subtract_fusion.3
  44.9 1.8 %collective-permute-start.3 = (f32[64,128]{1,0:T(8,128)S(1)}, f32[64,128]{1,0:T(8,128)S(1)}, u32[]{:S(2)}, u32[]{:S(2)}) collective-permute-start(f32[64,128]{1,0:T(8,128)S(1)} %pad_maximum_fusion), channel_id=1, source_target_pairs={{0,2},{1,3},{2,0},{3,1},{4,6},{5,7},{6,4},{7,5},{8,10},{9,11},{10,... | collective-permute-start | bytes 98312 | tf_op jit(solution)/shard_map/ppermute | solution.py:540
  46.7 2.2 %collective-permute-done.3 = f32[64,128]{1,0:T(8,128)S(1)} collective-permute-done((f32[64,128]{1,0:T(8,128)S(1)}, f32[64,128]{1,0:T(8,128)S(1)}, u32[]{:S(2)}, u32[]{:S(2)}) %collective-permute-start.3) | collective-permute-done | bytes 32800 | tf_op jit(solution)/shard_map/ppermute | solution.py:540
  48.9 2.7 %collective-permute-start.4 = (f32[64,128]{1,0:T(8,128)S(1)}, f32[64,128]{1,0:T(8,128)S(1)}, u32[]{:S(2)}, u32[]{:S(2)}) collective-permute-start(f32[64,128]{1,0:T(8,128)S(1)} %pad_maximum_fusion.1), channel_id=1, source_target_pairs={{0,4},{1,5},{2,6},{3,7},{4,0},{5,1},{6,2},{7,3},{8,12},{9,13},{10,... | collective-permute-start | bytes 98312 | tf_op jit(solution)/shard_map/ppermute | solution.py:540
  51.6 1.9 %collective-permute-done.4 = f32[64,128]{1,0:T(8,128)S(1)} collective-permute-done((f32[64,128]{1,0:T(8,128)S(1)}, f32[64,128]{1,0:T(8,128)S(1)}, u32[]{:S(2)}, u32[]{:S(2)}) %collective-permute-start.4) | collective-permute-done | bytes 32800 | tf_op jit(solution)/shard_map/ppermute | solution.py:540
  53.5 3.3 %collective-permute-start.5 = (f32[64,128]{1,0:T(8,128)S(1)}, f32[64,128]{1,0:T(8,128)S(1)}, u32[]{:S(2)}, u32[]{:S(2)}) collective-permute-start(f32[64,128]{1,0:T(8,128)S(1)} %pad_maximum_fusion.2), channel_id=1, source_target_pairs={{0,8},{1,9},{2,10},{3,11},{4,12},{5,13},{6,14},{7,15},{8,0},{9,1},... | collective-permute-start | bytes 98312 | tf_op jit(solution)/shard_map/ppermute | solution.py:540
  56.8 1.9 %collective-permute-done.5 = f32[64,128]{1,0:T(8,128)S(1)} collective-permute-done((f32[64,128]{1,0:T(8,128)S(1)}, f32[64,128]{1,0:T(8,128)S(1)}, u32[]{:S(2)}, u32[]{:S(2)}) %collective-permute-start.5) | collective-permute-done | bytes 32800 | tf_op jit(solution)/shard_map/ppermute | solution.py:540
  58.7 0.6 pad_maximum_fusion.3.pairs
  59.4 20.5 %solve.1 = (f32[64,32,512]{2,1,0:T(8,128)}, f32[64,64]{1,0:T(8,128)}) custom-call(f32[64,128]{1,0:T(8,128)} %pad_maximum_fusion.3.pairs, f32[64,128]{1,0:T(8,128)} %get-tuple-element.20.inner_scale, f32[64,128]{1,0:T(8,128)} %get-tuple-element.21.edge_scale, bf16[24,256,512]{2,1,0:T(8,128)(2,1)} %get-tuple-element.22.inner, ...), custom_call_target="tpu_custom_call" | custom-call | tf_op jit(solution)/shard_map/solve/pallas_call | solution.py:604
  (6 shorter events, 0.1 us)
Async XLA Ops:
  4.2 25.4 %collective-permute-start = (f32[4,72,512]{2,1,0:T(8,128)}, f32[4,72,512]{2,1,0:T(8,128)S(1)}, u32[]{:S(2)}, u32[]{:S(2)}) collective-permute-start(f32[4,72,512]{2,1,0:T(8,128)} %get-tuple-element.13), channel_id=1, source_target_pairs={{0,1},{1,2},{2,3},{3,4},{4,5},{5,6},{6,7},{7,8},{8,9},{9,10},{10,1... | collective-permute-start | bytes 1769480 | tf_op jit(solution)/shard_map/ppermute | solution.py:561
  6.6 23.0 %collective-permute-start.1 = (f32[4,72,512]{2,1,0:T(8,128)}, f32[4,72,512]{2,1,0:T(8,128)S(1)}, u32[]{:S(2)}, u32[]{:S(2)}) collective-permute-start(f32[4,72,512]{2,1,0:T(8,128)} %get-tuple-element.14), channel_id=1, source_target_pairs={{1,0},{2,1},{3,2},{4,3},{5,4},{6,5},{7,6},{8,7},{9,8},{10,9},{11,1... | collective-permute-start | bytes 1769480 | tf_op jit(solution)/shard_map/ppermute | solution.py:562
  29.6 0.8 %copy-start = (f32[4,72,512]{2,1,0:T(8,128)}, f32[4,72,512]{2,1,0:T(8,128)S(1)}, u32[]{:S(2)}) copy-start(f32[4,72,512]{2,1,0:T(8,128)S(1)} %collective-permute-done.above) | copy-start | bytes 1769476
  29.6 1.0 %copy-start.1 = (f32[4,72,512]{2,1,0:T(8,128)}, f32[4,72,512]{2,1,0:T(8,128)S(1)}, u32[]{:S(2)}) copy-start(f32[4,72,512]{2,1,0:T(8,128)S(1)} %collective-permute-done.1.below) | copy-start | bytes 1769476
  39.8 4.3 %collective-permute-start.2 = (f32[64,128]{1,0:T(8,128)}, f32[64,128]{1,0:T(8,128)S(1)}, u32[]{:S(2)}, u32[]{:S(2)}) collective-permute-start(f32[64,128]{1,0:T(8,128)} %get-tuple-element.19), channel_id=1, source_target_pairs={{0,1},{1,0},{2,3},{3,2},{4,5},{5,4},{6,7},{7,6},{8,9},{9,8},{10,11... | collective-permute-start | bytes 98312 | tf_op jit(solution)/shard_map/ppermute | solution.py:540
  44.9 4.0 %collective-permute-start.3 = (f32[64,128]{1,0:T(8,128)S(1)}, f32[64,128]{1,0:T(8,128)S(1)}, u32[]{:S(2)}, u32[]{:S(2)}) collective-permute-start(f32[64,128]{1,0:T(8,128)S(1)} %pad_maximum_fusion), channel_id=1, source_target_pairs={{0,2},{1,3},{2,0},{3,1},{4,6},{5,7},{6,4},{7,5},{8,10},{9,11},{10,... | collective-permute-start | bytes 98312 | tf_op jit(solution)/shard_map/ppermute | solution.py:540
  48.9 4.6 %collective-permute-start.4 = (f32[64,128]{1,0:T(8,128)S(1)}, f32[64,128]{1,0:T(8,128)S(1)}, u32[]{:S(2)}, u32[]{:S(2)}) collective-permute-start(f32[64,128]{1,0:T(8,128)S(1)} %pad_maximum_fusion.1), channel_id=1, source_target_pairs={{0,4},{1,5},{2,6},{3,7},{4,0},{5,1},{6,2},{7,3},{8,12},{9,13},{10,... | collective-permute-start | bytes 98312 | tf_op jit(solution)/shard_map/ppermute | solution.py:540
  53.5 5.2 %collective-permute-start.5 = (f32[64,128]{1,0:T(8,128)S(1)}, f32[64,128]{1,0:T(8,128)S(1)}, u32[]{:S(2)}, u32[]{:S(2)}) collective-permute-start(f32[64,128]{1,0:T(8,128)S(1)} %pad_maximum_fusion.2), channel_id=1, source_target_pairs={{0,8},{1,9},{2,10},{3,11},{4,12},{5,13},{6,14},{7,15},{8,0},{9,1},... | collective-permute-start | bytes 98312 | tf_op jit(solution)/shard_map/ppermute | solution.py:540

commit v2 on v1

--- a/solution.py
+++ b/solution.py
@@ -70,24 +70,28 @@
     )
 
 
-def add_impulses(sites, target, place_of, probes, columns, strength):
+def find_impulses(sites, found, held, probes, columns):
+    def one(k, count):
+        found[count] = k
+        return count + held(lax.div(sites[k], columns)).astype(jnp.int32)
+
+    return lax.fori_loop(0, probes, one, 0)
+
+
+def add_impulses(sites, found, count, target, place_of, columns, strength):
     column_ids = lax.broadcasted_iota(jnp.int32, (1, columns), 1)
 
-    def one(k, carry):
+    def one(index, carry):
+        k = found[index]
         site = sites[k]
-        held, place = place_of(lax.div(site, columns))
-
-        @pl.when(held)
-        def _():
-            hit = jnp.where(column_ids == lax.rem(site, columns), strength, 0.0)
-            target[place, pl.ds(k, 1), :] += hit
-
+        hit = jnp.where(column_ids == lax.rem(site, columns), strength, 0.0)
+        target[place_of(lax.div(site, columns)), pl.ds(k, 1), :] += hit
         return carry
 
-    lax.fori_loop(0, probes, one, 0)
-
-
-def pack_kernel(cells, kappa, speed, friction, upwind, weights, to_below, to_above, sems):
+    lax.fori_loop(0, count, one, 0)
+
+
+def pack_kernel(cells, kappa, speed, friction, upwind, weights, to_below, to_above, behind, sems):
     probes, rows, columns = cells.shape
     copies = []
     for r in range(DEPTH):
@@ -119,17 +123,20 @@
     for index, layer in enumerate(layers):
         weights[index] = layer
         for r in range(DEPTH):
-            to_above[r, probes + index : probes + index + 1, :] = layer[r : r + 1]
-            to_below[r, probes + index : probes + index + 1, :] = layer[rows - DEPTH + r : rows - DEPTH + r + 1]
-    for r in range(DEPTH):
-        for side in (to_above, to_below):
-            side[r, probes + 5 :, :] = jnp.zeros((PACK - 5, columns), jnp.float32)
+            behind[0, r, index : index + 1, :] = layer[r : r + 1]
+            behind[1, r, index : index + 1, :] = layer[rows - DEPTH + r : rows - DEPTH + r + 1]
+    behind[:, :, 5:, :] = jnp.zeros((2, DEPTH, PACK - 5, columns), jnp.float32)
+    for side, target in enumerate((to_above, to_below)):
+        copies.append(
+            pltpu.make_async_copy(behind.at[side], target.at[:, pl.ds(probes, PACK), :], sems.at[side, DEPTH])
+        )
+        copies[-1].start()
     for copy in copies:
         copy.wait()
 
 
 def inner_kernel(
-    strength, sites, cells, weights, digits, scale, pairs, top, bottom, v, f1, f2, a1, response, kept, sums, sems, out_sems
+    strength, sites, cells, weights, digits, scale, pairs, top, bottom, v, f1, f2, a1, response, kept, sums, found, sems, out_sems
 ):
     rows, probes, columns = v.shape
     first_row = lax.axis_index(AXIS) * rows
@@ -137,11 +144,12 @@
     copies = [pltpu.make_async_copy(cells.at[:, r, :], v.at[r], sems.at[r]) for r in range(rows)]
     for copy in copies:
         copy.start()
+    hits = find_impulses(
+        sites, found, lambda row: (row >= first_row) & (row < first_row + rows), probes, columns
+    )
     for copy in copies:
         copy.wait()
-    add_impulses(
-        sites, v, lambda row: ((row >= first_row) & (row < first_row + rows), row - first_row), probes, columns, strength
-    )
+    add_impulses(sites, found, hits, v, lambda row: row - first_row, columns, strength)
 
     def sweep(row_fn, source, target, first, shift=0):
         def body(r):
@@ -163,37 +171,45 @@
 
 def edge_kernel(
     strength, rows, sites, above, below, weights, top, bottom, inner_pairs, digits, scale, pairs,
-    w, va, la, lb, response, kept, sums, out_sems,
+    w, va, la, lb, behind, response, kept, sums, found, sems, out_sems,
 ):
     probes, columns = top.shape[2:]
     first_row = lax.axis_index(AXIS) * rows
     start_a, start_b = 2 * DEPTH, 4 * DEPTH
     vb = va.at[DEPTH + 2 :]
+    copies = [
+        (above.at[:, pl.ds(probes, PACK), :], behind.at[0]),
+        (below.at[:, pl.ds(probes, PACK), :], behind.at[1]),
+        (weights.at[:, pl.ds(0, 8), :], w.at[:, pl.ds(start_a, 8), :]),
+        (weights.at[:, pl.ds(rows - 8, 8), :], w.at[:, pl.ds(start_b, 8), :]),
+        (above.at[:, pl.ds(0, probes), :], va.at[pl.ds(0, DEPTH)]),
+        (below.at[:, pl.ds(0, probes), :], va.at[pl.ds(DEPTH + 4, DEPTH)]),
+        (top.at[0], va.at[pl.ds(DEPTH, 2)]),
+        (bottom.at[0], va.at[pl.ds(DEPTH + 2, 2)]),
+        (top.at[pl.ds(1, 3)], la.at[:, pl.ds(DEPTH, 2)]),
+        (bottom.at[pl.ds(1, 3)], lb.at[:, pl.ds(0, 2)]),
+    ]
+    copies = [pltpu.make_async_copy(source, target, sems.at[i]) for i, (source, target) in enumerate(copies)]
+    for copy in copies:
+        copy.start()
+
+    def is_above(row):
+        return (row >= first_row - DEPTH) & (row < first_row)
+
+    def held(row):
+        return is_above(row) | ((row >= first_row + rows) & (row < first_row + rows + DEPTH))
+
+    hits = find_impulses(sites, found, held, probes, columns)
+    for copy in copies:
+        copy.wait()
     for layer in range(5):
         for r in range(DEPTH):
-            w[layer, DEPTH + r : DEPTH + r + 1, :] = above[r, probes + layer : probes + layer + 1, :]
-            w[layer, start_b + 2 * DEPTH + r : start_b + 2 * DEPTH + r + 1, :] = below[
-                r, probes + layer : probes + layer + 1, :
-            ]
-        w[layer, start_a : start_a + 8, :] = weights[layer, :8, :]
-        w[layer, start_b : start_b + 8, :] = weights[layer, rows - 8 :, :]
-    for r in range(DEPTH):
-        va[r] = above[r, :probes, :]
-        vb[2 + r] = below[r, :probes, :]
-    for j in range(2):
-        va[DEPTH + j] = top[0, j]
-        vb[j] = bottom[0, j]
-        for level in range(1, 4):
-            la[level - 1, DEPTH + j] = top[level, j]
-            lb[level - 1, j] = bottom[level, j]
-
-    def place_of(row):
-        near = row - first_row
-        is_above = (near >= -DEPTH) & (near < 0)
-        is_below = (near >= rows) & (near < rows + DEPTH)
-        return is_above | is_below, jnp.where(is_above, near + DEPTH, near - rows + DEPTH + 4)
-
-    add_impulses(sites, va, place_of, probes, columns, strength)
+            w[layer, DEPTH + r : DEPTH + r + 1, :] = behind[0, r, layer : layer + 1, :]
+            w[layer, start_b + 2 * DEPTH + r : start_b + 2 * DEPTH + r + 1, :] = behind[1, r, layer : layer + 1, :]
+    add_impulses(
+        sites, found, hits, va,
+        lambda row: jnp.where(is_above(row), row - first_row + DEPTH, row - first_row - rows + DEPTH + 4), columns, strength,
+    )
     chain_a = [va, la.at[0], la.at[1], la.at[2], response]
     chain_b = [vb, lb.at[0], lb.at[1], lb.at[2], response]
     for level in range(4):
@@ -276,7 +292,6 @@
             for r in (4 * index + 2 * pair, 4 * index + 2 * pair + 1):
                 parts = digits_of(field[r] * scale)
                 cells[r] = jnp.concatenate([part.astype(jnp.bfloat16) for part in parts], axis=0)
-                pltpu.make_async_copy(cells.at[r], cells_out.at[r], sems.at[r]).start()
         total = sums[...]
         for pair in range(2):
             r = 4 * index + 2 * pair
@@ -284,6 +299,8 @@
             product = lax.dot_general(two, two, (((1,), (1,)), ((), ())), preferred_element_type=jnp.float32)
             total = total + product.astype(jnp.int32)
         sums[...] = total
+        for r in range(4):
+            pltpu.make_async_copy(cells.at[4 * index + r], cells_out.at[4 * index + r], sems.at[4 * index + r]).start()
         return carry
 
     lax.fori_loop(0, rows // 4, cut, 0)
@@ -335,22 +352,36 @@
     return jnp.transpose(square)[:, :size]
 
 
+PANEL = 4
+
+
 def eliminated(block):
     size, wide = block.shape
-    groups = [block[8 * g : 8 * g + 8] for g in range(size // 8)]
+    count = size // 8
+    groups = [block[8 * g : 8 * g + 8] for g in range(count)]
     like = (8, wide)
     below = lax.broadcasted_iota(jnp.int32, like, 0)
-    for j in range(size):
-        g, s = divmod(j, 8)
-        row = jnp.broadcast_to(groups[g][s : s + 1], like)
-        scaled = row / jnp.broadcast_to(row[:, j : j + 1], like)
-        for other in range(g, size // 8):
-            column = jnp.broadcast_to(groups[other][:, j : j + 1], like)
-            if other == g:
-                if s == 7:
+    for first in range(0, size, PANEL):
+        g, start = divmod(first, 8)
+        columns = {
+            o: [jnp.broadcast_to(groups[o][:, first + t : first + t + 1], like) for t in range(PANEL)]
+            for o in range(g, count)
+        }
+        for t in range(PANEL):
+            s = start + t
+            across = [jnp.broadcast_to(columns[g][u][s : s + 1], like) for u in range(t, PANEL)]
+            inverse = 1.0 / across[0]
+            row = jnp.broadcast_to(groups[g][s : s + 1], like) * inverse
+            across = [value * inverse for value in across]
+            for o in range(g, count):
+                if o == g and s == 7:
                     continue
-                column = jnp.where(below > s, column, 0.0)
-            groups[other] = groups[other] - column * scaled
+                column = columns[o][t]
+                if o == g:
+                    column = jnp.where(below > s, column, 0.0)
+                groups[o] = groups[o] - column * row
+                for u in range(t + 1, PANEL):
+                    columns[o][u] = columns[o][u] - column * across[u - t]
     return normalised(jnp.concatenate(groups, axis=0))
 
 
@@ -484,13 +515,17 @@
         return jnp.concatenate([tall * 256.0**-a for a in range(DIGITS)], axis=1).astype(jnp.bfloat16)
 
     def finish(matrix, cells, first_row, count, shift):
-        def one(r, carry):
-            product = jnp.dot(matrix, cells[r + shift], preferred_element_type=jnp.float32)
-            rows_out[r + first_row] = product[:size] + (product[size : 2 * size] + product[2 * size :])
-            pltpu.make_async_copy(rows_out.at[r + first_row], basis.at[:, r + first_row, :], out_sems.at[r + first_row]).start()
+        def four(index, carry):
+            for j in range(4):
+                r = 4 * index + j
+                product = jnp.dot(matrix, cells[r + shift], preferred_element_type=jnp.float32)
+                rows_out[r + first_row] = product[:size] + (product[size : 2 * size] + product[2 * size :])
+            for j in range(4):
+                at = 4 * index + j + first_row
+                pltpu.make_async_copy(rows_out.at[at], basis.at[:, at, :], out_sems.at[at]).start()
             return carry
 
-        lax.fori_loop(0, count, one, 0, unroll=4)
+        lax.fori_loop(0, count // 4, four, 0)
 
     for copy in loads:
         copy.wait()
@@ -555,8 +590,8 @@
         "pack",
         (shape((5, rows, columns), f32), halo, halo),
         [whole(pl.ANY), whole(), whole(), whole(), whole()],
-        (whole(), whole(), whole()),
-        [pltpu.SemaphoreType.DMA((2, DEPTH))],
+        (whole(), whole(pl.ANY), whole(pl.ANY)),
+        [pltpu.VMEM((2, DEPTH, PACK, columns), f32), pltpu.SemaphoreType.DMA((2, DEPTH + 1))],
     )(probes, kappa, speed, friction, upwind.T)
     from_above = lax.ppermute(to_below, AXIS, [(i, i + 1) for i in range(size - 1)])
     from_below = lax.ppermute(to_above, AXIS, [(i + 1, i) for i in range(size - 1)])
@@ -584,6 +619,7 @@
         (whole(pl.ANY), whole(), whole(), whole(), whole()),
         [field] * 4
         + digit_scratch(inner_count)
+        + [pltpu.SMEM((count + 1,), jnp.int32)]
         + [pltpu.SemaphoreType.DMA((rows,)), pltpu.SemaphoreType.DMA((inner_count,))],
         pl.CostEstimate(flops=10**10, bytes_accessed=16 * MIB, transcendentals=0),
     )(probe_sites, probes, weights)
@@ -593,11 +629,14 @@
         functools.partial(edge_kernel, strength, rows),
         "edge_rows",
         digit_rows(edge_count),
-        [whole(pltpu.SMEM)] + [whole()] * 6,
+        [whole(pltpu.SMEM)] + [whole(pl.ANY)] * 5 + [whole()],
         (whole(pl.ANY), whole(), whole()),
-        [pltpu.VMEM((5, 8 * DEPTH, columns), f32), fields, levels, levels]
+        [
+            pltpu.VMEM((5, 8 * DEPTH, columns), f32), fields, levels, levels,
+            pltpu.VMEM((2, DEPTH, PACK, columns), f32),
+        ]
         + digit_scratch(edge_count)
-        + [pltpu.SemaphoreType.DMA((edge_count,))],
+        + [pltpu.SMEM((count + 1,), jnp.int32), pltpu.SemaphoreType.DMA((10,)), pltpu.SemaphoreType.DMA((edge_count,))],
     )(probe_sites, from_above, from_below, weights, top, bottom, pairs)
     pairs = summed(pairs)
     square = pltpu.VMEM((count, count), f32)

time: 80.4 us -> 101 us (1.26)
  Pallas kernels: 54.9 us -> 75.1 us
    pallas_call x1, Pallas kernels: 3.53 us -> 34.6 us  [on_device(): call(pack_kernel, 'pack', (shape((5, rows, columns), f32), halo, halo), [...]
    pallas_call x1, Pallas kernels: 20.5 us -> 11.7 us  [on_device(): call(functools.partial(solve_kernel, cell_scale), 'solve', (shape((count,...]
    pallas_call x1, Pallas kernels: 21.7 us -> 20.2 us  [on_device(): call(functools.partial(inner_kernel, strength), 'inner_rows', digit_rows(...]
  transfers between devices with their start and end apart: 6 -> 6, of which waited for: 4 -> 4; matrix products, arithmetic and copies ran while one was open for 0% -> 0% of each run, Pallas kernels for 27% -> 20%
where the time goes in v2:
time: 101 us; the launch traced here: 100 us
  Pallas kernels  75.1 us (74%)
  starting transfers between devices  15.2 us (15%)
  waiting for transfers between devices  6.76 us (7%)
  other arithmetic  1.43 us (1%)
    pallas_call x1, Pallas kernels, on_device(): call(pack_kernel, 'pack', (shape((5, rows, columns), f32), halo, halo), [...  34.6 us
    pallas_call x1, Pallas kernels, on_device(): call(functools.partial(inner_kernel, strength), 'inner_rows', digit_rows(...  20.2 us
    pallas_call x1, Pallas kernels, on_device(): call(functools.partial(solve_kernel, cell_scale), 'solve', (shape((count,...  11.7 us
    ppermute x4, starting transfers between devices, summed(): lax.ppermute(pairs, AXIS, [(i, i ^ distance) for i in range(count)])  11.5 us
    pallas_call x1, Pallas kernels, on_device(): call(functools.partial(edge_kernel, strength, rows), 'edge_rows', digit_r...  8.58 us
    ppermute x4, waiting for transfers between devices, summed(): lax.ppermute(pairs, AXIS, [(i, i ^ distance) for i in range(count)])  6.75 us
    ppermute x1, starting transfers between devices, on_device(): lax.ppermute(to_below, AXIS, [(i, i + 1) for i in range(size - 1)])  2.39 us
  transfers between devices with their start and end apart: 6, of which 4 were waited for; matrix products, arithmetic and copies ran while one was open for 0% of the time, Pallas kernels for 20%

profile of v2, /device:TPU:0, one launch (start us, length us, event | category | flops | bytes accessed | tf_op | source)
XLA Modules:
  0.0 100.2 jit_solution(12732280535611051130)
XLA Ops:
  0.6 34.6 %pack.1 = (f32[5,32,512]{2,1,0:T(8,128)}, f32[4,72,512]{2,1,0:T(8,128)}, f32[4,72,512]{2,1,0:T(8,128)}) custom-call(f32[64,32,512]{2,1,0:T(8,128)} %cells.3, f32[32,512]{1,0:T(8,128)} %kappa.1, f32[32,512]{1,0:T(8,128)} %speed.1, f32[32,512]{1,0:T(8,128)} %friction.1, s32[16,32]{1,0:T(8,128)} %bitcast.1), custom_call_target="tpu_custom_call" | custom-call | tf_op jit(solution)/shard_map/pack/pallas_call | solution.py:588
  35.2 2.4 %collective-permute-start = (f32[4,72,512]{2,1,0:T(8,128)}, f32[4,72,512]{2,1,0:T(8,128)S(1)}, u32[]{:S(2)}, u32[]{:S(2)}) collective-permute-start(f32[4,72,512]{2,1,0:T(8,128)} %get-tuple-element.13), channel_id=1, source_target_pairs={{0,1},{1,2},{2,3},{3,4},{4,5},{5,6},{6,7},{7,8},{8,9},{9,10},{10,1... | collective-permute-start | bytes 1769480 | tf_op jit(solution)/shard_map/ppermute | solution.py:596
  37.6 1.3 %collective-permute-start.1 = (f32[4,72,512]{2,1,0:T(8,128)}, f32[4,72,512]{2,1,0:T(8,128)S(1)}, u32[]{:S(2)}, u32[]{:S(2)}) collective-permute-start(f32[4,72,512]{2,1,0:T(8,128)} %get-tuple-element.14), channel_id=1, source_target_pairs={{1,0},{2,1},{3,2},{4,3},{5,4},{6,5},{7,6},{8,7},{9,8},{10,9},{11,1... | collective-permute-start | bytes 1769480 | tf_op jit(solution)/shard_map/ppermute | solution.py:597
  38.9 20.2 %inner_rows.1 = (bf16[24,256,512]{2,1,0:T(8,128)(2,1)}, f32[64,128]{1,0:T(8,128)}, f32[64,128]{1,0:T(8,128)}, f32[4,2,64,512]{3,2,1,0:T(8,128)}, f32[4,2,64,512]{3,2,1,0:T(8,128)}) custom-call(s32[64]{0:T(128)} %sites.3, f32[64,32,512]{2,1,0:T(8,128)} %cells.3, f32[5,32,512]{2,1,0:T(8,128)} %get-tuple-element.15.weights), custom_call_target="tpu_custom_call" | custom-call | flops 10000000000 | bytes 16777216 | tf_op jit(solution)/shard_map/inner_rows/pallas_call | solution.py:614
  59.2 0.0 collective-permute-done.above
  59.2 0.0 copy-start
  59.2 0.0 collective-permute-done.1.below
  59.2 0.0 copy-start.1
  59.2 0.8 copy-done
  60.0 0.2 copy-done.1
  60.2 8.6 %edge_rows.1 = (bf16[8,256,512]{2,1,0:T(8,128)(2,1)}, f32[64,128]{1,0:T(8,128)}, f32[64,128]{1,0:T(8,128)}) custom-call(s32[64]{0:T(128)} %sites.3, f32[4,72,512]{2,1,0:T(8,128)} %copy-done, f32[4,72,512]{2,1,0:T(8,128)} %copy-done.1, f32[5,32,512]{2,1,0:T(8,128)} %get-tuple-element.15.weights, f32[4,2,64,512]{3,2,1,0:T(8,128)} %get-tuple-element.16.top, ...), custom_call_target="tpu_custom_call" | custom-call | tf_op jit(solution)/shard_map/edge_rows/pallas_call | solution.py:628
  68.8 3.3 %collective-permute-start.2 = (f32[64,128]{1,0:T(8,128)}, f32[64,128]{1,0:T(8,128)S(1)}, u32[]{:S(2)}, u32[]{:S(2)}) collective-permute-start(f32[64,128]{1,0:T(8,128)} %get-tuple-element.19), channel_id=1, source_target_pairs={{0,1},{1,0},{2,3},{3,2},{4,5},{5,4},{6,7},{7,6},{8,9},{9,8},{10,11... | collective-permute-start | bytes 98312 | tf_op jit(solution)/shard_map/ppermute | solution.py:575
  72.1 1.1 %collective-permute-done.2 = f32[64,128]{1,0:T(8,128)S(1)} collective-permute-done((f32[64,128]{1,0:T(8,128)}, f32[64,128]{1,0:T(8,128)S(1)}, u32[]{:S(2)}, u32[]{:S(2)}) %collective-permute-start.2) | collective-permute-done | bytes 32800 | tf_op jit(solution)/shard_map/ppermute | solution.py:575
  73.1 0.7 subtract_subtract_fusion.3
  73.9 2.1 %collective-permute-start.3 = (f32[64,128]{1,0:T(8,128)S(1)}, f32[64,128]{1,0:T(8,128)S(1)}, u32[]{:S(2)}, u32[]{:S(2)}) collective-permute-start(f32[64,128]{1,0:T(8,128)S(1)} %pad_maximum_fusion), channel_id=1, source_target_pairs={{0,2},{1,3},{2,0},{3,1},{4,6},{5,7},{6,4},{7,5},{8,10},{9,11},{10,... | collective-permute-start | bytes 98312 | tf_op jit(solution)/shard_map/ppermute | solution.py:575
  76.0 1.9 %collective-permute-done.3 = f32[64,128]{1,0:T(8,128)S(1)} collective-permute-done((f32[64,128]{1,0:T(8,128)S(1)}, f32[64,128]{1,0:T(8,128)S(1)}, u32[]{:S(2)}, u32[]{:S(2)}) %collective-permute-start.3) | collective-permute-done | bytes 32800 | tf_op jit(solution)/shard_map/ppermute | solution.py:575
  78.0 3.0 %collective-permute-start.4 = (f32[64,128]{1,0:T(8,128)S(1)}, f32[64,128]{1,0:T(8,128)S(1)}, u32[]{:S(2)}, u32[]{:S(2)}) collective-permute-start(f32[64,128]{1,0:T(8,128)S(1)} %pad_maximum_fusion.1), channel_id=1, source_target_pairs={{0,4},{1,5},{2,6},{3,7},{4,0},{5,1},{6,2},{7,3},{8,12},{9,13},{10,... | collective-permute-start | bytes 98312 | tf_op jit(solution)/shard_map/ppermute | solution.py:575
  81.0 1.9 %collective-permute-done.4 = f32[64,128]{1,0:T(8,128)S(1)} collective-permute-done((f32[64,128]{1,0:T(8,128)S(1)}, f32[64,128]{1,0:T(8,128)S(1)}, u32[]{:S(2)}, u32[]{:S(2)}) %collective-permute-start.4) | collective-permute-done | bytes 32800 | tf_op jit(solution)/shard_map/ppermute | solution.py:575
  82.9 3.1 %collective-permute-start.5 = (f32[64,128]{1,0:T(8,128)S(1)}, f32[64,128]{1,0:T(8,128)S(1)}, u32[]{:S(2)}, u32[]{:S(2)}) collective-permute-start(f32[64,128]{1,0:T(8,128)S(1)} %pad_maximum_fusion.2), channel_id=1, source_target_pairs={{0,8},{1,9},{2,10},{3,11},{4,12},{5,13},{6,14},{7,15},{8,0},{9,1},... | collective-permute-start | bytes 98312 | tf_op jit(solution)/shard_map/ppermute | solution.py:575
  86.0 1.9 %collective-permute-done.5 = f32[64,128]{1,0:T(8,128)S(1)} collective-permute-done((f32[64,128]{1,0:T(8,128)S(1)}, f32[64,128]{1,0:T(8,128)S(1)}, u32[]{:S(2)}, u32[]{:S(2)}) %collective-permute-start.5) | collective-permute-done | bytes 32800 | tf_op jit(solution)/shard_map/ppermute | solution.py:575
  87.9 0.6 pad_maximum_fusion.3.pairs
  88.5 11.7 %solve.1 = (f32[64,32,512]{2,1,0:T(8,128)}, f32[64,64]{1,0:T(8,128)}) custom-call(f32[64,128]{1,0:T(8,128)} %pad_maximum_fusion.3.pairs, f32[64,128]{1,0:T(8,128)} %get-tuple-element.20.inner_scale, f32[64,128]{1,0:T(8,128)} %get-tuple-element.21.edge_scale, bf16[24,256,512]{2,1,0:T(8,128)(2,1)} %get-tuple-element.22.inner, ...), custom_call_target="tpu_custom_call" | custom-call | tf_op jit(solution)/shard_map/solve/pallas_call | solution.py:643
  (6 shorter events, 0.1 us)
Async XLA Ops:
  35.2 23.9 %collective-permute-start = (f32[4,72,512]{2,1,0:T(8,128)}, f32[4,72,512]{2,1,0:T(8,128)S(1)}, u32[]{:S(2)}, u32[]{:S(2)}) collective-permute-start(f32[4,72,512]{2,1,0:T(8,128)} %get-tuple-element.13), channel_id=1, source_target_pairs={{0,1},{1,2},{2,3},{3,4},{4,5},{5,6},{6,7},{7,8},{8,9},{9,10},{10,1... | collective-permute-start | bytes 1769480 | tf_op jit(solution)/shard_map/ppermute | solution.py:596
  37.6 21.6 %collective-permute-start.1 = (f32[4,72,512]{2,1,0:T(8,128)}, f32[4,72,512]{2,1,0:T(8,128)S(1)}, u32[]{:S(2)}, u32[]{:S(2)}) collective-permute-start(f32[4,72,512]{2,1,0:T(8,128)} %get-tuple-element.14), channel_id=1, source_target_pairs={{1,0},{2,1},{3,2},{4,3},{5,4},{6,5},{7,6},{8,7},{9,8},{10,9},{11,1... | collective-permute-start | bytes 1769480 | tf_op jit(solution)/shard_map/ppermute | solution.py:597
  59.2 0.8 copy-start
  59.2 1.0 %copy-start.1 = (f32[4,72,512]{2,1,0:T(8,128)}, f32[4,72,512]{2,1,0:T(8,128)S(1)}, u32[]{:S(2)}) copy-start(f32[4,72,512]{2,1,0:T(8,128)S(1)} %collective-permute-done.1.below) | copy-start | bytes 1769476
  68.8 4.3 %collective-permute-start.2 = (f32[64,128]{1,0:T(8,128)}, f32[64,128]{1,0:T(8,128)S(1)}, u32[]{:S(2)}, u32[]{:S(2)}) collective-permute-start(f32[64,128]{1,0:T(8,128)} %get-tuple-element.19), channel_id=1, source_target_pairs={{0,1},{1,0},{2,3},{3,2},{4,5},{5,4},{6,7},{7,6},{8,9},{9,8},{10,11... | collective-permute-start | bytes 98312 | tf_op jit(solution)/shard_map/ppermute | solution.py:575
  73.9 4.0 %collective-permute-start.3 = (f32[64,128]{1,0:T(8,128)S(1)}, f32[64,128]{1,0:T(8,128)S(1)}, u32[]{:S(2)}, u32[]{:S(2)}) collective-permute-start(f32[64,128]{1,0:T(8,128)S(1)} %pad_maximum_fusion), channel_id=1, source_target_pairs={{0,2},{1,3},{2,0},{3,1},{4,6},{5,7},{6,4},{7,5},{8,10},{9,11},{10,... | collective-permute-start | bytes 98312 | tf_op jit(solution)/shard_map/ppermute | solution.py:575
  78.0 4.9 %collective-permute-start.4 = (f32[64,128]{1,0:T(8,128)S(1)}, f32[64,128]{1,0:T(8,128)S(1)}, u32[]{:S(2)}, u32[]{:S(2)}) collective-permute-start(f32[64,128]{1,0:T(8,128)S(1)} %pad_maximum_fusion.1), channel_id=1, source_target_pairs={{0,4},{1,5},{2,6},{3,7},{4,0},{5,1},{6,2},{7,3},{8,12},{9,13},{10,... | collective-permute-start | bytes 98312 | tf_op jit(solution)/shard_map/ppermute | solution.py:575
  82.9 5.0 %collective-permute-start.5 = (f32[64,128]{1,0:T(8,128)S(1)}, f32[64,128]{1,0:T(8,128)S(1)}, u32[]{:S(2)}, u32[]{:S(2)}) collective-permute-start(f32[64,128]{1,0:T(8,128)S(1)} %pad_maximum_fusion.2), channel_id=1, source_target_pairs={{0,8},{1,9},{2,10},{3,11},{4,12},{5,13},{6,14},{7,15},{8,0},{9,1},... | collective-permute-start | bytes 98312 | tf_op jit(solution)/shard_map/ppermute | solution.py:575

commit v3 on v2

--- a/solution.py
+++ b/solution.py
@@ -91,7 +91,7 @@
     lax.fori_loop(0, count, one, 0)
 
 
-def pack_kernel(cells, kappa, speed, friction, upwind, weights, to_below, to_above, behind, sems):
+def pack_kernel(cells, kappa, speed, friction, upwind, weights, to_below, to_above, sems):
     probes, rows, columns = cells.shape
     copies = []
     for r in range(DEPTH):
@@ -123,20 +123,17 @@
     for index, layer in enumerate(layers):
         weights[index] = layer
         for r in range(DEPTH):
-            behind[0, r, index : index + 1, :] = layer[r : r + 1]
-            behind[1, r, index : index + 1, :] = layer[rows - DEPTH + r : rows - DEPTH + r + 1]
-    behind[:, :, 5:, :] = jnp.zeros((2, DEPTH, PACK - 5, columns), jnp.float32)
-    for side, target in enumerate((to_above, to_below)):
-        copies.append(
-            pltpu.make_async_copy(behind.at[side], target.at[:, pl.ds(probes, PACK), :], sems.at[side, DEPTH])
-        )
-        copies[-1].start()
+            place = probes + index
+            to_above[r, place : place + 1, :] = layer[r : r + 1]
+            to_below[r, place : place + 1, :] = layer[rows - DEPTH + r : rows - DEPTH + r + 1]
+    for side in (to_above, to_below):
+        side[:, probes + 5 :, :] = jnp.zeros((DEPTH, PACK - 5, columns), jnp.float32)
     for copy in copies:
         copy.wait()
 
 
 def inner_kernel(
-    strength, sites, cells, weights, digits, scale, pairs, top, bottom, v, f1, f2, a1, response, kept, sums, found, sems, out_sems
+    strength, sites, cells, weights, digits, scale, pairs, top, bottom, v, f1, f2, a1, response, sums, found, sems
 ):
     rows, probes, columns = v.shape
     first_row = lax.axis_index(AXIS) * rows
@@ -165,13 +162,13 @@
         for j in range(2):
             top[level, j] = field[level + j]
             bottom[level, j] = field[rows - 2 - level + j]
-    high, low = gram_pair(response, rows - 2 * DEPTH, digits, scale, kept, sums, out_sems)
+    high, low = gram_pair(response, rows - 2 * DEPTH, digits, scale, sums)
     pairs[...] = jnp.concatenate([folded(high), folded(low)], axis=0)
 
 
 def edge_kernel(
     strength, rows, sites, above, below, weights, top, bottom, inner_pairs, digits, scale, pairs,
-    w, va, la, lb, behind, response, kept, sums, found, sems, out_sems,
+    w, va, la, lb, behind, response, sums, found, sems,
 ):
     probes, columns = top.shape[2:]
     first_row = lax.axis_index(AXIS) * rows
@@ -218,7 +215,7 @@
             row_fn(chain_a[level], j + 1, chain_a[level + 1], j, w, start_a + level - 3 + j, probes, columns)
             to = j + (DEPTH if level == 3 else 2)
             row_fn(chain_b[level], j + 1, chain_b[level + 1], to, w, start_b + 7 - level + j, probes, columns)
-    ours = gram_pair(response, 2 * DEPTH, digits, scale, kept, sums, out_sems)
+    ours = gram_pair(response, 2 * DEPTH, digits, scale, sums)
     half = probes // 2
     high, low = pair_sum(ours, (unfolded(inner_pairs[:half, :]), unfolded(inner_pairs[half:, :])))
     pairs[...] = jnp.concatenate([folded(high), folded(low)], axis=0)
@@ -272,7 +269,7 @@
     return pair_of(total, error + (a_low + b_low))
 
 
-def gram_pair(field, rows, cells_out, scale_out, cells, sums, sems):
+def gram_pair(field, rows, cells, scale_out, sums):
     probes, columns = field.shape[1:]
 
     def largest(index, so_far):
@@ -299,8 +296,6 @@
             product = lax.dot_general(two, two, (((1,), (1,)), ((), ())), preferred_element_type=jnp.float32)
             total = total + product.astype(jnp.int32)
         sums[...] = total
-        for r in range(4):
-            pltpu.make_async_copy(cells.at[4 * index + r], cells_out.at[4 * index + r], sems.at[4 * index + r]).start()
         return carry
 
     lax.fori_loop(0, rows // 4, cut, 0)
@@ -322,11 +317,6 @@
     total, rest = pair_of(high, middle)
     total, rest = pair_of(total, rest + low)
     across = as_row(inverse)
-    def wait(r, carry):
-        pltpu.make_async_copy(cells.at[r], cells_out.at[r], sems.at[r]).wait()
-        return carry
-
-    lax.fori_loop(0, rows, wait, 0)
     return total * inverse * across, rest * inverse * across
 
 
@@ -443,17 +433,11 @@
 
 def solve_kernel(
     cell_scale, pairs, inner_scale, edge_scale, inner, edge, basis, factor,
-    inner_cells, edge_cells, rows_out, work, change, change_inverse, in_sems, out_sems,
+    rows_out, work, change, change_inverse, out_sems,
 ):
     size = pairs.shape[0]
     inner_rows, edge_rows = inner.shape[0], edge.shape[0]
     rows = inner_rows + edge_rows
-    loads = [
-        pltpu.make_async_copy(inner, inner_cells, in_sems.at[0]),
-        pltpu.make_async_copy(edge, edge_cells, in_sems.at[1]),
-    ]
-    for copy in loads:
-        copy.start()
     high, low = unfolded(pairs[: size // 2, :]), unfolded(pairs[size // 2 :, :])
     is_diagonal = unit(size)
     diagonal = jnp.sum(jnp.where(is_diagonal, high, 0.0), axis=1, keepdims=True)
@@ -527,12 +511,10 @@
 
         lax.fori_loop(0, count // 4, four, 0)
 
-    for copy in loads:
-        copy.wait()
-    finish(stacked(inner_scale), inner_cells, DEPTH, inner_rows, 0)
+    finish(stacked(inner_scale), inner, DEPTH, inner_rows, 0)
     matrix = stacked(edge_scale)
-    finish(matrix, edge_cells, 0, DEPTH, 0)
-    finish(matrix, edge_cells, rows - DEPTH, DEPTH, DEPTH)
+    finish(matrix, edge, 0, DEPTH, 0)
+    finish(matrix, edge, rows - DEPTH, DEPTH, DEPTH)
 
     def wait(r, carry):
         pltpu.make_async_copy(rows_out.at[r], basis.at[:, r, :], out_sems.at[r]).wait()
@@ -545,14 +527,14 @@
     return pl.BlockSpec(memory_space=memory)
 
 
-def call(kernel, name, out_shape, in_specs, out_specs, scratch_shapes=(), cost=None):
+def call(kernel, name, out_shape, in_specs, out_specs, scratch_shapes=(), cost=None, vmem=56):
     return pl.pallas_call(
         kernel,
         out_shape=out_shape,
         in_specs=in_specs,
         out_specs=out_specs,
         scratch_shapes=scratch_shapes,
-        compiler_params=pltpu.CompilerParams(vmem_limit_bytes=56 * MIB),
+        compiler_params=pltpu.CompilerParams(vmem_limit_bytes=vmem * MIB),
         cost_estimate=cost,
         name=name,
     )
@@ -590,8 +572,9 @@
         "pack",
         (shape((5, rows, columns), f32), halo, halo),
         [whole(pl.ANY), whole(), whole(), whole(), whole()],
-        (whole(), whole(pl.ANY), whole(pl.ANY)),
-        [pltpu.VMEM((2, DEPTH, PACK, columns), f32), pltpu.SemaphoreType.DMA((2, DEPTH + 1))],
+        (whole(), whole(), whole()),
+        [pltpu.SemaphoreType.DMA((2, DEPTH))],
+        vmem=56,
     )(probes, kappa, speed, friction, upwind.T)
     from_above = lax.ppermute(to_below, AXIS, [(i, i + 1) for i in range(size - 1)])
     from_below = lax.ppermute(to_above, AXIS, [(i + 1, i) for i in range(size - 1)])
@@ -605,7 +588,6 @@
     def digit_scratch(number):
         return [
             pltpu.VMEM((number, count, columns), f32),
-            pltpu.VMEM((number, tall, columns), jnp.bfloat16),
             pltpu.VMEM((tall, tall), jnp.int32),
         ]
 
@@ -616,12 +598,13 @@
         "inner_rows",
         digit_rows(inner_count) + (kept, kept),
         [whole(pltpu.SMEM), whole(pl.ANY), whole()],
-        (whole(pl.ANY), whole(), whole(), whole(), whole()),
+        (whole(), whole(), whole(), whole(), whole()),
         [field] * 4
         + digit_scratch(inner_count)
         + [pltpu.SMEM((count + 1,), jnp.int32)]
-        + [pltpu.SemaphoreType.DMA((rows,)), pltpu.SemaphoreType.DMA((inner_count,))],
+        + [pltpu.SemaphoreType.DMA((rows,))],
         pl.CostEstimate(flops=10**10, bytes_accessed=16 * MIB, transcendentals=0),
+        vmem=32,
     )(probe_sites, probes, weights)
     fields = pltpu.VMEM((2 * DEPTH + 4, count, columns), f32)
     levels = pltpu.VMEM((3, DEPTH + 2, count, columns), f32)
@@ -630,13 +613,14 @@
         "edge_rows",
         digit_rows(edge_count),
         [whole(pltpu.SMEM)] + [whole(pl.ANY)] * 5 + [whole()],
-        (whole(pl.ANY), whole(), whole()),
+        (whole(), whole(), whole()),
         [
             pltpu.VMEM((5, 8 * DEPTH, columns), f32), fields, levels, levels,
             pltpu.VMEM((2, DEPTH, PACK, columns), f32),
         ]
         + digit_scratch(edge_count)
-        + [pltpu.SMEM((count + 1,), jnp.int32), pltpu.SemaphoreType.DMA((10,)), pltpu.SemaphoreType.DMA((edge_count,))],
+        + [pltpu.SMEM((count + 1,), jnp.int32), pltpu.SemaphoreType.DMA((10,))],
+        vmem=16,
     )(probe_sites, from_above, from_below, weights, top, bottom, pairs)
     pairs = summed(pairs)
     square = pltpu.VMEM((count, count), f32)
@@ -644,18 +628,16 @@
         functools.partial(solve_kernel, cell_scale),
         "solve",
         (shape((count, rows, columns), f32), shape((count, count), f32)),
-        [whole(), whole(), whole(), whole(pl.ANY), whole(pl.ANY)],
+        [whole()] * 5,
         (whole(pl.ANY), whole()),
         [
-            pltpu.VMEM((inner_count, tall, columns), jnp.bfloat16),
-            pltpu.VMEM((edge_count, tall, columns), jnp.bfloat16),
             pltpu.VMEM((rows, count, columns), f32),
             pltpu.VMEM((count, 2 * count), f32),
             square,
             square,
-            pltpu.SemaphoreType.DMA((2,)),
             pltpu.SemaphoreType.DMA((rows,)),
         ],
+        vmem=24,
     )(pairs, inner_scale, edge_scale, inner, edge)
 
 

time: 101 us -> 63.5 us (0.63)
  Pallas kernels: 75.1 us -> 39.6 us
  other arithmetic: 1.43 us -> 0.07 us
    pallas_call x1, Pallas kernels: 34.6 us -> 3.98 us  [on_device(): call(pack_kernel, 'pack', (shape((5, rows, columns), f32), halo, halo), [...]
    pallas_call x1, Pallas kernels: 8.58 us -> 6.55 us  [on_device(): call(functools.partial(edge_kernel, strength, rows), 'edge_rows', digit_r...]
    pallas_call x1, Pallas kernels: 20.2 us -> 18.6 us  [on_device(): call(functools.partial(inner_kernel, strength), 'inner_rows', digit_rows(...]
    pallas_call x1, Pallas kernels: 11.7 us -> 10.5 us  [on_device(): call(functools.partial(solve_kernel, cell_scale), 'solve', (shape((count,...]
  transfers between devices with their start and end apart: 6 -> 6, of which waited for: 4 -> 4; matrix products, arithmetic and copies ran while one was open for 0% -> 0% of each run, Pallas kernels for 20% -> 29%
where the time goes in v3:
time: 63.5 us; the launch traced here: 63.4 us
  Pallas kernels  39.6 us (62%)
  starting transfers between devices  15.2 us (24%)
  waiting for transfers between devices  6.55 us (10%)
  local copies, waits for them, and re-layouts  0.97 us (2%)
  between operations  0.94 us (1%)
    pallas_call x1, Pallas kernels, on_device(): call(functools.partial(inner_kernel, strength), 'inner_rows', digit_rows(...  18.6 us
    ppermute x4, starting transfers between devices, summed(): lax.ppermute(pairs, AXIS, [(i, i ^ distance) for i in range(count)])  11.6 us
    pallas_call x1, Pallas kernels, on_device(): call(functools.partial(solve_kernel, cell_scale), 'solve', (shape((count,...  10.5 us
    pallas_call x1, Pallas kernels, on_device(): call(functools.partial(edge_kernel, strength, rows), 'edge_rows', digit_r...  6.55 us
    ppermute x4, waiting for transfers between devices, summed(): lax.ppermute(pairs, AXIS, [(i, i ^ distance) for i in range(count)])  6.55 us
    pallas_call x1, Pallas kernels, on_device(): call(pack_kernel, 'pack', (shape((5, rows, columns), f32), halo, halo), [...  3.98 us
    ppermute x1, starting transfers between devices, on_device(): lax.ppermute(to_below, AXIS, [(i, i + 1) for i in range(size - 1)])  2.39 us
    ppermute x1, starting transfers between devices, on_device(): lax.ppermute(to_above, AXIS, [(i + 1, i) for i in range(size - 1)])  1.29 us
  transfers between devices with their start and end apart: 6, of which 4 were waited for; matrix products, arithmetic and copies ran while one was open for 0% of the time, Pallas kernels for 29%

profile of v3, /device:TPU:0, one launch (start us, length us, event | category | flops | bytes accessed | tf_op | source)
XLA Modules:
  0.0 63.4 jit_solution(3900688541292130648)
XLA Ops:
  0.6 0.0 copy-start
  0.6 0.0 copy-start.2
  0.7 4.0 %pack.1 = (f32[5,32,512]{2,1,0:T(8,128)}, f32[4,72,512]{2,1,0:T(8,128)}, f32[4,72,512]{2,1,0:T(8,128)}) custom-call(f32[64,32,512]{2,1,0:T(8,128)} %cells.3, f32[32,512]{1,0:T(8,128)} %kappa.1, f32[32,512]{1,0:T(8,128)} %speed.1, f32[32,512]{1,0:T(8,128)} %friction.1, s32[16,32]{1,0:T(8,128)} %bitcast.1), custom_call_target="tpu_custom_call" | custom-call | tf_op jit(solution)/shard_map/pack/pallas_call | solution.py:570
  4.6 2.4 %collective-permute-start = (f32[4,72,512]{2,1,0:T(8,128)}, f32[4,72,512]{2,1,0:T(8,128)S(1)}, u32[]{:S(2)}, u32[]{:S(2)}) collective-permute-start(f32[4,72,512]{2,1,0:T(8,128)} %get-tuple-element.13), channel_id=1, source_target_pairs={{0,1},{1,2},{2,3},{3,4},{4,5},{5,6},{6,7},{7,8},{8,9},{9,10},{10,1... | collective-permute-start | bytes 1769480 | tf_op jit(solution)/shard_map/ppermute | solution.py:579
  7.0 1.3 %collective-permute-start.1 = (f32[4,72,512]{2,1,0:T(8,128)}, f32[4,72,512]{2,1,0:T(8,128)S(1)}, u32[]{:S(2)}, u32[]{:S(2)}) collective-permute-start(f32[4,72,512]{2,1,0:T(8,128)} %get-tuple-element.14), channel_id=1, source_target_pairs={{1,0},{2,1},{3,2},{4,3},{5,4},{6,5},{7,6},{8,7},{9,8},{10,9},{11,1... | collective-permute-start | bytes 1769480 | tf_op jit(solution)/shard_map/ppermute | solution.py:580
  8.3 0.0 copy-done
  8.3 0.0 copy-done.2
  8.4 0.0 copy-start.1
  8.4 1.0 %copy-done.1 = f32[5,32,512]{2,1,0:T(8,128)S(1)} copy-done((f32[5,32,512]{2,1,0:T(8,128)S(1)}, f32[5,32,512]{2,1,0:T(8,128)}, u32[]{:S(2)}) %copy-start.1) | copy-done | bytes 327704
  9.3 18.6 %inner_rows.1 = (bf16[24,256,512]{2,1,0:T(8,128)(2,1)S(1)}, f32[64,128]{1,0:T(8,128)S(1)}, f32[64,128]{1,0:T(8,128)S(1)}, f32[4,2,64,512]{3,2,1,0:T(8,128)S(1)}, f32[4,2,64,512]{3,2,1,0:T(8,128)S(1)}) custom-call(s32[64]{0:T(128)S(1)} %copy-done.2, f32[64,32,512]{2,1,0:T(8,128)S(1)} %copy-done, f32[5,32,512]{2,1,0:T(8,128)S(1)} %copy-done.1), custom_call_target="tpu_custom_call" | custom-call | flops 10000000000 | bytes 16777216 | tf_op jit(solution)/shard_map/inner_rows/pallas_call | solution.py:596
  28.0 0.0 collective-permute-done.above
  28.0 0.0 collective-permute-done.1.below
  28.0 6.6 %edge_rows.1 = (bf16[8,256,512]{2,1,0:T(8,128)(2,1)S(1)}, f32[64,128]{1,0:T(8,128)S(1)}, f32[64,128]{1,0:T(8,128)S(1)}) custom-call(s32[64]{0:T(128)S(1)} %copy-done.2, f32[4,72,512]{2,1,0:T(8,128)S(1)} %collective-permute-done.above, f32[4,72,512]{2,1,0:T(8,128)S(1)} %collective-permute-done.1.below, f32[5,32,512]{2,1,0:T(8,128)S(1)} %copy-done.1, ...), custom_call_target="tpu_custom_call" | custom-call | tf_op jit(solution)/shard_map/edge_rows/pallas_call | solution.py:611
  34.5 3.3 %collective-permute-start.2 = (f32[64,128]{1,0:T(8,128)S(1)}, f32[64,128]{1,0:T(8,128)S(1)}, u32[]{:S(2)}, u32[]{:S(2)}) collective-permute-start(f32[64,128]{1,0:T(8,128)S(1)} %get-tuple-element.19), channel_id=1, source_target_pairs={{0,1},{1,0},{2,3},{3,2},{4,5},{5,4},{6,7},{7,6},{8,9},{9,8},{10,11... | collective-permute-start | bytes 98312 | tf_op jit(solution)/shard_map/ppermute | solution.py:557
  37.8 0.9 %collective-permute-done.2 = f32[64,128]{1,0:T(8,128)S(1)} collective-permute-done((f32[64,128]{1,0:T(8,128)S(1)}, f32[64,128]{1,0:T(8,128)S(1)}, u32[]{:S(2)}, u32[]{:S(2)}) %collective-permute-start.2) | collective-permute-done | bytes 32800 | tf_op jit(solution)/shard_map/ppermute | solution.py:557
  38.7 2.1 %collective-permute-start.3 = (f32[64,128]{1,0:T(8,128)S(1)}, f32[64,128]{1,0:T(8,128)S(1)}, u32[]{:S(2)}, u32[]{:S(2)}) collective-permute-start(f32[64,128]{1,0:T(8,128)S(1)} %pad_maximum_fusion), channel_id=1, source_target_pairs={{0,2},{1,3},{2,0},{3,1},{4,6},{5,7},{6,4},{7,5},{8,10},{9,11},{10,... | collective-permute-start | bytes 98312 | tf_op jit(solution)/shard_map/ppermute | solution.py:557
  40.8 1.9 %collective-permute-done.3 = f32[64,128]{1,0:T(8,128)S(1)} collective-permute-done((f32[64,128]{1,0:T(8,128)S(1)}, f32[64,128]{1,0:T(8,128)S(1)}, u32[]{:S(2)}, u32[]{:S(2)}) %collective-permute-start.3) | collective-permute-done | bytes 32800 | tf_op jit(solution)/shard_map/ppermute | solution.py:557
  42.7 2.9 %collective-permute-start.4 = (f32[64,128]{1,0:T(8,128)S(1)}, f32[64,128]{1,0:T(8,128)S(1)}, u32[]{:S(2)}, u32[]{:S(2)}) collective-permute-start(f32[64,128]{1,0:T(8,128)S(1)} %pad_maximum_fusion.1), channel_id=1, source_target_pairs={{0,4},{1,5},{2,6},{3,7},{4,0},{5,1},{6,2},{7,3},{8,12},{9,13},{10,... | collective-permute-start | bytes 98312 | tf_op jit(solution)/shard_map/ppermute | solution.py:557
  45.7 1.9 %collective-permute-done.4 = f32[64,128]{1,0:T(8,128)S(1)} collective-permute-done((f32[64,128]{1,0:T(8,128)S(1)}, f32[64,128]{1,0:T(8,128)S(1)}, u32[]{:S(2)}, u32[]{:S(2)}) %collective-permute-start.4) | collective-permute-done | bytes 32800 | tf_op jit(solution)/shard_map/ppermute | solution.py:557
  47.6 3.3 %collective-permute-start.5 = (f32[64,128]{1,0:T(8,128)S(1)}, f32[64,128]{1,0:T(8,128)S(1)}, u32[]{:S(2)}, u32[]{:S(2)}) collective-permute-start(f32[64,128]{1,0:T(8,128)S(1)} %pad_maximum_fusion.2), channel_id=1, source_target_pairs={{0,8},{1,9},{2,10},{3,11},{4,12},{5,13},{6,14},{7,15},{8,0},{9,1},... | collective-permute-start | bytes 98312 | tf_op jit(solution)/shard_map/ppermute | solution.py:557
  50.9 1.9 %collective-permute-done.5 = f32[64,128]{1,0:T(8,128)S(1)} collective-permute-done((f32[64,128]{1,0:T(8,128)S(1)}, f32[64,128]{1,0:T(8,128)S(1)}, u32[]{:S(2)}, u32[]{:S(2)}) %collective-permute-start.5) | collective-permute-done | bytes 32800 | tf_op jit(solution)/shard_map/ppermute | solution.py:557
  52.8 10.5 %solve.1 = (f32[64,32,512]{2,1,0:T(8,128)}, f32[64,64]{1,0:T(8,128)}) custom-call(f32[64,128]{1,0:T(8,128)S(1)} %pad_maximum_fusion.3.pairs, f32[64,128]{1,0:T(8,128)S(1)} %get-tuple-element.20.inner_scale, f32[64,128]{1,0:T(8,128)S(1)} %get-tuple-element.21.edge_scale, bf16[24,256,512]{2,1,0:T(8,128)(2,1)S(1)} %get-tuple-element.22.inner, ...), custom_call_target="tpu_custom_call" | custom-call | tf_op jit(solution)/shard_map/solve/pallas_call | solution.py:627
  (8 shorter events, 0.1 us)
Async XLA Ops:
  0.6 7.7 %copy-start = (f32[64,32,512]{2,1,0:T(8,128)S(1)}, f32[64,32,512]{2,1,0:T(8,128)}, u32[]{:S(2)}) copy-start(f32[64,32,512]{2,1,0:T(8,128)} %cells.3) | copy-start | bytes 12582916
  0.6 7.7 %copy-start.2 = (s32[64]{0:T(128)S(1)}, s32[64]{0:T(128)}, u32[]{:S(2)}) copy-start(s32[64]{0:T(128)} %sites.3) | copy-start | bytes 772
  4.6 23.3 %collective-permute-start = (f32[4,72,512]{2,1,0:T(8,128)}, f32[4,72,512]{2,1,0:T(8,128)S(1)}, u32[]{:S(2)}, u32[]{:S(2)}) collective-permute-start(f32[4,72,512]{2,1,0:T(8,128)} %get-tuple-element.13), channel_id=1, source_target_pairs={{0,1},{1,2},{2,3},{3,4},{4,5},{5,6},{6,7},{7,8},{8,9},{9,10},{10,1... | collective-permute-start | bytes 1769480 | tf_op jit(solution)/shard_map/ppermute | solution.py:579
  7.0 20.9 %collective-permute-start.1 = (f32[4,72,512]{2,1,0:T(8,128)}, f32[4,72,512]{2,1,0:T(8,128)S(1)}, u32[]{:S(2)}, u32[]{:S(2)}) collective-permute-start(f32[4,72,512]{2,1,0:T(8,128)} %get-tuple-element.14), channel_id=1, source_target_pairs={{1,0},{2,1},{3,2},{4,3},{5,4},{6,5},{7,6},{8,7},{9,8},{10,9},{11,1... | collective-permute-start | bytes 1769480 | tf_op jit(solution)/shard_map/ppermute | solution.py:580
  8.4 1.0 %copy-start.1 = (f32[5,32,512]{2,1,0:T(8,128)S(1)}, f32[5,32,512]{2,1,0:T(8,128)}, u32[]{:S(2)}) copy-start(f32[5,32,512]{2,1,0:T(8,128)} %get-tuple-element.15.weights) | copy-start | bytes 983044
  34.5 4.1 %collective-permute-start.2 = (f32[64,128]{1,0:T(8,128)S(1)}, f32[64,128]{1,0:T(8,128)S(1)}, u32[]{:S(2)}, u32[]{:S(2)}) collective-permute-start(f32[64,128]{1,0:T(8,128)S(1)} %get-tuple-element.19), channel_id=1, source_target_pairs={{0,1},{1,0},{2,3},{3,2},{4,5},{5,4},{6,7},{7,6},{8,9},{9,8},{10,11... | collective-permute-start | bytes 98312 | tf_op jit(solution)/shard_map/ppermute | solution.py:557
  38.7 4.0 %collective-permute-start.3 = (f32[64,128]{1,0:T(8,128)S(1)}, f32[64,128]{1,0:T(8,128)S(1)}, u32[]{:S(2)}, u32[]{:S(2)}) collective-permute-start(f32[64,128]{1,0:T(8,128)S(1)} %pad_maximum_fusion), channel_id=1, source_target_pairs={{0,2},{1,3},{2,0},{3,1},{4,6},{5,7},{6,4},{7,5},{8,10},{9,11},{10,... | collective-permute-start | bytes 98312 | tf_op jit(solution)/shard_map/ppermute | solution.py:557
  42.7 4.8 %collective-permute-start.4 = (f32[64,128]{1,0:T(8,128)S(1)}, f32[64,128]{1,0:T(8,128)S(1)}, u32[]{:S(2)}, u32[]{:S(2)}) collective-permute-start(f32[64,128]{1,0:T(8,128)S(1)} %pad_maximum_fusion.1), channel_id=1, source_target_pairs={{0,4},{1,5},{2,6},{3,7},{4,0},{5,1},{6,2},{7,3},{8,12},{9,13},{10,... | collective-permute-start | bytes 98312 | tf_op jit(solution)/shard_map/ppermute | solution.py:557
  47.6 5.1 %collective-permute-start.5 = (f32[64,128]{1,0:T(8,128)S(1)}, f32[64,128]{1,0:T(8,128)S(1)}, u32[]{:S(2)}, u32[]{:S(2)}) collective-permute-start(f32[64,128]{1,0:T(8,128)S(1)} %pad_maximum_fusion.2), channel_id=1, source_target_pairs={{0,8},{1,9},{2,10},{3,11},{4,12},{5,13},{6,14},{7,15},{8,0},{9,1},... | collective-permute-start | bytes 98312 | tf_op jit(solution)/shard_map/ppermute | solution.py:557

commit v4 on v3

--- a/solution.py
+++ b/solution.py
@@ -24,7 +24,7 @@
     return jnp.broadcast_to(weights[layer, pl.ds(row, 1), :], like)
 
 
-def in_steps(first, last, body, step=6):
+def in_steps(first, last, body, step=10):
     whole_steps = (last - first) // step
 
     def several(index, carry):
@@ -70,12 +70,23 @@
     )
 
 
-def find_impulses(sites, found, held, probes, columns):
-    def one(k, count):
-        found[count] = k
-        return count + held(lax.div(sites[k], columns)).astype(jnp.int32)
-
-    return lax.fori_loop(0, probes, one, 0)
+def find_impulses(sites, found, held, probes):
+    unroll = 8
+
+    def several(index, count):
+        for j in range(unroll):
+            k = index * unroll + j
+            found[count] = k
+            count = jnp.where(held(sites[k]), count + 1, count)
+        return count
+
+    return lax.fori_loop(0, probes // unroll, several, 0)
+
+
+def row_and_column(site, columns):
+    if columns & (columns - 1):
+        return lax.div(site, columns), lax.rem(site, columns)
+    return site >> (columns.bit_length() - 1), site & (columns - 1)
 
 
 def add_impulses(sites, found, count, target, place_of, columns, strength):
@@ -83,15 +94,36 @@
 
     def one(index, carry):
         k = found[index]
-        site = sites[k]
-        hit = jnp.where(column_ids == lax.rem(site, columns), strength, 0.0)
-        target[place_of(lax.div(site, columns)), pl.ds(k, 1), :] += hit
+        row, column = row_and_column(sites[k], columns)
+        target[place_of(row), pl.ds(k, 1), :] += jnp.where(column_ids == column, strength, 0.0)
         return carry
 
     lax.fori_loop(0, count, one, 0)
 
 
-def pack_kernel(cells, kappa, speed, friction, upwind, weights, to_below, to_above, sems):
+def weight_layers(kappa, speed, friction, upwind):
+    rows, columns = kappa.shape
+    blocks = upwind.shape[0]
+    width = columns // blocks
+    spread = (
+        lax.broadcasted_iota(jnp.int32, (blocks, columns), 1) // width
+        == lax.broadcasted_iota(jnp.int32, (blocks, columns), 0)
+    ).astype(jnp.bfloat16)
+    directions = lax.dot_general(
+        upwind.astype(jnp.float32).astype(jnp.bfloat16), spread, (((0,), (0,)), ((), ())),
+        preferred_element_type=jnp.float32,
+    )
+    column_ids = lax.broadcasted_iota(jnp.int32, (rows, columns), 1)
+    layers = [1.0 - TIME_STEP * (4.0 * kappa + speed + friction)]
+    for direction in range(4):
+        chosen = jnp.where(jnp.abs(directions - direction) < 0.5, speed, 0.0)
+        layers.append(TIME_STEP * (kappa + chosen))
+    layers[3] = jnp.where(column_ids == 0, 0.0, layers[3])
+    layers[4] = jnp.where(column_ids == columns - 1, 0.0, layers[4])
+    return layers
+
+
+def pack_kernel(cells, kappa, speed, friction, upwind, to_below, to_above, cell_rows, directions, sems, cell_sems):
     probes, rows, columns = cells.shape
     copies = []
     for r in range(DEPTH):
@@ -100,32 +132,24 @@
             copies.append(
                 pltpu.make_async_copy(cells.at[:, row, :], target.at[r, pl.ds(0, probes), :], sems.at[side, r])
             )
-    for copy in copies:
+    small = [pltpu.make_async_copy(upwind, directions, cell_sems.at[3, 0])]
+    for index, source in enumerate((kappa, speed, friction)):
+        for side, row in enumerate((0, rows - 8)):
+            small.append(
+                pltpu.make_async_copy(
+                    source.at[pl.ds(row, 8)], cell_rows.at[index, pl.ds(8 * side, 8)], cell_sems.at[index, side]
+                )
+            )
+    for copy in copies + small:
         copy.start()
-    blocks = upwind.shape[0]
-    width = columns // blocks
-    spread = (
-        lax.broadcasted_iota(jnp.int32, (blocks, columns), 1) // width
-        == lax.broadcasted_iota(jnp.int32, (blocks, columns), 0)
-    ).astype(jnp.bfloat16)
-    directions = lax.dot_general(
-        upwind[...].astype(jnp.float32).astype(jnp.bfloat16), spread, (((0,), (0,)), ((), ())),
-        preferred_element_type=jnp.float32,
-    )
-    column_ids = lax.broadcasted_iota(jnp.int32, (rows, columns), 1)
-    k, s = kappa[...], speed[...]
-    layers = [1.0 - TIME_STEP * (4.0 * k + s + friction[...])]
-    for direction in range(4):
-        chosen = jnp.where(jnp.abs(directions - direction) < 0.5, s, 0.0)
-        layers.append(TIME_STEP * (k + chosen))
-    layers[3] = jnp.where(column_ids == 0, 0.0, layers[3])
-    layers[4] = jnp.where(column_ids == columns - 1, 0.0, layers[4])
-    for index, layer in enumerate(layers):
-        weights[index] = layer
+    for copy in small:
+        copy.wait()
+    ends = jnp.concatenate([directions[:, :8], directions[:, rows - 8 :]], axis=1)
+    for index, layer in enumerate(weight_layers(cell_rows[0], cell_rows[1], cell_rows[2], ends)):
+        place = probes + index
         for r in range(DEPTH):
-            place = probes + index
             to_above[r, place : place + 1, :] = layer[r : r + 1]
-            to_below[r, place : place + 1, :] = layer[rows - DEPTH + r : rows - DEPTH + r + 1]
+            to_below[r, place : place + 1, :] = layer[16 - DEPTH + r : 16 - DEPTH + r + 1]
     for side in (to_above, to_below):
         side[:, probes + 5 :, :] = jnp.zeros((DEPTH, PACK - 5, columns), jnp.float32)
     for copy in copies:
@@ -133,7 +157,7 @@
 
 
 def inner_kernel(
-    strength, sites, cells, weights, digits, scale, pairs, top, bottom, v, f1, f2, a1, response, sums, found, sems
+    strength, sites, cells, kappa, speed, friction, upwind, digits, scale, pairs, top, bottom, weights, v, f1, f2, a1, response, sums, found, sems
 ):
     rows, probes, columns = v.shape
     first_row = lax.axis_index(AXIS) * rows
@@ -141,9 +165,10 @@
     copies = [pltpu.make_async_copy(cells.at[:, r, :], v.at[r], sems.at[r]) for r in range(rows)]
     for copy in copies:
         copy.start()
-    hits = find_impulses(
-        sites, found, lambda row: (row >= first_row) & (row < first_row + rows), probes, columns
-    )
+    for index, layer in enumerate(weight_layers(kappa[...], speed[...], friction[...], upwind[...])):
+        weights[index] = layer
+    first_cell, end_cell = first_row * columns, (first_row + rows) * columns
+    hits = find_impulses(sites, found, lambda site: (site >= first_cell) & (site < end_cell), probes)
     for copy in copies:
         copy.wait()
     add_impulses(sites, found, hits, v, lambda row: row - first_row, columns, strength)
@@ -190,13 +215,15 @@
     for copy in copies:
         copy.start()
 
-    def is_above(row):
-        return (row >= first_row - DEPTH) & (row < first_row)
-
-    def held(row):
-        return is_above(row) | ((row >= first_row + rows) & (row < first_row + rows + DEPTH))
-
-    hits = find_impulses(sites, found, held, probes, columns)
+    cells = rows * columns
+    first_cell = first_row * columns
+
+    def held(site):
+        near = site - first_cell
+        is_above = (near >= -DEPTH * columns) & (near < 0)
+        return is_above | ((near >= cells) & (near < cells + DEPTH * columns))
+
+    hits = find_impulses(sites, found, held, probes)
     for copy in copies:
         copy.wait()
     for layer in range(5):
@@ -205,7 +232,7 @@
             w[layer, start_b + 2 * DEPTH + r : start_b + 2 * DEPTH + r + 1, :] = behind[1, r, layer : layer + 1, :]
     add_impulses(
         sites, found, hits, va,
-        lambda row: jnp.where(is_above(row), row - first_row + DEPTH, row - first_row - rows + DEPTH + 4), columns, strength,
+        lambda row: jnp.where(row < first_row, row - first_row + DEPTH, row - first_row - rows + DEPTH + 4), columns, strength,
     )
     chain_a = [va, la.at[0], la.at[1], la.at[2], response]
     chain_b = [vb, lb.at[0], lb.at[1], lb.at[2], response]
@@ -567,13 +594,18 @@
     strength = IMPULSE_GAIN * cell_scale
     shape = jax.ShapeDtypeStruct
     halo = shape((DEPTH, count + PACK, columns), f32)
-    weights, to_below, to_above = call(
+    to_below, to_above = call(
         pack_kernel,
         "pack",
-        (shape((5, rows, columns), f32), halo, halo),
-        [whole(pl.ANY), whole(), whole(), whole(), whole()],
-        (whole(), whole(), whole()),
-        [pltpu.SemaphoreType.DMA((2, DEPTH))],
+        (halo, halo),
+        [whole(pl.ANY)] * 5,
+        (whole(), whole()),
+        [
+            pltpu.VMEM((3, 16, columns), f32),
+            pltpu.VMEM(upwind.shape[::-1], jnp.int32),
+            pltpu.SemaphoreType.DMA((2, DEPTH)),
+            pltpu.SemaphoreType.DMA((4, 2)),
+        ],
         vmem=56,
     )(probes, kappa, speed, friction, upwind.T)
     from_above = lax.ppermute(to_below, AXIS, [(i, i + 1) for i in range(size - 1)])
@@ -593,19 +625,19 @@
 
     kept = shape((4, 2, count, columns), f32)
     field = pltpu.VMEM((rows, count, columns), f32)
-    inner, inner_scale, pairs, top, bottom = call(
+    inner, inner_scale, pairs, top, bottom, weights = call(
         functools.partial(inner_kernel, strength),
         "inner_rows",
-        digit_rows(inner_count) + (kept, kept),
-        [whole(pltpu.SMEM), whole(pl.ANY), whole()],
-        (whole(), whole(), whole(), whole(), whole()),
+        digit_rows(inner_count) + (kept, kept, shape((5, rows, columns), f32)),
+        [whole(pltpu.SMEM), whole(pl.ANY)] + [whole()] * 4,
+        (whole(),) * 6,
         [field] * 4
         + digit_scratch(inner_count)
         + [pltpu.SMEM((count + 1,), jnp.int32)]
         + [pltpu.SemaphoreType.DMA((rows,))],
         pl.CostEstimate(flops=10**10, bytes_accessed=16 * MIB, transcendentals=0),
         vmem=32,
-    )(probe_sites, probes, weights)
+    )(probe_sites, probes, kappa, speed, friction, upwind.T)
     fields = pltpu.VMEM((2 * DEPTH + 4, count, columns), f32)
     levels = pltpu.VMEM((3, DEPTH + 2, count, columns), f32)
     edge, edge_scale, pairs = call(

time: 63.5 us -> 60.2 us (0.948)
  Pallas kernels: 39.6 us -> 37.3 us
  local copies, waits for them, and re-layouts: 0.97 us -> 0.03 us
    pallas_call x1, Pallas kernels: 3.98 us -> 2.9 us  [on_device(): call(pack_kernel, 'pack', (halo, halo), [whole(pl.ANY)] * 5, (whole(), wh...]
    unnamed x6 -> x12, local copies, waits for them, and re-layouts: 0.97 us -> 0.03 us
    pallas_call x1, Pallas kernels: 18.6 us -> 17.9 us  [on_device(): call(functools.partial(inner_kernel, strength), 'inner_rows', digit_rows(...]
  transfers between devices with their start and end apart: 6 -> 6, of which waited for: 4 -> 4; matrix products, arithmetic and copies ran while one was open for 0% -> 0% of each run, Pallas kernels for 29% -> 30%
where the time goes in v4:
time: 60.2 us; the launch traced here: 59.9 us
  Pallas kernels  37.3 us (62%)
  starting transfers between devices  15 us (25%)
  waiting for transfers between devices  6.61 us (11%)
  between operations  0.99 us (2%)
    pallas_call x1, Pallas kernels, on_device(): call(functools.partial(inner_kernel, strength), 'inner_rows', digit_rows(...  17.9 us
    ppermute x4, starting transfers between devices, summed(): lax.ppermute(pairs, AXIS, [(i, i ^ distance) for i in range(count)])  11.3 us
    pallas_call x1, Pallas kernels, on_device(): call(functools.partial(solve_kernel, cell_scale), 'solve', (shape((count,...  10.5 us
    ppermute x4, waiting for transfers between devices, summed(): lax.ppermute(pairs, AXIS, [(i, i ^ distance) for i in range(count)])  6.61 us
    pallas_call x1, Pallas kernels, on_device(): call(functools.partial(edge_kernel, strength, rows), 'edge_rows', digit_r...  6.06 us
    pallas_call x1, Pallas kernels, on_device(): call(pack_kernel, 'pack', (halo, halo), [whole(pl.ANY)] * 5, (whole(), wh...  2.9 us
    ppermute x1, starting transfers between devices, on_device(): lax.ppermute(to_below, AXIS, [(i, i + 1) for i in range(size - 1)])  2.39 us
    ppermute x1, starting transfers between devices, on_device(): lax.ppermute(to_above, AXIS, [(i + 1, i) for i in range(size - 1)])  1.29 us
  transfers between devices with their start and end apart: 6, of which 4 were waited for; matrix products, arithmetic and copies ran while one was open for 0% of the time, Pallas kernels for 30%

profile of v4, /device:TPU:0, one launch (start us, length us, event | category | flops | bytes accessed | tf_op | source)
XLA Modules:
  0.0 59.9 jit_solution(6838686522903201198)
XLA Ops:
  0.6 0.0 copy-start.3
  0.6 0.0 copy-start.2
  0.7 0.0 copy-start.1
  0.7 0.0 copy-start
  0.7 0.0 copy-start.4
  0.7 0.0 copy-start.5
  0.7 2.9 %pack.1 = (f32[4,72,512]{2,1,0:T(8,128)}, f32[4,72,512]{2,1,0:T(8,128)}) custom-call(f32[64,32,512]{2,1,0:T(8,128)} %cells.3, f32[32,512]{1,0:T(8,128)} %kappa.3, f32[32,512]{1,0:T(8,128)} %speed.3, f32[32,512]{1,0:T(8,128)} %friction.3, s32[16,32]{1,0:T(8,128)} %bitcast.1), custom_call_target="tpu_custom_call" | custom-call | tf_op jit(solution)/shard_map/pack/pallas_call | solution.py:597
  3.6 2.4 %collective-permute-start = (f32[4,72,512]{2,1,0:T(8,128)}, f32[4,72,512]{2,1,0:T(8,128)S(1)}, u32[]{:S(2)}, u32[]{:S(2)}) collective-permute-start(f32[4,72,512]{2,1,0:T(8,128)} %get-tuple-element.13), channel_id=1, source_target_pairs={{0,1},{1,2},{2,3},{3,4},{4,5},{5,6},{6,7},{7,8},{8,9},{9,10},{10,1... | collective-permute-start | bytes 1769480 | tf_op jit(solution)/shard_map/ppermute | solution.py:611
  6.0 1.3 %collective-permute-start.1 = (f32[4,72,512]{2,1,0:T(8,128)}, f32[4,72,512]{2,1,0:T(8,128)S(1)}, u32[]{:S(2)}, u32[]{:S(2)}) collective-permute-start(f32[4,72,512]{2,1,0:T(8,128)} %get-tuple-element.14), channel_id=1, source_target_pairs={{1,0},{2,1},{3,2},{4,3},{5,4},{6,5},{7,6},{8,7},{9,8},{10,9},{11,1... | collective-permute-start | bytes 1769480 | tf_op jit(solution)/shard_map/ppermute | solution.py:612
  7.3 0.0 copy-done.3
  7.3 0.0 copy-done.2
  7.3 0.0 copy-done.1
  7.3 0.0 copy-done
  7.3 0.0 copy-done.4
  7.3 0.0 copy-done.5
  7.4 17.9 %inner_rows.1 = (bf16[24,256,512]{2,1,0:T(8,128)(2,1)S(1)}, f32[64,128]{1,0:T(8,128)S(1)}, f32[64,128]{1,0:T(8,128)S(1)}, f32[4,2,64,512]{3,2,1,0:T(8,128)S(1)},...) custom-call(s32[64]{0:T(128)S(1)} %copy-done.5, f32[64,32,512]{2,1,0:T(8,128)S(1)} %copy-done, ...), custom_call_target="tpu_custom_call" | custom-call | flops 10000000000 | bytes 16777216 | tf_op jit(solution)/shard_map/inner_rows/pallas_call | solution.py:628
  25.2 0.0 collective-permute-done.above
  25.2 0.0 collective-permute-done.1.below
  25.2 6.1 %edge_rows.1 = (bf16[8,256,512]{2,1,0:T(8,128)(2,1)S(1)}, f32[64,128]{1,0:T(8,128)S(1)}, f32[64,128]{1,0:T(8,128)S(1)}) custom-call(s32[64]{0:T(128)S(1)} %copy-done.5, f32[4,72,512]{2,1,0:T(8,128)S(1)} %collective-permute-done.above, f32[4,72,512]{2,1,0:T(8,128)S(1)} %collective-permute-done.1.below, f32[5,32,512]{2,1,0:T(8,128)S(1)} %get-tuple-element.15.weights, ...), custom_call_target="tpu_custom_call" | custom-call | tf_op jit(solution)/shard_map/edge_rows/pallas_call | solution.py:643
  31.3 3.2 %collective-permute-start.2 = (f32[64,128]{1,0:T(8,128)S(1)}, f32[64,128]{1,0:T(8,128)S(1)}, u32[]{:S(2)}, u32[]{:S(2)}) collective-permute-start(f32[64,128]{1,0:T(8,128)S(1)} %get-tuple-element.19), channel_id=1, source_target_pairs={{0,1},{1,0},{2,3},{3,2},{4,5},{5,4},{6,7},{7,6},{8,9},{9,8},{10,11... | collective-permute-start | bytes 98312 | tf_op jit(solution)/shard_map/ppermute | solution.py:584
  34.5 0.9 %collective-permute-done.2 = f32[64,128]{1,0:T(8,128)S(1)} collective-permute-done((f32[64,128]{1,0:T(8,128)S(1)}, f32[64,128]{1,0:T(8,128)S(1)}, u32[]{:S(2)}, u32[]{:S(2)}) %collective-permute-start.2) | collective-permute-done | bytes 32800 | tf_op jit(solution)/shard_map/ppermute | solution.py:584
  35.4 2.0 %collective-permute-start.3 = (f32[64,128]{1,0:T(8,128)S(1)}, f32[64,128]{1,0:T(8,128)S(1)}, u32[]{:S(2)}, u32[]{:S(2)}) collective-permute-start(f32[64,128]{1,0:T(8,128)S(1)} %pad_maximum_fusion), channel_id=1, source_target_pairs={{0,2},{1,3},{2,0},{3,1},{4,6},{5,7},{6,4},{7,5},{8,10},{9,11},{10,... | collective-permute-start | bytes 98312 | tf_op jit(solution)/shard_map/ppermute | solution.py:584
  37.4 2.0 %collective-permute-done.3 = f32[64,128]{1,0:T(8,128)S(1)} collective-permute-done((f32[64,128]{1,0:T(8,128)S(1)}, f32[64,128]{1,0:T(8,128)S(1)}, u32[]{:S(2)}, u32[]{:S(2)}) %collective-permute-start.3) | collective-permute-done | bytes 32800 | tf_op jit(solution)/shard_map/ppermute | solution.py:584
  39.4 3.0 %collective-permute-start.4 = (f32[64,128]{1,0:T(8,128)S(1)}, f32[64,128]{1,0:T(8,128)S(1)}, u32[]{:S(2)}, u32[]{:S(2)}) collective-permute-start(f32[64,128]{1,0:T(8,128)S(1)} %pad_maximum_fusion.1), channel_id=1, source_target_pairs={{0,4},{1,5},{2,6},{3,7},{4,0},{5,1},{6,2},{7,3},{8,12},{9,13},{10,... | collective-permute-start | bytes 98312 | tf_op jit(solution)/shard_map/ppermute | solution.py:584
  42.4 1.9 %collective-permute-done.4 = f32[64,128]{1,0:T(8,128)S(1)} collective-permute-done((f32[64,128]{1,0:T(8,128)S(1)}, f32[64,128]{1,0:T(8,128)S(1)}, u32[]{:S(2)}, u32[]{:S(2)}) %collective-permute-start.4) | collective-permute-done | bytes 32800 | tf_op jit(solution)/shard_map/ppermute | solution.py:584
  44.4 3.1 %collective-permute-start.5 = (f32[64,128]{1,0:T(8,128)S(1)}, f32[64,128]{1,0:T(8,128)S(1)}, u32[]{:S(2)}, u32[]{:S(2)}) collective-permute-start(f32[64,128]{1,0:T(8,128)S(1)} %pad_maximum_fusion.2), channel_id=1, source_target_pairs={{0,8},{1,9},{2,10},{3,11},{4,12},{5,13},{6,14},{7,15},{8,0},{9,1},... | collective-permute-start | bytes 98312 | tf_op jit(solution)/shard_map/ppermute | solution.py:584
  47.4 1.9 %collective-permute-done.5 = f32[64,128]{1,0:T(8,128)S(1)} collective-permute-done((f32[64,128]{1,0:T(8,128)S(1)}, f32[64,128]{1,0:T(8,128)S(1)}, u32[]{:S(2)}, u32[]{:S(2)}) %collective-permute-start.5) | collective-permute-done | bytes 32800 | tf_op jit(solution)/shard_map/ppermute | solution.py:584
  49.3 10.5 %solve.1 = (f32[64,32,512]{2,1,0:T(8,128)}, f32[64,64]{1,0:T(8,128)}) custom-call(f32[64,128]{1,0:T(8,128)S(1)} %pad_maximum_fusion.3.pairs, f32[64,128]{1,0:T(8,128)S(1)} %get-tuple-element.20.inner_scale, f32[64,128]{1,0:T(8,128)S(1)} %get-tuple-element.21.edge_scale, bf16[24,256,512]{2,1,0:T(8,128)(2,1)S(1)} %get-tuple-element.22.inner, ...), custom_call_target="tpu_custom_call" | custom-call | tf_op jit(solution)/shard_map/solve/pallas_call | solution.py:659
  (8 shorter events, 0.1 us)
Async XLA Ops:
  0.6 6.7 %copy-start.3 = (f32[32,512]{1,0:T(8,128)S(1)}, f32[32,512]{1,0:T(8,128)}, u32[]{:S(2)}) copy-start(f32[32,512]{1,0:T(8,128)} %friction.3) | copy-start | bytes 196612
  0.6 6.7 %copy-start.2 = (f32[32,512]{1,0:T(8,128)S(1)}, f32[32,512]{1,0:T(8,128)}, u32[]{:S(2)}) copy-start(f32[32,512]{1,0:T(8,128)} %speed.3) | copy-start | bytes 196612
  0.7 6.7 %copy-start.1 = (f32[32,512]{1,0:T(8,128)S(1)}, f32[32,512]{1,0:T(8,128)}, u32[]{:S(2)}) copy-start(f32[32,512]{1,0:T(8,128)} %kappa.3) | copy-start | bytes 196612
  0.7 6.7 %copy-start = (f32[64,32,512]{2,1,0:T(8,128)S(1)}, f32[64,32,512]{2,1,0:T(8,128)}, u32[]{:S(2)}) copy-start(f32[64,32,512]{2,1,0:T(8,128)} %cells.3) | copy-start | bytes 12582916
  0.7 6.7 %copy-start.4 = (s32[32,16]{0,1:T(8,128)S(1)}, s32[32,16]{0,1:T(8,128)}, u32[]{:S(2)}) copy-start(s32[32,16]{0,1:T(8,128)} %param.10) | copy-start | bytes 6148
  0.7 6.7 %copy-start.5 = (s32[64]{0:T(128)S(1)}, s32[64]{0:T(128)}, u32[]{:S(2)}) copy-start(s32[64]{0:T(128)} %sites.3) | copy-start | bytes 772
  3.6 21.6 %collective-permute-start = (f32[4,72,512]{2,1,0:T(8,128)}, f32[4,72,512]{2,1,0:T(8,128)S(1)}, u32[]{:S(2)}, u32[]{:S(2)}) collective-permute-start(f32[4,72,512]{2,1,0:T(8,128)} %get-tuple-element.13), channel_id=1, source_target_pairs={{0,1},{1,2},{2,3},{3,4},{4,5},{5,6},{6,7},{7,8},{8,9},{9,10},{10,1... | collective-permute-start | bytes 1769480 | tf_op jit(solution)/shard_map/ppermute | solution.py:611
  6.0 19.2 %collective-permute-start.1 = (f32[4,72,512]{2,1,0:T(8,128)}, f32[4,72,512]{2,1,0:T(8,128)S(1)}, u32[]{:S(2)}, u32[]{:S(2)}) collective-permute-start(f32[4,72,512]{2,1,0:T(8,128)} %get-tuple-element.14), channel_id=1, source_target_pairs={{1,0},{2,1},{3,2},{4,3},{5,4},{6,5},{7,6},{8,7},{9,8},{10,9},{11,1... | collective-permute-start | bytes 1769480 | tf_op jit(solution)/shard_map/ppermute | solution.py:612
  31.3 4.1 %collective-permute-start.2 = (f32[64,128]{1,0:T(8,128)S(1)}, f32[64,128]{1,0:T(8,128)S(1)}, u32[]{:S(2)}, u32[]{:S(2)}) collective-permute-start(f32[64,128]{1,0:T(8,128)S(1)} %get-tuple-element.19), channel_id=1, source_target_pairs={{0,1},{1,0},{2,3},{3,2},{4,5},{5,4},{6,7},{7,6},{8,9},{9,8},{10,11... | collective-permute-start | bytes 98312 | tf_op jit(solution)/shard_map/ppermute | solution.py:584
  35.4 4.0 %collective-permute-start.3 = (f32[64,128]{1,0:T(8,128)S(1)}, f32[64,128]{1,0:T(8,128)S(1)}, u32[]{:S(2)}, u32[]{:S(2)}) collective-permute-start(f32[64,128]{1,0:T(8,128)S(1)} %pad_maximum_fusion), channel_id=1, source_target_pairs={{0,2},{1,3},{2,0},{3,1},{4,6},{5,7},{6,4},{7,5},{8,10},{9,11},{10,... | collective-permute-start | bytes 98312 | tf_op jit(solution)/shard_map/ppermute | solution.py:584
  39.4 4.9 %collective-permute-start.4 = (f32[64,128]{1,0:T(8,128)S(1)}, f32[64,128]{1,0:T(8,128)S(1)}, u32[]{:S(2)}, u32[]{:S(2)}) collective-permute-start(f32[64,128]{1,0:T(8,128)S(1)} %pad_maximum_fusion.1), channel_id=1, source_target_pairs={{0,4},{1,5},{2,6},{3,7},{4,0},{5,1},{6,2},{7,3},{8,12},{9,13},{10,... | collective-permute-start | bytes 98312 | tf_op jit(solution)/shard_map/ppermute | solution.py:584
  44.4 5.0 %collective-permute-start.5 = (f32[64,128]{1,0:T(8,128)S(1)}, f32[64,128]{1,0:T(8,128)S(1)}, u32[]{:S(2)}, u32[]{:S(2)}) collective-permute-start(f32[64,128]{1,0:T(8,128)S(1)} %pad_maximum_fusion.2), channel_id=1, source_target_pairs={{0,8},{1,9},{2,10},{3,11},{4,12},{5,13},{6,14},{7,15},{8,0},{9,1},... | collective-permute-start | bytes 98312 | tf_op jit(solution)/shard_map/ppermute | solution.py:584

commit v5 on v4

--- a/solution.py
+++ b/solution.py
@@ -12,6 +12,7 @@
 IMPULSE_GAIN = 3.0
 AXIS = "gx"
 DEPTH = 4
+ARRIVALS = 11
 PACK = 8
 MIB = 1024 * 1024
 
@@ -65,8 +66,8 @@
         weight_row(weights, w_at, 0, like),
         weight_row(weights, w_at - 1, 2, like),
         weight_row(weights, w_at + 1, 1, like),
-        rolled(weight_row(weights, w_at, 4, like), 1),
-        rolled(weight_row(weights, w_at, 3, like), -1),
+        weight_row(weights, w_at, 5, like),
+        weight_row(weights, w_at, 6, like),
     )
 
 
@@ -89,13 +90,20 @@
     return site >> (columns.bit_length() - 1), site & (columns - 1)
 
 
-def add_impulses(sites, found, count, target, place_of, columns, strength):
+def add_impulses(sites, found, count, target, place_of, columns, strength, wanted=None):
     column_ids = lax.broadcasted_iota(jnp.int32, (1, columns), 1)
 
     def one(index, carry):
         k = found[index]
         row, column = row_and_column(sites[k], columns)
-        target[place_of(row), pl.ds(k, 1), :] += jnp.where(column_ids == column, strength, 0.0)
+
+        def add():
+            target[place_of(row), pl.ds(k, 1), :] += jnp.where(column_ids == column, strength, 0.0)
+
+        if wanted is None:
+            add()
+        else:
+            pl.when(wanted(row))(add)
         return carry
 
     lax.fori_loop(0, count, one, 0)
@@ -121,6 +129,11 @@
     layers[3] = jnp.where(column_ids == 0, 0.0, layers[3])
     layers[4] = jnp.where(column_ids == columns - 1, 0.0, layers[4])
     return layers
+
+
+def turn_weights(weights):
+    weights[5] = rolled(weights[4], 1)
+    weights[6] = rolled(weights[3], -1)
 
 
 def pack_kernel(cells, kappa, speed, friction, upwind, to_below, to_above, cell_rows, directions, sems, cell_sems):
@@ -163,15 +176,30 @@
     first_row = lax.axis_index(AXIS) * rows
 
     copies = [pltpu.make_async_copy(cells.at[:, r, :], v.at[r], sems.at[r]) for r in range(rows)]
-    for copy in copies:
+    for copy in copies[:ARRIVALS]:
         copy.start()
     for index, layer in enumerate(weight_layers(kappa[...], speed[...], friction[...], upwind[...])):
         weights[index] = layer
+    turn_weights(weights)
     first_cell, end_cell = first_row * columns, (first_row + rows) * columns
     hits = find_impulses(sites, found, lambda site: (site >= first_cell) & (site < end_cell), probes)
-    for copy in copies:
-        copy.wait()
-    add_impulses(sites, found, hits, v, lambda row: row - first_row, columns, strength)
+    def forward_first(r):
+        forward_row(v, r, f1, r, weights, r, probes, columns)
+
+    ready, done = 0, 1
+    while ready < rows:
+        upto = min(rows, ready + ARRIVALS)
+        for copy in copies[upto : upto + ARRIVALS]:
+            copy.start()
+        for copy in copies[ready:upto]:
+            copy.wait()
+        low, high = first_row + ready, first_row + upto
+        add_impulses(
+            sites, found, hits, v, lambda row: row - first_row, columns, strength,
+            lambda row, low=low, high=high: (row >= low) & (row < high),
+        )
+        in_steps(done, upto - 1, forward_first)
+        ready, done = upto, upto - 1
 
     def sweep(row_fn, source, target, first, shift=0):
         def body(r):
@@ -179,7 +207,6 @@
 
         in_steps(first, rows - first, body)
 
-    sweep(forward_row, v, f1, 1)
     sweep(forward_row, f1, f2, 2)
     sweep(adjoint_row, f2, a1, 3)
     sweep(adjoint_row, a1, response, DEPTH, DEPTH)
@@ -202,8 +229,8 @@
     copies = [
         (above.at[:, pl.ds(probes, PACK), :], behind.at[0]),
         (below.at[:, pl.ds(probes, PACK), :], behind.at[1]),
-        (weights.at[:, pl.ds(0, 8), :], w.at[:, pl.ds(start_a, 8), :]),
-        (weights.at[:, pl.ds(rows - 8, 8), :], w.at[:, pl.ds(start_b, 8), :]),
+        (weights.at[pl.ds(0, 5), pl.ds(0, 8), :], w.at[pl.ds(0, 5), pl.ds(start_a, 8), :]),
+        (weights.at[pl.ds(0, 5), pl.ds(rows - 8, 8), :], w.at[pl.ds(0, 5), pl.ds(start_b, 8), :]),
         (above.at[:, pl.ds(0, probes), :], va.at[pl.ds(0, DEPTH)]),
         (below.at[:, pl.ds(0, probes), :], va.at[pl.ds(DEPTH + 4, DEPTH)]),
         (top.at[0], va.at[pl.ds(DEPTH, 2)]),
@@ -230,6 +257,7 @@
         for r in range(DEPTH):
             w[layer, DEPTH + r : DEPTH + r + 1, :] = behind[0, r, layer : layer + 1, :]
             w[layer, start_b + 2 * DEPTH + r : start_b + 2 * DEPTH + r + 1, :] = behind[1, r, layer : layer + 1, :]
+    turn_weights(w)
     add_impulses(
         sites, found, hits, va,
         lambda row: jnp.where(row < first_row, row - first_row + DEPTH, row - first_row - rows + DEPTH + 4), columns, strength,
@@ -311,21 +339,31 @@
     scale_out[...] = jnp.broadcast_to(inverse, scale_out.shape)
     sums[...] = jnp.zeros_like(sums)
 
-    def cut(index, carry):
-        for pair in range(2):
-            for r in (4 * index + 2 * pair, 4 * index + 2 * pair + 1):
-                parts = digits_of(field[r] * scale)
-                cells[r] = jnp.concatenate([part.astype(jnp.bfloat16) for part in parts], axis=0)
-        total = sums[...]
+    def cut(index):
+        for r in range(4):
+            parts = digits_of(field[4 * index + r] * scale)
+            cells[4 * index + r] = jnp.concatenate([part.astype(jnp.bfloat16) for part in parts], axis=0)
+
+    def products(index):
+        pairs = []
         for pair in range(2):
             r = 4 * index + 2 * pair
             two = jnp.concatenate([cells[r], cells[r + 1]], axis=1)
-            product = lax.dot_general(two, two, (((1,), (1,)), ((), ())), preferred_element_type=jnp.float32)
-            total = total + product.astype(jnp.int32)
-        sums[...] = total
+            pairs.append(lax.dot_general(two, two, (((1,), (1,)), ((), ())), preferred_element_type=jnp.float32))
+        return pairs
+
+    def gather(pairs):
+        sums[...] += pairs[0].astype(jnp.int32) + pairs[1].astype(jnp.int32)
+
+    def step(index, carry):
+        pairs = products(index)
+        cut(index + 1)
+        gather(pairs)
         return carry
 
-    lax.fori_loop(0, rows // 4, cut, 0)
+    cut(0)
+    lax.fori_loop(0, rows // 4 - 1, step, 0)
+    gather(products(rows // 4 - 1))
     places = []
     for place in range(2 * DIGITS - 1):
         terms = [
@@ -369,7 +407,7 @@
     return jnp.transpose(square)[:, :size]
 
 
-PANEL = 4
+PANEL = 8
 
 
 def eliminated(block):
@@ -497,8 +535,8 @@
     @pl.when(is_small)
     def _():
         y = weight * error
-        for _ in range(4):
-            y = weight * (error - dot(y, y, ((1,), (1,))))
+        rounds = jnp.where(spread < 1e-5, 2, 4)
+        y = lax.fori_loop(0, rounds, lambda _, y: weight * (error - dot(y, y, ((1,), (1,)))), y)
         change[...] = y
         square = dot(y, y)
         change_inverse[...] = (identity - y) + dot(identity - y, square)
@@ -628,7 +666,7 @@
     inner, inner_scale, pairs, top, bottom, weights = call(
         functools.partial(inner_kernel, strength),
         "inner_rows",
-        digit_rows(inner_count) + (kept, kept, shape((5, rows, columns), f32)),
+        digit_rows(inner_count) + (kept, kept, shape((7, rows, columns), f32)),
         [whole(pltpu.SMEM), whole(pl.ANY)] + [whole()] * 4,
         (whole(),) * 6,
         [field] * 4
@@ -647,7 +685,7 @@
         [whole(pltpu.SMEM)] + [whole(pl.ANY)] * 5 + [whole()],
         (whole(), whole(), whole()),
         [
-            pltpu.VMEM((5, 8 * DEPTH, columns), f32), fields, levels, levels,
+            pltpu.VMEM((7, 8 * DEPTH, columns), f32), fields, levels, levels,
             pltpu.VMEM((2, DEPTH, PACK, columns), f32),
         ]
         + digit_scratch(edge_count)

time: 60.2 us -> 58.8 us (0.977)
  Pallas kernels: 37.3 us -> 35.7 us
    pallas_call x1, Pallas kernels: 10.5 us -> 9.48 us  [on_device(): call(functools.partial(solve_kernel, cell_scale), 'solve', (shape((count,...]
where the time goes in v5:
time: 58.8 us; the launch traced here: 58.6 us
  Pallas kernels  35.7 us (61%)
  starting transfers between devices  15 us (26%)
  waiting for transfers between devices  6.77 us (12%)
  between operations  0.99 us (2%)
    pallas_call x1, Pallas kernels, on_device(): call(functools.partial(inner_kernel, strength), 'inner_rows', digit_rows(...  17.6 us
    ppermute x4, starting transfers between devices, summed(): lax.ppermute(pairs, AXIS, [(i, i ^ distance) for i in range(count)])  11.4 us
    pallas_call x1, Pallas kernels, on_device(): call(functools.partial(solve_kernel, cell_scale), 'solve', (shape((count,...  9.48 us
    ppermute x4, waiting for transfers between devices, summed(): lax.ppermute(pairs, AXIS, [(i, i ^ distance) for i in range(count)])  6.77 us
    pallas_call x1, Pallas kernels, on_device(): call(functools.partial(edge_kernel, strength, rows), 'edge_rows', digit_r...  5.69 us
    pallas_call x1, Pallas kernels, on_device(): call(pack_kernel, 'pack', (halo, halo), [whole(pl.ANY)] * 5, (whole(), wh...  2.9 us
    ppermute x1, starting transfers between devices, on_device(): lax.ppermute(to_below, AXIS, [(i, i + 1) for i in range(size - 1)])  2.39 us
    ppermute x1, starting transfers between devices, on_device(): lax.ppermute(to_above, AXIS, [(i + 1, i) for i in range(size - 1)])  1.29 us
  transfers between devices with their start and end apart: 6, of which 4 were waited for; matrix products, arithmetic and copies ran while one was open for 0% of the time, Pallas kernels for 30%

profile of v5, /device:TPU:0, one launch (start us, length us, event | category | flops | bytes accessed | tf_op | source)
XLA Modules:
  0.0 58.6 jit_solution(11380509235716246936)
XLA Ops:
  0.6 0.0 copy-start.3
  0.6 0.0 copy-start.2
  0.7 0.0 copy-start.1
  0.7 0.0 copy-start
  0.7 0.0 copy-start.4
  0.7 0.0 copy-start.5
  0.7 2.9 %pack.1 = (f32[4,72,512]{2,1,0:T(8,128)}, f32[4,72,512]{2,1,0:T(8,128)}) custom-call(f32[64,32,512]{2,1,0:T(8,128)} %cells.3, f32[32,512]{1,0:T(8,128)} %kappa.3, f32[32,512]{1,0:T(8,128)} %speed.3, f32[32,512]{1,0:T(8,128)} %friction.3, s32[16,32]{1,0:T(8,128)} %bitcast.1), custom_call_target="tpu_custom_call" | custom-call | tf_op jit(solution)/shard_map/pack/pallas_call | solution.py:635
  3.6 2.4 %collective-permute-start = (f32[4,72,512]{2,1,0:T(8,128)}, f32[4,72,512]{2,1,0:T(8,128)S(1)}, u32[]{:S(2)}, u32[]{:S(2)}) collective-permute-start(f32[4,72,512]{2,1,0:T(8,128)} %get-tuple-element.13), channel_id=1, source_target_pairs={{0,1},{1,2},{2,3},{3,4},{4,5},{5,6},{6,7},{7,8},{8,9},{9,10},{10,1... | collective-permute-start | bytes 1769480 | tf_op jit(solution)/shard_map/ppermute | solution.py:649
  6.0 1.3 %collective-permute-start.1 = (f32[4,72,512]{2,1,0:T(8,128)}, f32[4,72,512]{2,1,0:T(8,128)S(1)}, u32[]{:S(2)}, u32[]{:S(2)}) collective-permute-start(f32[4,72,512]{2,1,0:T(8,128)} %get-tuple-element.14), channel_id=1, source_target_pairs={{1,0},{2,1},{3,2},{4,3},{5,4},{6,5},{7,6},{8,7},{9,8},{10,9},{11,1... | collective-permute-start | bytes 1769480 | tf_op jit(solution)/shard_map/ppermute | solution.py:650
  7.3 0.0 copy-done.3
  7.3 0.0 copy-done.2
  7.3 0.0 copy-done.1
  7.3 0.0 copy-done
  7.3 0.0 copy-done.4
  7.3 0.0 copy-done.5
  7.4 17.6 %inner_rows.1 = (bf16[24,256,512]{2,1,0:T(8,128)(2,1)S(1)}, f32[64,128]{1,0:T(8,128)S(1)}, f32[64,128]{1,0:T(8,128)S(1)}, f32[4,2,64,512]{3,2,1,0:T(8,128)S(1)},...) custom-call(s32[64]{0:T(128)S(1)} %copy-done.5, f32[64,32,512]{2,1,0:T(8,128)S(1)} %copy-done, ...), custom_call_target="tpu_custom_call" | custom-call | flops 10000000000 | bytes 16777216 | tf_op jit(solution)/shard_map/inner_rows/pallas_call | solution.py:666
  25.0 0.0 collective-permute-done.above
  25.0 0.0 collective-permute-done.1.below
  25.0 5.7 %edge_rows.1 = (bf16[8,256,512]{2,1,0:T(8,128)(2,1)S(1)}, f32[64,128]{1,0:T(8,128)S(1)}, f32[64,128]{1,0:T(8,128)S(1)}) custom-call(s32[64]{0:T(128)S(1)} %copy-done.5, f32[4,72,512]{2,1,0:T(8,128)S(1)} %collective-permute-done.above, f32[4,72,512]{2,1,0:T(8,128)S(1)} %collective-permute-done.1.below, f32[7,32,512]{2,1,0:T(8,128)S(1)} %get-tuple-element.15.weights, ...), custom_call_target="tpu_custom_call" | custom-call | tf_op jit(solution)/shard_map/edge_rows/pallas_call | solution.py:681
  30.7 3.3 %collective-permute-start.2 = (f32[64,128]{1,0:T(8,128)S(1)}, f32[64,128]{1,0:T(8,128)S(1)}, u32[]{:S(2)}, u32[]{:S(2)}) collective-permute-start(f32[64,128]{1,0:T(8,128)S(1)} %get-tuple-element.19), channel_id=1, source_target_pairs={{0,1},{1,0},{2,3},{3,2},{4,5},{5,4},{6,7},{7,6},{8,9},{9,8},{10,11... | collective-permute-start | bytes 98312 | tf_op jit(solution)/shard_map/ppermute | solution.py:622
  34.0 0.9 %collective-permute-done.2 = f32[64,128]{1,0:T(8,128)S(1)} collective-permute-done((f32[64,128]{1,0:T(8,128)S(1)}, f32[64,128]{1,0:T(8,128)S(1)}, u32[]{:S(2)}, u32[]{:S(2)}) %collective-permute-start.2) | collective-permute-done | bytes 32800 | tf_op jit(solution)/shard_map/ppermute | solution.py:622
  34.9 1.9 %collective-permute-start.3 = (f32[64,128]{1,0:T(8,128)S(1)}, f32[64,128]{1,0:T(8,128)S(1)}, u32[]{:S(2)}, u32[]{:S(2)}) collective-permute-start(f32[64,128]{1,0:T(8,128)S(1)} %pad_maximum_fusion), channel_id=1, source_target_pairs={{0,2},{1,3},{2,0},{3,1},{4,6},{5,7},{6,4},{7,5},{8,10},{9,11},{10,... | collective-permute-start | bytes 98312 | tf_op jit(solution)/shard_map/ppermute | solution.py:622
  36.7 2.1 %collective-permute-done.3 = f32[64,128]{1,0:T(8,128)S(1)} collective-permute-done((f32[64,128]{1,0:T(8,128)S(1)}, f32[64,128]{1,0:T(8,128)S(1)}, u32[]{:S(2)}, u32[]{:S(2)}) %collective-permute-start.3) | collective-permute-done | bytes 32800 | tf_op jit(solution)/shard_map/ppermute | solution.py:622
  38.9 3.2 %collective-permute-start.4 = (f32[64,128]{1,0:T(8,128)S(1)}, f32[64,128]{1,0:T(8,128)S(1)}, u32[]{:S(2)}, u32[]{:S(2)}) collective-permute-start(f32[64,128]{1,0:T(8,128)S(1)} %pad_maximum_fusion.1), channel_id=1, source_target_pairs={{0,4},{1,5},{2,6},{3,7},{4,0},{5,1},{6,2},{7,3},{8,12},{9,13},{10,... | collective-permute-start | bytes 98312 | tf_op jit(solution)/shard_map/ppermute | solution.py:622
  42.1 1.9 %collective-permute-done.4 = f32[64,128]{1,0:T(8,128)S(1)} collective-permute-done((f32[64,128]{1,0:T(8,128)S(1)}, f32[64,128]{1,0:T(8,128)S(1)}, u32[]{:S(2)}, u32[]{:S(2)}) %collective-permute-start.4) | collective-permute-done | bytes 32800 | tf_op jit(solution)/shard_map/ppermute | solution.py:622
  44.0 3.1 %collective-permute-start.5 = (f32[64,128]{1,0:T(8,128)S(1)}, f32[64,128]{1,0:T(8,128)S(1)}, u32[]{:S(2)}, u32[]{:S(2)}) collective-permute-start(f32[64,128]{1,0:T(8,128)S(1)} %pad_maximum_fusion.2), channel_id=1, source_target_pairs={{0,8},{1,9},{2,10},{3,11},{4,12},{5,13},{6,14},{7,15},{8,0},{9,1},... | collective-permute-start | bytes 98312 | tf_op jit(solution)/shard_map/ppermute | solution.py:622
  47.0 1.9 %collective-permute-done.5 = f32[64,128]{1,0:T(8,128)S(1)} collective-permute-done((f32[64,128]{1,0:T(8,128)S(1)}, f32[64,128]{1,0:T(8,128)S(1)}, u32[]{:S(2)}, u32[]{:S(2)}) %collective-permute-start.5) | collective-permute-done | bytes 32800 | tf_op jit(solution)/shard_map/ppermute | solution.py:622
  49.0 9.5 %solve.1 = (f32[64,32,512]{2,1,0:T(8,128)}, f32[64,64]{1,0:T(8,128)}) custom-call(f32[64,128]{1,0:T(8,128)S(1)} %pad_maximum_fusion.3.pairs, f32[64,128]{1,0:T(8,128)S(1)} %get-tuple-element.20.inner_scale, f32[64,128]{1,0:T(8,128)S(1)} %get-tuple-element.21.edge_scale, bf16[24,256,512]{2,1,0:T(8,128)(2,1)S(1)} %get-tuple-element.22.inner, ...), custom_call_target="tpu_custom_call" | custom-call | tf_op jit(solution)/shard_map/solve/pallas_call | solution.py:697
  (8 shorter events, 0.1 us)
Async XLA Ops:
  0.6 6.7 %copy-start.3 = (f32[32,512]{1,0:T(8,128)S(1)}, f32[32,512]{1,0:T(8,128)}, u32[]{:S(2)}) copy-start(f32[32,512]{1,0:T(8,128)} %friction.3) | copy-start | bytes 196612
  0.6 6.7 %copy-start.2 = (f32[32,512]{1,0:T(8,128)S(1)}, f32[32,512]{1,0:T(8,128)}, u32[]{:S(2)}) copy-start(f32[32,512]{1,0:T(8,128)} %speed.3) | copy-start | bytes 196612
  0.7 6.7 %copy-start.1 = (f32[32,512]{1,0:T(8,128)S(1)}, f32[32,512]{1,0:T(8,128)}, u32[]{:S(2)}) copy-start(f32[32,512]{1,0:T(8,128)} %kappa.3) | copy-start | bytes 196612
  0.7 6.7 %copy-start = (f32[64,32,512]{2,1,0:T(8,128)S(1)}, f32[64,32,512]{2,1,0:T(8,128)}, u32[]{:S(2)}) copy-start(f32[64,32,512]{2,1,0:T(8,128)} %cells.3) | copy-start | bytes 12582916
  0.7 6.7 %copy-start.4 = (s32[32,16]{0,1:T(8,128)S(1)}, s32[32,16]{0,1:T(8,128)}, u32[]{:S(2)}) copy-start(s32[32,16]{0,1:T(8,128)} %param.10) | copy-start | bytes 6148
  0.7 6.7 %copy-start.5 = (s32[64]{0:T(128)S(1)}, s32[64]{0:T(128)}, u32[]{:S(2)}) copy-start(s32[64]{0:T(128)} %sites.3) | copy-start | bytes 772
  3.6 21.4 %collective-permute-start = (f32[4,72,512]{2,1,0:T(8,128)}, f32[4,72,512]{2,1,0:T(8,128)S(1)}, u32[]{:S(2)}, u32[]{:S(2)}) collective-permute-start(f32[4,72,512]{2,1,0:T(8,128)} %get-tuple-element.13), channel_id=1, source_target_pairs={{0,1},{1,2},{2,3},{3,4},{4,5},{5,6},{6,7},{7,8},{8,9},{9,10},{10,1... | collective-permute-start | bytes 1769480 | tf_op jit(solution)/shard_map/ppermute | solution.py:649
  6.0 19.0 %collective-permute-start.1 = (f32[4,72,512]{2,1,0:T(8,128)}, f32[4,72,512]{2,1,0:T(8,128)S(1)}, u32[]{:S(2)}, u32[]{:S(2)}) collective-permute-start(f32[4,72,512]{2,1,0:T(8,128)} %get-tuple-element.14), channel_id=1, source_target_pairs={{1,0},{2,1},{3,2},{4,3},{5,4},{6,5},{7,6},{8,7},{9,8},{10,9},{11,1... | collective-permute-start | bytes 1769480 | tf_op jit(solution)/shard_map/ppermute | solution.py:650
  30.7 4.1 %collective-permute-start.2 = (f32[64,128]{1,0:T(8,128)S(1)}, f32[64,128]{1,0:T(8,128)S(1)}, u32[]{:S(2)}, u32[]{:S(2)}) collective-permute-start(f32[64,128]{1,0:T(8,128)S(1)} %get-tuple-element.19), channel_id=1, source_target_pairs={{0,1},{1,0},{2,3},{3,2},{4,5},{5,4},{6,7},{7,6},{8,9},{9,8},{10,11... | collective-permute-start | bytes 98312 | tf_op jit(solution)/shard_map/ppermute | solution.py:622
  34.9 4.0 %collective-permute-start.3 = (f32[64,128]{1,0:T(8,128)S(1)}, f32[64,128]{1,0:T(8,128)S(1)}, u32[]{:S(2)}, u32[]{:S(2)}) collective-permute-start(f32[64,128]{1,0:T(8,128)S(1)} %pad_maximum_fusion), channel_id=1, source_target_pairs={{0,2},{1,3},{2,0},{3,1},{4,6},{5,7},{6,4},{7,5},{8,10},{9,11},{10,... | collective-permute-start | bytes 98312 | tf_op jit(solution)/shard_map/ppermute | solution.py:622
  38.9 5.1 %collective-permute-start.4 = (f32[64,128]{1,0:T(8,128)S(1)}, f32[64,128]{1,0:T(8,128)S(1)}, u32[]{:S(2)}, u32[]{:S(2)}) collective-permute-start(f32[64,128]{1,0:T(8,128)S(1)} %pad_maximum_fusion.1), channel_id=1, source_target_pairs={{0,4},{1,5},{2,6},{3,7},{4,0},{5,1},{6,2},{7,3},{8,12},{9,13},{10,... | collective-permute-start | bytes 98312 | tf_op jit(solution)/shard_map/ppermute | solution.py:622
  44.0 5.0 %collective-permute-start.5 = (f32[64,128]{1,0:T(8,128)S(1)}, f32[64,128]{1,0:T(8,128)S(1)}, u32[]{:S(2)}, u32[]{:S(2)}) collective-permute-start(f32[64,128]{1,0:T(8,128)S(1)} %pad_maximum_fusion.2), channel_id=1, source_target_pairs={{0,8},{1,9},{2,10},{3,11},{4,12},{5,13},{6,14},{7,15},{8,0},{9,1},... | collective-permute-start | bytes 98312 | tf_op jit(solution)/shard_map/ppermute | solution.py:622

commit v6 on v5

--- a/solution.py
+++ b/solution.py
@@ -13,6 +13,7 @@
 AXIS = "gx"
 DEPTH = 4
 ARRIVALS = 11
+GROUP = 4
 PACK = 8
 MIB = 1024 * 1024
 
@@ -38,17 +39,20 @@
         body(r)
 
 
-def sweep_row(source, at, target, to, probes, columns, center, above, below, left, right):
+def sweep_row(source, at, target, to, probes, columns, center, above, below, left, right, tops=None):
     for first in range(0, probes, 8):
         octet = slice(first, first + 8)
         middle = source[at, octet, :]
-        target[to, octet, :] = (
+        result = (
             center * middle
             + above * source[at - 1, octet, :]
             + below * source[at + 1, octet, :]
             + left * rolled(middle, 1)
             + right * rolled(middle, -1)
         )
+        target[to, octet, :] = result
+        if tops is not None:
+            tops[octet, :] = jnp.maximum(tops[octet, :], jnp.abs(result))
 
 
 def forward_row(source, at, target, to, weights, w_at, probes, columns):
@@ -59,7 +63,7 @@
     )
 
 
-def adjoint_row(source, at, target, to, weights, w_at, probes, columns):
+def adjoint_row(source, at, target, to, weights, w_at, probes, columns, tops=None):
     like = (8, columns)
     sweep_row(
         source, at, target, to, probes, columns,
@@ -68,6 +72,7 @@
         weight_row(weights, w_at + 1, 1, like),
         weight_row(weights, w_at, 5, like),
         weight_row(weights, w_at, 6, like),
+        tops=tops,
     )
 
 
@@ -170,7 +175,7 @@
 
 
 def inner_kernel(
-    strength, sites, cells, kappa, speed, friction, upwind, digits, scale, pairs, top, bottom, weights, v, f1, f2, a1, response, sums, found, sems
+    strength, sites, cells, kappa, speed, friction, upwind, digits, scale, pairs, top, bottom, weights, v, f1, f2, a1, response, sums, tops, found, sems
 ):
     rows, probes, columns = v.shape
     first_row = lax.axis_index(AXIS) * rows
@@ -201,26 +206,27 @@
         in_steps(done, upto - 1, forward_first)
         ready, done = upto, upto - 1
 
-    def sweep(row_fn, source, target, first, shift=0):
+    def sweep(row_fn, source, target, first, shift=0, **kept):
         def body(r):
-            row_fn(source, r, target, r - shift, weights, r, probes, columns)
+            row_fn(source, r, target, r - shift, weights, r, probes, columns, **kept)
 
         in_steps(first, rows - first, body)
 
     sweep(forward_row, f1, f2, 2)
     sweep(adjoint_row, f2, a1, 3)
-    sweep(adjoint_row, a1, response, DEPTH, DEPTH)
+    tops[...] = jnp.zeros_like(tops)
+    sweep(adjoint_row, a1, response, DEPTH, DEPTH, tops=tops)
     for level, field in enumerate((v, f1, f2, a1)):
         for j in range(2):
             top[level, j] = field[level + j]
             bottom[level, j] = field[rows - 2 - level + j]
-    high, low = gram_pair(response, rows - 2 * DEPTH, digits, scale, sums)
+    high, low = gram_pair(response, rows - 2 * DEPTH, tops, digits, scale, sums)
     pairs[...] = jnp.concatenate([folded(high), folded(low)], axis=0)
 
 
 def edge_kernel(
     strength, rows, sites, above, below, weights, top, bottom, inner_pairs, digits, scale, pairs,
-    w, va, la, lb, behind, response, sums, found, sems,
+    w, va, la, lb, behind, response, sums, tops, found, sems,
 ):
     probes, columns = top.shape[2:]
     first_row = lax.axis_index(AXIS) * rows
@@ -270,7 +276,10 @@
             row_fn(chain_a[level], j + 1, chain_a[level + 1], j, w, start_a + level - 3 + j, probes, columns)
             to = j + (DEPTH if level == 3 else 2)
             row_fn(chain_b[level], j + 1, chain_b[level + 1], to, w, start_b + 7 - level + j, probes, columns)
-    ours = gram_pair(response, 2 * DEPTH, digits, scale, sums)
+    for first in range(0, probes, 8):
+        sizes = [jnp.abs(response[r, first : first + 8, :]) for r in range(2 * DEPTH)]
+        tops[first : first + 8, :] = functools.reduce(jnp.maximum, sizes)
+    ours = gram_pair(response, 2 * DEPTH, tops, digits, scale, sums)
     half = probes // 2
     high, low = pair_sum(ours, (unfolded(inner_pairs[:half, :]), unfolded(inner_pairs[half:, :])))
     pairs[...] = jnp.concatenate([folded(high), folded(low)], axis=0)
@@ -324,46 +333,40 @@
     return pair_of(total, error + (a_low + b_low))
 
 
-def gram_pair(field, rows, cells, scale_out, sums):
+def gram_pair(field, rows, tops, cells, scale_out, sums):
     probes, columns = field.shape[1:]
 
-    def largest(index, so_far):
-        for r in (2 * index, 2 * index + 1):
-            so_far = tuple(jnp.maximum(m, jnp.abs(field[r, 8 * o : 8 * o + 8, :])) for o, m in enumerate(so_far))
-        return so_far
-
-    tops = lax.fori_loop(0, rows // 2, largest, tuple(jnp.zeros((8, columns), jnp.float32) for _ in range(probes // 8)))
-    top = jnp.concatenate([jnp.max(m, axis=1, keepdims=True) for m in tops], axis=0)
+    top = jnp.max(tops[...], axis=1, keepdims=True)
     scale = largest_power(lambda power: top * power <= 128.0, (probes, 1))
     inverse = 1.0 / scale
     scale_out[...] = jnp.broadcast_to(inverse, scale_out.shape)
     sums[...] = jnp.zeros_like(sums)
 
     def cut(index):
-        for r in range(4):
-            parts = digits_of(field[4 * index + r] * scale)
-            cells[4 * index + r] = jnp.concatenate([part.astype(jnp.bfloat16) for part in parts], axis=0)
+        for r in range(GROUP):
+            at = GROUP * index + r
+            parts = digits_of(field[at] * scale)
+            cells[at] = jnp.concatenate([part.astype(jnp.bfloat16) for part in parts], axis=0)
 
     def products(index):
-        pairs = []
-        for pair in range(2):
-            r = 4 * index + 2 * pair
+        total = None
+        for pair in range(GROUP // 2):
+            r = GROUP * index + 2 * pair
             two = jnp.concatenate([cells[r], cells[r + 1]], axis=1)
-            pairs.append(lax.dot_general(two, two, (((1,), (1,)), ((), ())), preferred_element_type=jnp.float32))
-        return pairs
-
-    def gather(pairs):
-        sums[...] += pairs[0].astype(jnp.int32) + pairs[1].astype(jnp.int32)
+            product = lax.dot_general(two, two, (((1,), (1,)), ((), ())), preferred_element_type=jnp.float32)
+            product = product.astype(jnp.int32)
+            total = product if total is None else total + product
+        return total
 
     def step(index, carry):
-        pairs = products(index)
+        total = products(index)
         cut(index + 1)
-        gather(pairs)
+        sums[...] += total
         return carry
 
     cut(0)
-    lax.fori_loop(0, rows // 4 - 1, step, 0)
-    gather(products(rows // 4 - 1))
+    lax.fori_loop(0, rows // GROUP - 1, step, 0)
+    sums[...] += products(rows // GROUP - 1)
     places = []
     for place in range(2 * DIGITS - 1):
         terms = [
@@ -564,17 +567,19 @@
         return jnp.concatenate([tall * 256.0**-a for a in range(DIGITS)], axis=1).astype(jnp.bfloat16)
 
     def finish(matrix, cells, first_row, count, shift):
-        def four(index, carry):
-            for j in range(4):
-                r = 4 * index + j
+        group = min(2 * GROUP, count)
+
+        def several(index, carry):
+            for j in range(group):
+                r = group * index + j
                 product = jnp.dot(matrix, cells[r + shift], preferred_element_type=jnp.float32)
                 rows_out[r + first_row] = product[:size] + (product[size : 2 * size] + product[2 * size :])
-            for j in range(4):
-                at = 4 * index + j + first_row
+            for j in range(group):
+                at = group * index + j + first_row
                 pltpu.make_async_copy(rows_out.at[at], basis.at[:, at, :], out_sems.at[at]).start()
             return carry
 
-        lax.fori_loop(0, count // 4, four, 0)
+        lax.fori_loop(0, count // group, several, 0)
 
     finish(stacked(inner_scale), inner, DEPTH, inner_rows, 0)
     matrix = stacked(edge_scale)
@@ -659,6 +664,7 @@
         return [
             pltpu.VMEM((number, count, columns), f32),
             pltpu.VMEM((tall, tall), jnp.int32),
+            pltpu.VMEM((count, columns), f32),
         ]
 
     kept = shape((4, 2, count, columns), f32)

time: 58.8 us -> 58 us (0.986)
  Pallas kernels: 35.7 us -> 35.1 us
where the time goes in v6:
time: 58 us; the launch traced here: 57.8 us
  Pallas kernels  35.1 us (61%)
  starting transfers between devices  15.1 us (26%)
  waiting for transfers between devices  6.55 us (11%)
  between operations  0.99 us (2%)
    pallas_call x1, Pallas kernels, on_device(): call(functools.partial(inner_kernel, strength), 'inner_rows', digit_rows(...  17.3 us
    ppermute x4, starting transfers between devices, summed(): lax.ppermute(pairs, AXIS, [(i, i ^ distance) for i in range(count)])  11.4 us
    pallas_call x1, Pallas kernels, on_device(): call(functools.partial(solve_kernel, cell_scale), 'solve', (shape((count,...  9.01 us
    ppermute x4, waiting for transfers between devices, summed(): lax.ppermute(pairs, AXIS, [(i, i ^ distance) for i in range(count)])  6.54 us
    pallas_call x1, Pallas kernels, on_device(): call(functools.partial(edge_kernel, strength, rows), 'edge_rows', digit_r...  5.89 us
    pallas_call x1, Pallas kernels, on_device(): call(pack_kernel, 'pack', (halo, halo), [whole(pl.ANY)] * 5, (whole(), wh...  2.9 us
    ppermute x1, starting transfers between devices, on_device(): lax.ppermute(to_below, AXIS, [(i, i + 1) for i in range(size - 1)])  2.39 us
    ppermute x1, starting transfers between devices, on_device(): lax.ppermute(to_above, AXIS, [(i + 1, i) for i in range(size - 1)])  1.29 us
  transfers between devices with their start and end apart: 6, of which 4 were waited for; matrix products, arithmetic and copies ran while one was open for 0% of the time, Pallas kernels for 30%

profile of v6, /device:TPU:0, one launch (start us, length us, event | category | flops | bytes accessed | tf_op | source)
XLA Modules:
  0.0 57.8 jit_solution(4342464529474566236)
XLA Ops:
  0.6 0.0 copy-start.3
  0.6 0.0 copy-start.2
  0.7 0.0 copy-start.1
  0.7 0.0 copy-start
  0.7 0.0 copy-start.4
  0.7 0.0 copy-start.5
  0.7 2.9 %pack.1 = (f32[4,72,512]{2,1,0:T(8,128)}, f32[4,72,512]{2,1,0:T(8,128)}) custom-call(f32[64,32,512]{2,1,0:T(8,128)} %cells.3, f32[32,512]{1,0:T(8,128)} %kappa.3, f32[32,512]{1,0:T(8,128)} %speed.3, f32[32,512]{1,0:T(8,128)} %friction.3, s32[16,32]{1,0:T(8,128)} %bitcast.1), custom_call_target="tpu_custom_call" | custom-call | tf_op jit(solution)/shard_map/pack/pallas_call | solution.py:640
  3.6 2.4 %collective-permute-start = (f32[4,72,512]{2,1,0:T(8,128)}, f32[4,72,512]{2,1,0:T(8,128)S(1)}, u32[]{:S(2)}, u32[]{:S(2)}) collective-permute-start(f32[4,72,512]{2,1,0:T(8,128)} %get-tuple-element.13), channel_id=1, source_target_pairs={{0,1},{1,2},{2,3},{3,4},{4,5},{5,6},{6,7},{7,8},{8,9},{9,10},{10,1... | collective-permute-start | bytes 1769480 | tf_op jit(solution)/shard_map/ppermute | solution.py:654
  6.0 1.3 %collective-permute-start.1 = (f32[4,72,512]{2,1,0:T(8,128)}, f32[4,72,512]{2,1,0:T(8,128)S(1)}, u32[]{:S(2)}, u32[]{:S(2)}) collective-permute-start(f32[4,72,512]{2,1,0:T(8,128)} %get-tuple-element.14), channel_id=1, source_target_pairs={{1,0},{2,1},{3,2},{4,3},{5,4},{6,5},{7,6},{8,7},{9,8},{10,9},{11,1... | collective-permute-start | bytes 1769480 | tf_op jit(solution)/shard_map/ppermute | solution.py:655
  7.3 0.0 copy-done.3
  7.3 0.0 copy-done.2
  7.3 0.0 copy-done.1
  7.3 0.0 copy-done
  7.3 0.0 copy-done.4
  7.3 0.0 copy-done.5
  7.4 17.3 %inner_rows.1 = (bf16[24,256,512]{2,1,0:T(8,128)(2,1)S(1)}, f32[64,128]{1,0:T(8,128)S(1)}, f32[64,128]{1,0:T(8,128)S(1)}, f32[4,2,64,512]{3,2,1,0:T(8,128)S(1)},...) custom-call(s32[64]{0:T(128)S(1)} %copy-done.5, f32[64,32,512]{2,1,0:T(8,128)S(1)} %copy-done, ...), custom_call_target="tpu_custom_call" | custom-call | flops 10000000000 | bytes 16777216 | tf_op jit(solution)/shard_map/inner_rows/pallas_call | solution.py:672
  24.6 0.0 collective-permute-done.above
  24.6 0.0 collective-permute-done.1.below
  24.7 5.9 %edge_rows.1 = (bf16[8,256,512]{2,1,0:T(8,128)(2,1)S(1)}, f32[64,128]{1,0:T(8,128)S(1)}, f32[64,128]{1,0:T(8,128)S(1)}) custom-call(s32[64]{0:T(128)S(1)} %copy-done.5, f32[4,72,512]{2,1,0:T(8,128)S(1)} %collective-permute-done.above, f32[4,72,512]{2,1,0:T(8,128)S(1)} %collective-permute-done.1.below, f32[7,32,512]{2,1,0:T(8,128)S(1)} %get-tuple-element.15.weights, ...), custom_call_target="tpu_custom_call" | custom-call | tf_op jit(solution)/shard_map/edge_rows/pallas_call | solution.py:687
  30.6 3.2 %collective-permute-start.2 = (f32[64,128]{1,0:T(8,128)S(1)}, f32[64,128]{1,0:T(8,128)S(1)}, u32[]{:S(2)}, u32[]{:S(2)}) collective-permute-start(f32[64,128]{1,0:T(8,128)S(1)} %get-tuple-element.19), channel_id=1, source_target_pairs={{0,1},{1,0},{2,3},{3,2},{4,5},{5,4},{6,7},{7,6},{8,9},{9,8},{10,11... | collective-permute-start | bytes 98312 | tf_op jit(solution)/shard_map/ppermute | solution.py:627
  33.8 0.9 %collective-permute-done.2 = f32[64,128]{1,0:T(8,128)S(1)} collective-permute-done((f32[64,128]{1,0:T(8,128)S(1)}, f32[64,128]{1,0:T(8,128)S(1)}, u32[]{:S(2)}, u32[]{:S(2)}) %collective-permute-start.2) | collective-permute-done | bytes 32800 | tf_op jit(solution)/shard_map/ppermute | solution.py:627
  34.7 2.1 %collective-permute-start.3 = (f32[64,128]{1,0:T(8,128)S(1)}, f32[64,128]{1,0:T(8,128)S(1)}, u32[]{:S(2)}, u32[]{:S(2)}) collective-permute-start(f32[64,128]{1,0:T(8,128)S(1)} %pad_maximum_fusion), channel_id=1, source_target_pairs={{0,2},{1,3},{2,0},{3,1},{4,6},{5,7},{6,4},{7,5},{8,10},{9,11},{10,... | collective-permute-start | bytes 98312 | tf_op jit(solution)/shard_map/ppermute | solution.py:627
  36.8 1.9 %collective-permute-done.3 = f32[64,128]{1,0:T(8,128)S(1)} collective-permute-done((f32[64,128]{1,0:T(8,128)S(1)}, f32[64,128]{1,0:T(8,128)S(1)}, u32[]{:S(2)}, u32[]{:S(2)}) %collective-permute-start.3) | collective-permute-done | bytes 32800 | tf_op jit(solution)/shard_map/ppermute | solution.py:627
  38.7 2.9 %collective-permute-start.4 = (f32[64,128]{1,0:T(8,128)S(1)}, f32[64,128]{1,0:T(8,128)S(1)}, u32[]{:S(2)}, u32[]{:S(2)}) collective-permute-start(f32[64,128]{1,0:T(8,128)S(1)} %pad_maximum_fusion.1), channel_id=1, source_target_pairs={{0,4},{1,5},{2,6},{3,7},{4,0},{5,1},{6,2},{7,3},{8,12},{9,13},{10,... | collective-permute-start | bytes 98312 | tf_op jit(solution)/shard_map/ppermute | solution.py:627
  41.6 1.9 %collective-permute-done.4 = f32[64,128]{1,0:T(8,128)S(1)} collective-permute-done((f32[64,128]{1,0:T(8,128)S(1)}, f32[64,128]{1,0:T(8,128)S(1)}, u32[]{:S(2)}, u32[]{:S(2)}) %collective-permute-start.4) | collective-permute-done | bytes 32800 | tf_op jit(solution)/shard_map/ppermute | solution.py:627
  43.6 3.1 %collective-permute-start.5 = (f32[64,128]{1,0:T(8,128)S(1)}, f32[64,128]{1,0:T(8,128)S(1)}, u32[]{:S(2)}, u32[]{:S(2)}) collective-permute-start(f32[64,128]{1,0:T(8,128)S(1)} %pad_maximum_fusion.2), channel_id=1, source_target_pairs={{0,8},{1,9},{2,10},{3,11},{4,12},{5,13},{6,14},{7,15},{8,0},{9,1},... | collective-permute-start | bytes 98312 | tf_op jit(solution)/shard_map/ppermute | solution.py:627
  46.7 1.9 %collective-permute-done.5 = f32[64,128]{1,0:T(8,128)S(1)} collective-permute-done((f32[64,128]{1,0:T(8,128)S(1)}, f32[64,128]{1,0:T(8,128)S(1)}, u32[]{:S(2)}, u32[]{:S(2)}) %collective-permute-start.5) | collective-permute-done | bytes 32800 | tf_op jit(solution)/shard_map/ppermute | solution.py:627
  48.6 9.0 %solve.1 = (f32[64,32,512]{2,1,0:T(8,128)}, f32[64,64]{1,0:T(8,128)}) custom-call(f32[64,128]{1,0:T(8,128)S(1)} %pad_maximum_fusion.3.pairs, f32[64,128]{1,0:T(8,128)S(1)} %get-tuple-element.20.inner_scale, f32[64,128]{1,0:T(8,128)S(1)} %get-tuple-element.21.edge_scale, bf16[24,256,512]{2,1,0:T(8,128)(2,1)S(1)} %get-tuple-element.22.inner, ...), custom_call_target="tpu_custom_call" | custom-call | tf_op jit(solution)/shard_map/solve/pallas_call | solution.py:703
  (8 shorter events, 0.1 us)
Async XLA Ops:
  0.6 6.7 %copy-start.3 = (f32[32,512]{1,0:T(8,128)S(1)}, f32[32,512]{1,0:T(8,128)}, u32[]{:S(2)}) copy-start(f32[32,512]{1,0:T(8,128)} %friction.3) | copy-start | bytes 196612
  0.6 6.7 %copy-start.2 = (f32[32,512]{1,0:T(8,128)S(1)}, f32[32,512]{1,0:T(8,128)}, u32[]{:S(2)}) copy-start(f32[32,512]{1,0:T(8,128)} %speed.3) | copy-start | bytes 196612
  0.7 6.7 %copy-start.1 = (f32[32,512]{1,0:T(8,128)S(1)}, f32[32,512]{1,0:T(8,128)}, u32[]{:S(2)}) copy-start(f32[32,512]{1,0:T(8,128)} %kappa.3) | copy-start | bytes 196612
  0.7 6.7 %copy-start = (f32[64,32,512]{2,1,0:T(8,128)S(1)}, f32[64,32,512]{2,1,0:T(8,128)}, u32[]{:S(2)}) copy-start(f32[64,32,512]{2,1,0:T(8,128)} %cells.3) | copy-start | bytes 12582916
  0.7 6.7 %copy-start.4 = (s32[32,16]{0,1:T(8,128)S(1)}, s32[32,16]{0,1:T(8,128)}, u32[]{:S(2)}) copy-start(s32[32,16]{0,1:T(8,128)} %param.10) | copy-start | bytes 6148
  0.7 6.7 %copy-start.5 = (s32[64]{0:T(128)S(1)}, s32[64]{0:T(128)}, u32[]{:S(2)}) copy-start(s32[64]{0:T(128)} %sites.3) | copy-start | bytes 772
  3.6 21.0 %collective-permute-start = (f32[4,72,512]{2,1,0:T(8,128)}, f32[4,72,512]{2,1,0:T(8,128)S(1)}, u32[]{:S(2)}, u32[]{:S(2)}) collective-permute-start(f32[4,72,512]{2,1,0:T(8,128)} %get-tuple-element.13), channel_id=1, source_target_pairs={{0,1},{1,2},{2,3},{3,4},{4,5},{5,6},{6,7},{7,8},{8,9},{9,10},{10,1... | collective-permute-start | bytes 1769480 | tf_op jit(solution)/shard_map/ppermute | solution.py:654
  6.0 18.7 %collective-permute-start.1 = (f32[4,72,512]{2,1,0:T(8,128)}, f32[4,72,512]{2,1,0:T(8,128)S(1)}, u32[]{:S(2)}, u32[]{:S(2)}) collective-permute-start(f32[4,72,512]{2,1,0:T(8,128)} %get-tuple-element.14), channel_id=1, source_target_pairs={{1,0},{2,1},{3,2},{4,3},{5,4},{6,5},{7,6},{8,7},{9,8},{10,9},{11,1... | collective-permute-start | bytes 1769480 | tf_op jit(solution)/shard_map/ppermute | solution.py:655
  30.6 4.1 %collective-permute-start.2 = (f32[64,128]{1,0:T(8,128)S(1)}, f32[64,128]{1,0:T(8,128)S(1)}, u32[]{:S(2)}, u32[]{:S(2)}) collective-permute-start(f32[64,128]{1,0:T(8,128)S(1)} %get-tuple-element.19), channel_id=1, source_target_pairs={{0,1},{1,0},{2,3},{3,2},{4,5},{5,4},{6,7},{7,6},{8,9},{9,8},{10,11... | collective-permute-start | bytes 98312 | tf_op jit(solution)/shard_map/ppermute | solution.py:627
  34.7 4.0 %collective-permute-start.3 = (f32[64,128]{1,0:T(8,128)S(1)}, f32[64,128]{1,0:T(8,128)S(1)}, u32[]{:S(2)}, u32[]{:S(2)}) collective-permute-start(f32[64,128]{1,0:T(8,128)S(1)} %pad_maximum_fusion), channel_id=1, source_target_pairs={{0,2},{1,3},{2,0},{3,1},{4,6},{5,7},{6,4},{7,5},{8,10},{9,11},{10,... | collective-permute-start | bytes 98312 | tf_op jit(solution)/shard_map/ppermute | solution.py:627
  38.7 4.8 %collective-permute-start.4 = (f32[64,128]{1,0:T(8,128)S(1)}, f32[64,128]{1,0:T(8,128)S(1)}, u32[]{:S(2)}, u32[]{:S(2)}) collective-permute-start(f32[64,128]{1,0:T(8,128)S(1)} %pad_maximum_fusion.1), channel_id=1, source_target_pairs={{0,4},{1,5},{2,6},{3,7},{4,0},{5,1},{6,2},{7,3},{8,12},{9,13},{10,... | collective-permute-start | bytes 98312 | tf_op jit(solution)/shard_map/ppermute | solution.py:627
  43.6 5.0 %collective-permute-start.5 = (f32[64,128]{1,0:T(8,128)S(1)}, f32[64,128]{1,0:T(8,128)S(1)}, u32[]{:S(2)}, u32[]{:S(2)}) collective-permute-start(f32[64,128]{1,0:T(8,128)S(1)} %pad_maximum_fusion.2), channel_id=1, source_target_pairs={{0,8},{1,9},{2,10},{3,11},{4,12},{5,13},{6,14},{7,15},{8,0},{9,1},... | collective-permute-start | bytes 98312 | tf_op jit(solution)/shard_map/ppermute | solution.py:627

commit v7 on v6

--- a/solution.py
+++ b/solution.py
@@ -567,7 +567,7 @@
         return jnp.concatenate([tall * 256.0**-a for a in range(DIGITS)], axis=1).astype(jnp.bfloat16)
 
     def finish(matrix, cells, first_row, count, shift):
-        group = min(2 * GROUP, count)
+        group = math.gcd(count, 6 * GROUP)
 
         def several(index, carry):
             for j in range(group):

time: 58 us -> 57.7 us (level)
  no operation moved by 1% of the time
where the time goes in v7:
time: 57.7 us; the launch traced here: 57.4 us
  Pallas kernels  34.7 us (60%)
  starting transfers between devices  15.1 us (26%)
  waiting for transfers between devices  6.55 us (11%)
  between operations  0.99 us (2%)
    pallas_call x1, Pallas kernels, on_device(): call(functools.partial(inner_kernel, strength), 'inner_rows', digit_rows(...  17.2 us
    ppermute x4, starting transfers between devices, summed(): lax.ppermute(pairs, AXIS, [(i, i ^ distance) for i in range(count)])  11.4 us
    pallas_call x1, Pallas kernels, on_device(): call(functools.partial(solve_kernel, cell_scale), 'solve', (shape((count,...  8.71 us
    ppermute x4, waiting for transfers between devices, summed(): lax.ppermute(pairs, AXIS, [(i, i ^ distance) for i in range(count)])  6.54 us
    pallas_call x1, Pallas kernels, on_device(): call(functools.partial(edge_kernel, strength, rows), 'edge_rows', digit_r...  5.89 us
    pallas_call x1, Pallas kernels, on_device(): call(pack_kernel, 'pack', (halo, halo), [whole(pl.ANY)] * 5, (whole(), wh...  2.9 us
    ppermute x1, starting transfers between devices, on_device(): lax.ppermute(to_below, AXIS, [(i, i + 1) for i in range(size - 1)])  2.39 us
    ppermute x1, starting transfers between devices, on_device(): lax.ppermute(to_above, AXIS, [(i + 1, i) for i in range(size - 1)])  1.29 us
  transfers between devices with their start and end apart: 6, of which 4 were waited for; matrix products, arithmetic and copies ran while one was open for 0% of the time, Pallas kernels for 30%

profile of v7, /device:TPU:0, one launch (start us, length us, event | category | flops | bytes accessed | tf_op | source)
XLA Modules:
  0.0 57.4 jit_solution(7766358408422586786)
XLA Ops:
  0.6 0.0 copy-start.3
  0.6 0.0 copy-start.2
  0.7 0.0 copy-start.1
  0.7 0.0 copy-start
  0.7 0.0 copy-start.4
  0.7 0.0 copy-start.5
  0.7 2.9 %pack.1 = (f32[4,72,512]{2,1,0:T(8,128)}, f32[4,72,512]{2,1,0:T(8,128)}) custom-call(f32[64,32,512]{2,1,0:T(8,128)} %cells.3, f32[32,512]{1,0:T(8,128)} %kappa.3, f32[32,512]{1,0:T(8,128)} %speed.3, f32[32,512]{1,0:T(8,128)} %friction.3, s32[16,32]{1,0:T(8,128)} %bitcast.1), custom_call_target="tpu_custom_call" | custom-call | tf_op jit(solution)/shard_map/pack/pallas_call | solution.py:640
  3.6 2.4 %collective-permute-start = (f32[4,72,512]{2,1,0:T(8,128)}, f32[4,72,512]{2,1,0:T(8,128)S(1)}, u32[]{:S(2)}, u32[]{:S(2)}) collective-permute-start(f32[4,72,512]{2,1,0:T(8,128)} %get-tuple-element.13), channel_id=1, source_target_pairs={{0,1},{1,2},{2,3},{3,4},{4,5},{5,6},{6,7},{7,8},{8,9},{9,10},{10,1... | collective-permute-start | bytes 1769480 | tf_op jit(solution)/shard_map/ppermute | solution.py:654
  6.0 1.3 %collective-permute-start.1 = (f32[4,72,512]{2,1,0:T(8,128)}, f32[4,72,512]{2,1,0:T(8,128)S(1)}, u32[]{:S(2)}, u32[]{:S(2)}) collective-permute-start(f32[4,72,512]{2,1,0:T(8,128)} %get-tuple-element.14), channel_id=1, source_target_pairs={{1,0},{2,1},{3,2},{4,3},{5,4},{6,5},{7,6},{8,7},{9,8},{10,9},{11,1... | collective-permute-start | bytes 1769480 | tf_op jit(solution)/shard_map/ppermute | solution.py:655
  7.3 0.0 copy-done.3
  7.3 0.0 copy-done.2
  7.3 0.0 copy-done.1
  7.3 0.0 copy-done
  7.3 0.0 copy-done.4
  7.3 0.0 copy-done.5
  7.4 17.2 %inner_rows.1 = (bf16[24,256,512]{2,1,0:T(8,128)(2,1)S(1)}, f32[64,128]{1,0:T(8,128)S(1)}, f32[64,128]{1,0:T(8,128)S(1)}, f32[4,2,64,512]{3,2,1,0:T(8,128)S(1)},...) custom-call(s32[64]{0:T(128)S(1)} %copy-done.5, f32[64,32,512]{2,1,0:T(8,128)S(1)} %copy-done, ...), custom_call_target="tpu_custom_call" | custom-call | flops 10000000000 | bytes 16777216 | tf_op jit(solution)/shard_map/inner_rows/pallas_call | solution.py:672
  24.6 0.0 collective-permute-done.above
  24.6 0.0 collective-permute-done.1.below
  24.6 5.9 %edge_rows.1 = (bf16[8,256,512]{2,1,0:T(8,128)(2,1)S(1)}, f32[64,128]{1,0:T(8,128)S(1)}, f32[64,128]{1,0:T(8,128)S(1)}) custom-call(s32[64]{0:T(128)S(1)} %copy-done.5, f32[4,72,512]{2,1,0:T(8,128)S(1)} %collective-permute-done.above, f32[4,72,512]{2,1,0:T(8,128)S(1)} %collective-permute-done.1.below, f32[7,32,512]{2,1,0:T(8,128)S(1)} %get-tuple-element.15.weights, ...), custom_call_target="tpu_custom_call" | custom-call | tf_op jit(solution)/shard_map/edge_rows/pallas_call | solution.py:687
  30.5 3.3 %collective-permute-start.2 = (f32[64,128]{1,0:T(8,128)S(1)}, f32[64,128]{1,0:T(8,128)S(1)}, u32[]{:S(2)}, u32[]{:S(2)}) collective-permute-start(f32[64,128]{1,0:T(8,128)S(1)} %get-tuple-element.19), channel_id=1, source_target_pairs={{0,1},{1,0},{2,3},{3,2},{4,5},{5,4},{6,7},{7,6},{8,9},{9,8},{10,11... | collective-permute-start | bytes 98312 | tf_op jit(solution)/shard_map/ppermute | solution.py:627
  33.8 0.9 %collective-permute-done.2 = f32[64,128]{1,0:T(8,128)S(1)} collective-permute-done((f32[64,128]{1,0:T(8,128)S(1)}, f32[64,128]{1,0:T(8,128)S(1)}, u32[]{:S(2)}, u32[]{:S(2)}) %collective-permute-start.2) | collective-permute-done | bytes 32800 | tf_op jit(solution)/shard_map/ppermute | solution.py:627
  34.7 2.1 %collective-permute-start.3 = (f32[64,128]{1,0:T(8,128)S(1)}, f32[64,128]{1,0:T(8,128)S(1)}, u32[]{:S(2)}, u32[]{:S(2)}) collective-permute-start(f32[64,128]{1,0:T(8,128)S(1)} %pad_maximum_fusion), channel_id=1, source_target_pairs={{0,2},{1,3},{2,0},{3,1},{4,6},{5,7},{6,4},{7,5},{8,10},{9,11},{10,... | collective-permute-start | bytes 98312 | tf_op jit(solution)/shard_map/ppermute | solution.py:627
  36.8 1.9 %collective-permute-done.3 = f32[64,128]{1,0:T(8,128)S(1)} collective-permute-done((f32[64,128]{1,0:T(8,128)S(1)}, f32[64,128]{1,0:T(8,128)S(1)}, u32[]{:S(2)}, u32[]{:S(2)}) %collective-permute-start.3) | collective-permute-done | bytes 32800 | tf_op jit(solution)/shard_map/ppermute | solution.py:627
  38.7 3.0 %collective-permute-start.4 = (f32[64,128]{1,0:T(8,128)S(1)}, f32[64,128]{1,0:T(8,128)S(1)}, u32[]{:S(2)}, u32[]{:S(2)}) collective-permute-start(f32[64,128]{1,0:T(8,128)S(1)} %pad_maximum_fusion.1), channel_id=1, source_target_pairs={{0,4},{1,5},{2,6},{3,7},{4,0},{5,1},{6,2},{7,3},{8,12},{9,13},{10,... | collective-permute-start | bytes 98312 | tf_op jit(solution)/shard_map/ppermute | solution.py:627
  41.7 1.9 %collective-permute-done.4 = f32[64,128]{1,0:T(8,128)S(1)} collective-permute-done((f32[64,128]{1,0:T(8,128)S(1)}, f32[64,128]{1,0:T(8,128)S(1)}, u32[]{:S(2)}, u32[]{:S(2)}) %collective-permute-start.4) | collective-permute-done | bytes 32800 | tf_op jit(solution)/shard_map/ppermute | solution.py:627
  43.6 3.0 %collective-permute-start.5 = (f32[64,128]{1,0:T(8,128)S(1)}, f32[64,128]{1,0:T(8,128)S(1)}, u32[]{:S(2)}, u32[]{:S(2)}) collective-permute-start(f32[64,128]{1,0:T(8,128)S(1)} %pad_maximum_fusion.2), channel_id=1, source_target_pairs={{0,8},{1,9},{2,10},{3,11},{4,12},{5,13},{6,14},{7,15},{8,0},{9,1},... | collective-permute-start | bytes 98312 | tf_op jit(solution)/shard_map/ppermute | solution.py:627
  46.6 1.9 %collective-permute-done.5 = f32[64,128]{1,0:T(8,128)S(1)} collective-permute-done((f32[64,128]{1,0:T(8,128)S(1)}, f32[64,128]{1,0:T(8,128)S(1)}, u32[]{:S(2)}, u32[]{:S(2)}) %collective-permute-start.5) | collective-permute-done | bytes 32800 | tf_op jit(solution)/shard_map/ppermute | solution.py:627
  48.5 8.7 %solve.1 = (f32[64,32,512]{2,1,0:T(8,128)}, f32[64,64]{1,0:T(8,128)}) custom-call(f32[64,128]{1,0:T(8,128)S(1)} %pad_maximum_fusion.3.pairs, f32[64,128]{1,0:T(8,128)S(1)} %get-tuple-element.20.inner_scale, f32[64,128]{1,0:T(8,128)S(1)} %get-tuple-element.21.edge_scale, bf16[24,256,512]{2,1,0:T(8,128)(2,1)S(1)} %get-tuple-element.22.inner, ...), custom_call_target="tpu_custom_call" | custom-call | tf_op jit(solution)/shard_map/solve/pallas_call | solution.py:703
  (8 shorter events, 0.1 us)
Async XLA Ops:
  0.6 6.7 %copy-start.3 = (f32[32,512]{1,0:T(8,128)S(1)}, f32[32,512]{1,0:T(8,128)}, u32[]{:S(2)}) copy-start(f32[32,512]{1,0:T(8,128)} %friction.3) | copy-start | bytes 196612
  0.6 6.7 %copy-start.2 = (f32[32,512]{1,0:T(8,128)S(1)}, f32[32,512]{1,0:T(8,128)}, u32[]{:S(2)}) copy-start(f32[32,512]{1,0:T(8,128)} %speed.3) | copy-start | bytes 196612
  0.7 6.7 %copy-start.1 = (f32[32,512]{1,0:T(8,128)S(1)}, f32[32,512]{1,0:T(8,128)}, u32[]{:S(2)}) copy-start(f32[32,512]{1,0:T(8,128)} %kappa.3) | copy-start | bytes 196612
  0.7 6.7 %copy-start = (f32[64,32,512]{2,1,0:T(8,128)S(1)}, f32[64,32,512]{2,1,0:T(8,128)}, u32[]{:S(2)}) copy-start(f32[64,32,512]{2,1,0:T(8,128)} %cells.3) | copy-start | bytes 12582916
  0.7 6.7 %copy-start.4 = (s32[32,16]{0,1:T(8,128)S(1)}, s32[32,16]{0,1:T(8,128)}, u32[]{:S(2)}) copy-start(s32[32,16]{0,1:T(8,128)} %param.10) | copy-start | bytes 6148
  0.7 6.7 %copy-start.5 = (s32[64]{0:T(128)S(1)}, s32[64]{0:T(128)}, u32[]{:S(2)}) copy-start(s32[64]{0:T(128)} %sites.3) | copy-start | bytes 772
  3.6 21.0 %collective-permute-start = (f32[4,72,512]{2,1,0:T(8,128)}, f32[4,72,512]{2,1,0:T(8,128)S(1)}, u32[]{:S(2)}, u32[]{:S(2)}) collective-permute-start(f32[4,72,512]{2,1,0:T(8,128)} %get-tuple-element.13), channel_id=1, source_target_pairs={{0,1},{1,2},{2,3},{3,4},{4,5},{5,6},{6,7},{7,8},{8,9},{9,10},{10,1... | collective-permute-start | bytes 1769480 | tf_op jit(solution)/shard_map/ppermute | solution.py:654
  6.0 18.6 %collective-permute-start.1 = (f32[4,72,512]{2,1,0:T(8,128)}, f32[4,72,512]{2,1,0:T(8,128)S(1)}, u32[]{:S(2)}, u32[]{:S(2)}) collective-permute-start(f32[4,72,512]{2,1,0:T(8,128)} %get-tuple-element.14), channel_id=1, source_target_pairs={{1,0},{2,1},{3,2},{4,3},{5,4},{6,5},{7,6},{8,7},{9,8},{10,9},{11,1... | collective-permute-start | bytes 1769480 | tf_op jit(solution)/shard_map/ppermute | solution.py:655
  30.5 4.2 %collective-permute-start.2 = (f32[64,128]{1,0:T(8,128)S(1)}, f32[64,128]{1,0:T(8,128)S(1)}, u32[]{:S(2)}, u32[]{:S(2)}) collective-permute-start(f32[64,128]{1,0:T(8,128)S(1)} %get-tuple-element.19), channel_id=1, source_target_pairs={{0,1},{1,0},{2,3},{3,2},{4,5},{5,4},{6,7},{7,6},{8,9},{9,8},{10,11... | collective-permute-start | bytes 98312 | tf_op jit(solution)/shard_map/ppermute | solution.py:627
  34.7 4.0 %collective-permute-start.3 = (f32[64,128]{1,0:T(8,128)S(1)}, f32[64,128]{1,0:T(8,128)S(1)}, u32[]{:S(2)}, u32[]{:S(2)}) collective-permute-start(f32[64,128]{1,0:T(8,128)S(1)} %pad_maximum_fusion), channel_id=1, source_target_pairs={{0,2},{1,3},{2,0},{3,1},{4,6},{5,7},{6,4},{7,5},{8,10},{9,11},{10,... | collective-permute-start | bytes 98312 | tf_op jit(solution)/shard_map/ppermute | solution.py:627
  38.7 4.9 %collective-permute-start.4 = (f32[64,128]{1,0:T(8,128)S(1)}, f32[64,128]{1,0:T(8,128)S(1)}, u32[]{:S(2)}, u32[]{:S(2)}) collective-permute-start(f32[64,128]{1,0:T(8,128)S(1)} %pad_maximum_fusion.1), channel_id=1, source_target_pairs={{0,4},{1,5},{2,6},{3,7},{4,0},{5,1},{6,2},{7,3},{8,12},{9,13},{10,... | collective-permute-start | bytes 98312 | tf_op jit(solution)/shard_map/ppermute | solution.py:627
  43.6 4.9 %collective-permute-start.5 = (f32[64,128]{1,0:T(8,128)S(1)}, f32[64,128]{1,0:T(8,128)S(1)}, u32[]{:S(2)}, u32[]{:S(2)}) collective-permute-start(f32[64,128]{1,0:T(8,128)S(1)} %pad_maximum_fusion.2), channel_id=1, source_target_pairs={{0,8},{1,9},{2,10},{3,11},{4,12},{5,13},{6,14},{7,15},{8,0},{9,1},... | collective-permute-start | bytes 98312 | tf_op jit(solution)/shard_map/ppermute | solution.py:627

commit v8 on v7

--- a/solution.py
+++ b/solution.py
@@ -26,7 +26,7 @@
     return jnp.broadcast_to(weights[layer, pl.ds(row, 1), :], like)
 
 
-def in_steps(first, last, body, step=10):
+def in_steps(first, last, body, step=15):
     whole_steps = (last - first) // step
 
     def several(index, carry):

time: 57.7 us -> 58.1 us (level)
  no operation moved by 1% of the time
where the time goes in v8:
time: 58.1 us; the launch traced here: 57.9 us
  Pallas kernels  35.1 us (60%)
  starting transfers between devices  15.1 us (26%)
  waiting for transfers between devices  6.62 us (11%)
  between operations  1.01 us (2%)
    pallas_call x1, Pallas kernels, on_device(): call(functools.partial(inner_kernel, strength), 'inner_rows', digit_rows(...  17.5 us
    ppermute x4, starting transfers between devices, summed(): lax.ppermute(pairs, AXIS, [(i, i ^ distance) for i in range(count)])  11.5 us
    pallas_call x1, Pallas kernels, on_device(): call(functools.partial(solve_kernel, cell_scale), 'solve', (shape((count,...  8.71 us
    ppermute x4, waiting for transfers between devices, summed(): lax.ppermute(pairs, AXIS, [(i, i ^ distance) for i in range(count)])  6.61 us
    pallas_call x1, Pallas kernels, on_device(): call(functools.partial(edge_kernel, strength, rows), 'edge_rows', digit_r...  5.93 us
    pallas_call x1, Pallas kernels, on_device(): call(pack_kernel, 'pack', (halo, halo), [whole(pl.ANY)] * 5, (whole(), wh...  2.9 us
    ppermute x1, starting transfers between devices, on_device(): lax.ppermute(to_below, AXIS, [(i, i + 1) for i in range(size - 1)])  2.39 us
    ppermute x1, starting transfers between devices, on_device(): lax.ppermute(to_above, AXIS, [(i + 1, i) for i in range(size - 1)])  1.29 us
  transfers between devices with their start and end apart: 6, of which 4 were waited for; matrix products, arithmetic and copies ran while one was open for 0% of the time, Pallas kernels for 30%

profile of v8, /device:TPU:0, one launch (start us, length us, event | category | flops | bytes accessed | tf_op | source)
XLA Modules:
  0.0 57.9 jit_solution(11534471313508034570)
XLA Ops:
  0.6 0.0 copy-start.3
  0.6 0.0 copy-start.2
  0.7 0.0 copy-start.1
  0.7 0.0 copy-start
  0.7 0.0 copy-start.4
  0.7 0.0 copy-start.5
  0.7 2.9 %pack.1 = (f32[4,72,512]{2,1,0:T(8,128)}, f32[4,72,512]{2,1,0:T(8,128)}) custom-call(f32[64,32,512]{2,1,0:T(8,128)} %cells.3, f32[32,512]{1,0:T(8,128)} %kappa.3, f32[32,512]{1,0:T(8,128)} %speed.3, f32[32,512]{1,0:T(8,128)} %friction.3, s32[16,32]{1,0:T(8,128)} %bitcast.1), custom_call_target="tpu_custom_call" | custom-call | tf_op jit(solution)/shard_map/pack/pallas_call | solution.py:640
  3.6 2.4 %collective-permute-start = (f32[4,72,512]{2,1,0:T(8,128)}, f32[4,72,512]{2,1,0:T(8,128)S(1)}, u32[]{:S(2)}, u32[]{:S(2)}) collective-permute-start(f32[4,72,512]{2,1,0:T(8,128)} %get-tuple-element.13), channel_id=1, source_target_pairs={{0,1},{1,2},{2,3},{3,4},{4,5},{5,6},{6,7},{7,8},{8,9},{9,10},{10,1... | collective-permute-start | bytes 1769480 | tf_op jit(solution)/shard_map/ppermute | solution.py:654
  6.0 1.3 %collective-permute-start.1 = (f32[4,72,512]{2,1,0:T(8,128)}, f32[4,72,512]{2,1,0:T(8,128)S(1)}, u32[]{:S(2)}, u32[]{:S(2)}) collective-permute-start(f32[4,72,512]{2,1,0:T(8,128)} %get-tuple-element.14), channel_id=1, source_target_pairs={{1,0},{2,1},{3,2},{4,3},{5,4},{6,5},{7,6},{8,7},{9,8},{10,9},{11,1... | collective-permute-start | bytes 1769480 | tf_op jit(solution)/shard_map/ppermute | solution.py:655
  7.3 0.0 copy-done.3
  7.3 0.0 copy-done.2
  7.3 0.0 copy-done.1
  7.3 0.0 copy-done
  7.3 0.0 copy-done.4
  7.3 0.0 copy-done.5
  7.4 17.5 %inner_rows.1 = (bf16[24,256,512]{2,1,0:T(8,128)(2,1)S(1)}, f32[64,128]{1,0:T(8,128)S(1)}, f32[64,128]{1,0:T(8,128)S(1)}, f32[4,2,64,512]{3,2,1,0:T(8,128)S(1)},...) custom-call(s32[64]{0:T(128)S(1)} %copy-done.5, f32[64,32,512]{2,1,0:T(8,128)S(1)} %copy-done, ...), custom_call_target="tpu_custom_call" | custom-call | flops 10000000000 | bytes 16777216 | tf_op jit(solution)/shard_map/inner_rows/pallas_call | solution.py:672
  24.9 0.0 collective-permute-done.above
  24.9 0.0 collective-permute-done.1.below
  24.9 5.9 %edge_rows.1 = (bf16[8,256,512]{2,1,0:T(8,128)(2,1)S(1)}, f32[64,128]{1,0:T(8,128)S(1)}, f32[64,128]{1,0:T(8,128)S(1)}) custom-call(s32[64]{0:T(128)S(1)} %copy-done.5, f32[4,72,512]{2,1,0:T(8,128)S(1)} %collective-permute-done.above, f32[4,72,512]{2,1,0:T(8,128)S(1)} %collective-permute-done.1.below, f32[7,32,512]{2,1,0:T(8,128)S(1)} %get-tuple-element.15.weights, ...), custom_call_target="tpu_custom_call" | custom-call | tf_op jit(solution)/shard_map/edge_rows/pallas_call | solution.py:687
  30.8 3.1 %collective-permute-start.2 = (f32[64,128]{1,0:T(8,128)S(1)}, f32[64,128]{1,0:T(8,128)S(1)}, u32[]{:S(2)}, u32[]{:S(2)}) collective-permute-start(f32[64,128]{1,0:T(8,128)S(1)} %get-tuple-element.19), channel_id=1, source_target_pairs={{0,1},{1,0},{2,3},{3,2},{4,5},{5,4},{6,7},{7,6},{8,9},{9,8},{10,11... | collective-permute-start | bytes 98312 | tf_op jit(solution)/shard_map/ppermute | solution.py:627
  34.0 0.9 %collective-permute-done.2 = f32[64,128]{1,0:T(8,128)S(1)} collective-permute-done((f32[64,128]{1,0:T(8,128)S(1)}, f32[64,128]{1,0:T(8,128)S(1)}, u32[]{:S(2)}, u32[]{:S(2)}) %collective-permute-start.2) | collective-permute-done | bytes 32800 | tf_op jit(solution)/shard_map/ppermute | solution.py:627
  34.9 2.1 %collective-permute-start.3 = (f32[64,128]{1,0:T(8,128)S(1)}, f32[64,128]{1,0:T(8,128)S(1)}, u32[]{:S(2)}, u32[]{:S(2)}) collective-permute-start(f32[64,128]{1,0:T(8,128)S(1)} %pad_maximum_fusion), channel_id=1, source_target_pairs={{0,2},{1,3},{2,0},{3,1},{4,6},{5,7},{6,4},{7,5},{8,10},{9,11},{10,... | collective-permute-start | bytes 98312 | tf_op jit(solution)/shard_map/ppermute | solution.py:627
  37.0 1.9 %collective-permute-done.3 = f32[64,128]{1,0:T(8,128)S(1)} collective-permute-done((f32[64,128]{1,0:T(8,128)S(1)}, f32[64,128]{1,0:T(8,128)S(1)}, u32[]{:S(2)}, u32[]{:S(2)}) %collective-permute-start.3) | collective-permute-done | bytes 32800 | tf_op jit(solution)/shard_map/ppermute | solution.py:627
  38.9 3.3 %collective-permute-start.4 = (f32[64,128]{1,0:T(8,128)S(1)}, f32[64,128]{1,0:T(8,128)S(1)}, u32[]{:S(2)}, u32[]{:S(2)}) collective-permute-start(f32[64,128]{1,0:T(8,128)S(1)} %pad_maximum_fusion.1), channel_id=1, source_target_pairs={{0,4},{1,5},{2,6},{3,7},{4,0},{5,1},{6,2},{7,3},{8,12},{9,13},{10,... | collective-permute-start | bytes 98312 | tf_op jit(solution)/shard_map/ppermute | solution.py:627
  42.2 1.9 %collective-permute-done.4 = f32[64,128]{1,0:T(8,128)S(1)} collective-permute-done((f32[64,128]{1,0:T(8,128)S(1)}, f32[64,128]{1,0:T(8,128)S(1)}, u32[]{:S(2)}, u32[]{:S(2)}) %collective-permute-start.4) | collective-permute-done | bytes 32800 | tf_op jit(solution)/shard_map/ppermute | solution.py:627
  44.1 2.9 %collective-permute-start.5 = (f32[64,128]{1,0:T(8,128)S(1)}, f32[64,128]{1,0:T(8,128)S(1)}, u32[]{:S(2)}, u32[]{:S(2)}) collective-permute-start(f32[64,128]{1,0:T(8,128)S(1)} %pad_maximum_fusion.2), channel_id=1, source_target_pairs={{0,8},{1,9},{2,10},{3,11},{4,12},{5,13},{6,14},{7,15},{8,0},{9,1},... | collective-permute-start | bytes 98312 | tf_op jit(solution)/shard_map/ppermute | solution.py:627
  47.0 2.0 %collective-permute-done.5 = f32[64,128]{1,0:T(8,128)S(1)} collective-permute-done((f32[64,128]{1,0:T(8,128)S(1)}, f32[64,128]{1,0:T(8,128)S(1)}, u32[]{:S(2)}, u32[]{:S(2)}) %collective-permute-start.5) | collective-permute-done | bytes 32800 | tf_op jit(solution)/shard_map/ppermute | solution.py:627
  49.0 8.7 %solve.1 = (f32[64,32,512]{2,1,0:T(8,128)}, f32[64,64]{1,0:T(8,128)}) custom-call(f32[64,128]{1,0:T(8,128)S(1)} %pad_maximum_fusion.3.pairs, f32[64,128]{1,0:T(8,128)S(1)} %get-tuple-element.20.inner_scale, f32[64,128]{1,0:T(8,128)S(1)} %get-tuple-element.21.edge_scale, bf16[24,256,512]{2,1,0:T(8,128)(2,1)S(1)} %get-tuple-element.22.inner, ...), custom_call_target="tpu_custom_call" | custom-call | tf_op jit(solution)/shard_map/solve/pallas_call | solution.py:703
  (8 shorter events, 0.1 us)
Async XLA Ops:
  0.6 6.7 %copy-start.3 = (f32[32,512]{1,0:T(8,128)S(1)}, f32[32,512]{1,0:T(8,128)}, u32[]{:S(2)}) copy-start(f32[32,512]{1,0:T(8,128)} %friction.3) | copy-start | bytes 196612
  0.6 6.7 %copy-start.2 = (f32[32,512]{1,0:T(8,128)S(1)}, f32[32,512]{1,0:T(8,128)}, u32[]{:S(2)}) copy-start(f32[32,512]{1,0:T(8,128)} %speed.3) | copy-start | bytes 196612
  0.7 6.7 %copy-start.1 = (f32[32,512]{1,0:T(8,128)S(1)}, f32[32,512]{1,0:T(8,128)}, u32[]{:S(2)}) copy-start(f32[32,512]{1,0:T(8,128)} %kappa.3) | copy-start | bytes 196612
  0.7 6.7 %copy-start = (f32[64,32,512]{2,1,0:T(8,128)S(1)}, f32[64,32,512]{2,1,0:T(8,128)}, u32[]{:S(2)}) copy-start(f32[64,32,512]{2,1,0:T(8,128)} %cells.3) | copy-start | bytes 12582916
  0.7 6.7 %copy-start.4 = (s32[32,16]{0,1:T(8,128)S(1)}, s32[32,16]{0,1:T(8,128)}, u32[]{:S(2)}) copy-start(s32[32,16]{0,1:T(8,128)} %param.10) | copy-start | bytes 6148
  0.7 6.7 %copy-start.5 = (s32[64]{0:T(128)S(1)}, s32[64]{0:T(128)}, u32[]{:S(2)}) copy-start(s32[64]{0:T(128)} %sites.3) | copy-start | bytes 772
  3.6 21.3 %collective-permute-start = (f32[4,72,512]{2,1,0:T(8,128)}, f32[4,72,512]{2,1,0:T(8,128)S(1)}, u32[]{:S(2)}, u32[]{:S(2)}) collective-permute-start(f32[4,72,512]{2,1,0:T(8,128)} %get-tuple-element.13), channel_id=1, source_target_pairs={{0,1},{1,2},{2,3},{3,4},{4,5},{5,6},{6,7},{7,8},{8,9},{9,10},{10,1... | collective-permute-start | bytes 1769480 | tf_op jit(solution)/shard_map/ppermute | solution.py:654
  6.0 18.9 %collective-permute-start.1 = (f32[4,72,512]{2,1,0:T(8,128)}, f32[4,72,512]{2,1,0:T(8,128)S(1)}, u32[]{:S(2)}, u32[]{:S(2)}) collective-permute-start(f32[4,72,512]{2,1,0:T(8,128)} %get-tuple-element.14), channel_id=1, source_target_pairs={{1,0},{2,1},{3,2},{4,3},{5,4},{6,5},{7,6},{8,7},{9,8},{10,9},{11,1... | collective-permute-start | bytes 1769480 | tf_op jit(solution)/shard_map/ppermute | solution.py:655
  30.8 4.0 %collective-permute-start.2 = (f32[64,128]{1,0:T(8,128)S(1)}, f32[64,128]{1,0:T(8,128)S(1)}, u32[]{:S(2)}, u32[]{:S(2)}) collective-permute-start(f32[64,128]{1,0:T(8,128)S(1)} %get-tuple-element.19), channel_id=1, source_target_pairs={{0,1},{1,0},{2,3},{3,2},{4,5},{5,4},{6,7},{7,6},{8,9},{9,8},{10,11... | collective-permute-start | bytes 98312 | tf_op jit(solution)/shard_map/ppermute | solution.py:627
  34.9 4.0 %collective-permute-start.3 = (f32[64,128]{1,0:T(8,128)S(1)}, f32[64,128]{1,0:T(8,128)S(1)}, u32[]{:S(2)}, u32[]{:S(2)}) collective-permute-start(f32[64,128]{1,0:T(8,128)S(1)} %pad_maximum_fusion), channel_id=1, source_target_pairs={{0,2},{1,3},{2,0},{3,1},{4,6},{5,7},{6,4},{7,5},{8,10},{9,11},{10,... | collective-permute-start | bytes 98312 | tf_op jit(solution)/shard_map/ppermute | solution.py:627
  38.9 5.2 %collective-permute-start.4 = (f32[64,128]{1,0:T(8,128)S(1)}, f32[64,128]{1,0:T(8,128)S(1)}, u32[]{:S(2)}, u32[]{:S(2)}) collective-permute-start(f32[64,128]{1,0:T(8,128)S(1)} %pad_maximum_fusion.1), channel_id=1, source_target_pairs={{0,4},{1,5},{2,6},{3,7},{4,0},{5,1},{6,2},{7,3},{8,12},{9,13},{10,... | collective-permute-start | bytes 98312 | tf_op jit(solution)/shard_map/ppermute | solution.py:627
  44.1 4.9 %collective-permute-start.5 = (f32[64,128]{1,0:T(8,128)S(1)}, f32[64,128]{1,0:T(8,128)S(1)}, u32[]{:S(2)}, u32[]{:S(2)}) collective-permute-start(f32[64,128]{1,0:T(8,128)S(1)} %pad_maximum_fusion.2), channel_id=1, source_target_pairs={{0,8},{1,9},{2,10},{3,11},{4,12},{5,13},{6,14},{7,15},{8,0},{9,1},... | collective-permute-start | bytes 98312 | tf_op jit(solution)/shard_map/ppermute | solution.py:627
